TPU v7x, 32 devices: a whole 2x2x4 slice. The times are simulated.
32 devices in a mesh: slab: 8 (over y, x, core), orb: 4 (over z).
Axes of the slice: x: 2, y: 2, z: 4, core: 2. Of those that a mesh axis runs over, the one named last changes fastest.
Arguments:
- orbitals: float32 [256, 16384], P('orb', 'slab'), may hold values from -6 to 6
- cell_matrices: bfloat16 [64, 512, 512], P('slab'), as said below
- connectivity: int32 [64, 512], P('slab'), may hold values from 0 to 2559, as said below
- face_lower: int32 [2048], P('slab'), may hold values from 0 to 2047, as said below
- face_upper: int32 [2048], P('slab'), may hold values from 0 to 2047, as said below
Outputs:
- orthonormal_orbitals: float32 [256, 16384], P('orb', 'slab')
Inputs may be any that keep to these rules, and one draw needn't show every extreme that they name: `connectivity`: each row names 512 distinct positions of its slab's extended numbering. `face_lower`: each slab's block of 256 entries names distinct own nodes; it shares no entry with the same slab's block of face_upper. `face_upper`: each slab's block of 256 entries names distinct own nodes; it shares no entry with the same slab's block of face_lower. `cell_matrices`: each cell matrix is symmetric.
All inputs are finite; a program needn't handle non-finite values.
Results may differ from a plain program's by a relative error of at most 0.023.
Values may be sent and summed in bfloat16 or wider, within the bound.
No kernel may reach another device: no remote copies, remote signals or barrier semaphores. Data moves between devices by JAX's collectives and lax.ppermute only.
A program may use at most 64 MiB of HBM per device.

v0:
```python
import functools
import math

import jax
import jax.numpy as jnp
from jax import lax
from jax.experimental import pallas as pl
from jax.experimental.pallas import tpu as pltpu
from jax.sharding import PartitionSpec as P

DEGREE = 4
LANES = 128
SUBLANES = 8
CHUNK = LANES * SUBLANES
PITCH = SUBLANES + 1


def assemble_kernel(outputs, places_ref, column_ref, nodes_ref, cells_ref, *refs):
    total, even_terms, odd_terms, fetched, arrived = refs[-5:]
    out_refs = refs[-5 - outputs : -5]
    cell = pl.program_id(0)
    cells = pl.num_programs(0)
    cell_nodes = fetched.shape[1]
    ext_count = out_refs[0].shape[0]
    parts = CHUNK // 256
    part_rows = cell_nodes // parts
    group = 32

    def fetch(index, slot):
        return pltpu.make_async_copy(cells_ref.at[index], fetched.at[slot], arrived.at[slot])

    def spread_part(part, slot):
        columns = column_ref[:, part * 256 : (part + 1) * 256]
        picker = jnp.concatenate(
            [
                (nodes_ref[0] == columns[:, half * LANES : (half + 1) * LANES])
                .astype(jnp.float32)
                .astype(jnp.bfloat16)
                for half in range(2)
            ],
            axis=1,
        )
        return jnp.dot(fetched[slot], picker, preferred_element_type=jnp.float32)

    def keep_part(part, spread, terms):
        for first in range(0, cell_nodes, SUBLANES):
            for half in range(2):
                terms[pl.ds(first * PITCH + 2 * part + half, SUBLANES, stride=PITCH), :] = spread[
                    first : first + SUBLANES, half * LANES : (half + 1) * LANES
                ]

    def add_part(part, of_cell, terms):
        first = part * part_rows
        for start in range(0, part_rows, group):
            places = [places_ref[of_cell * cell_nodes + first + start + k] for k in range(group)]
            sums = [
                total[pl.ds(places[k], SUBLANES), :]
                + terms[pl.ds((first + start + k) * PITCH, SUBLANES), :]
                for k in range(group)
            ]
            for k in range(group):
                total[pl.ds(places[k], SUBLANES), :] = sums[k]

    @pl.when(cell == 0)
    def _():
        fetch(0, 0).start()
        fetch(1, 1).start()
        total[...] = jnp.zeros_like(total)
        fetch(0, 0).wait()
        for part in range(parts):
            keep_part(part, spread_part(part, 0), even_terms)

    for parity, (before, now) in enumerate(((odd_terms, even_terms), (even_terms, odd_terms))):

        @pl.when((cell > 0) & (cell % 2 == parity))
        def _():
            @pl.when(cell + 1 < cells)
            def _():
                fetch(cell + 1, 1 - parity).start()

            fetch(cell, parity).wait()
            spread = spread_part(0, parity)
            for part in range(parts):
                following = spread_part(part + 1, parity) if part + 1 < parts else None
                add_part(part, cell - 1, before)
                keep_part(part, spread, now)
                spread = following

        @pl.when((cell == cells - 1) & (cell % 2 == parity))
        def _():
            def body(part, carry):
                add_part(part, cell, now)
                return carry

            lax.fori_loop(0, parts, body, 0)

    @pl.when(cell == cells - 1)
    def _():
        per_out = SUBLANES // outputs

        def write_rows(step, carry):
            first = pl.multiple_of(step * 16, 16)
            for block in range(SUBLANES):
                upper = total[pl.ds(first * PITCH + block, SUBLANES, stride=PITCH), :]
                lower = total[pl.ds((first + 8) * PITCH + block, SUBLANES, stride=PITCH), :]
                at = block % per_out * LANES
                out_refs[block // per_out][pl.ds(first, 16), at : at + LANES] = jnp.concatenate(
                    [upper, lower], axis=0
                ).astype(jnp.bfloat16)
            return carry

        lax.fori_loop(0, ext_count // 16, write_rows, 0, unroll=4)


def assemble(places, columns, nodes, cell_matrices, shapes, after, at=0, partial=None):
    cells, cell_nodes, _ = cell_matrices.shape
    ext_count = shapes[0][0]
    width = CHUNK // len(shapes)
    extra = (after,) if partial is None else (after, partial)
    return pl.pallas_call(
        functools.partial(assemble_kernel, len(shapes)),
        out_shape=tuple(jax.ShapeDtypeStruct(shape, jnp.bfloat16) for shape in shapes),
        grid_spec=pltpu.PrefetchScalarGridSpec(
            num_scalar_prefetch=1,
            grid=(cells,),
            in_specs=[
                pl.BlockSpec((1, CHUNK), lambda c, places: (0, 0)),
                pl.BlockSpec((1, cell_nodes, LANES), lambda c, places: (c, 0, 0)),
                pl.BlockSpec(memory_space=pltpu.HBM),
            ]
            + [pl.BlockSpec(memory_space=pl.ANY)] * len(extra),
            out_specs=tuple(pl.BlockSpec((ext_count, width), lambda c, places: (0, at)) for _ in shapes),
            scratch_shapes=[
                pltpu.VMEM((ext_count * PITCH, LANES), jnp.float32),
                pltpu.VMEM((cell_nodes * PITCH, LANES), jnp.float32),
                pltpu.VMEM((cell_nodes * PITCH, LANES), jnp.float32),
                pltpu.VMEM((2, cell_nodes, cell_nodes), jnp.bfloat16),
                pltpu.SemaphoreType.DMA((2,)),
            ],
        ),
        input_output_aliases={} if partial is None else {5: 0},
        compiler_params=pltpu.CompilerParams(vmem_limit_bytes=32 * 1024 * 1024),
        cost_estimate=pl.CostEstimate(
            flops=16 * cells * cell_nodes * cell_nodes * CHUNK,
            bytes_accessed=cells * cell_nodes * cell_nodes * 2 + ext_count * CHUNK * 2,
            transcendentals=0,
        ),
    )(places, columns[None, :], nodes, cell_matrices, *extra)


def join_kernel(left_ref, right_ref, out_ref):
    width = left_ref.shape[1]
    out_ref[:, :width] = left_ref[...]
    out_ref[:, width:] = right_ref[...]


def join(left, right):
    return pl.pallas_call(
        join_kernel,
        out_shape=jax.ShapeDtypeStruct((left.shape[0], left.shape[1] + right.shape[1]), left.dtype),
        compiler_params=pltpu.CompilerParams(vmem_limit_bytes=16 * 1024 * 1024),
    )(left, right)


def own_kernel(first_step, extended_ref, matrix_ref, previous_ref, *refs):
    out_ref = refs[-1]
    width = 256

    def body(step, carry):
        at = pl.ds(pl.multiple_of(step * width, width), width)
        product = jnp.dot(extended_ref[...], matrix_ref[:, at], preferred_element_type=jnp.float32)
        if not first_step:
            product = 2.0 * product - previous_ref[:, at].astype(jnp.float32)
        out_ref[:, at] = product
        return carry

    lax.fori_loop(0, out_ref.shape[1] // width, body, 0)


def own_part(first_step, extended, matrix, previous, after):
    rows, depth = extended.shape
    columns = matrix.shape[1]
    whole = pl.BlockSpec(memory_space=pltpu.VMEM)
    return pl.pallas_call(
        functools.partial(own_kernel, first_step),
        out_shape=jax.ShapeDtypeStruct((rows, columns), jnp.float32),
        in_specs=[whole] * 3 + [pl.BlockSpec(memory_space=pl.ANY)] * len(after),
        out_specs=whole,
        compiler_params=pltpu.CompilerParams(vmem_limit_bytes=16 * 1024 * 1024),
        cost_estimate=pl.CostEstimate(
            flops=8 * rows * depth * columns,
            bytes_accessed=2 * depth * columns + 4 * rows * columns,
            transcendentals=0,
        ),
    )(extended, matrix, previous, *after)


def exact(left, right, contract):
    return lax.dot_general(
        left,
        right,
        (contract, ((), ())),
        precision=lax.Precision.HIGHEST,
        preferred_element_type=jnp.float32,
    )


def inverse_factor(block):
    size = block.shape[0]
    groups = size // SUBLANES
    row = lax.broadcasted_iota(jnp.int32, (SUBLANES, LANES), 0)
    lane = lax.broadcasted_iota(jnp.int32, (SUBLANES, LANES), 1)
    left = [block[g * SUBLANES : (g + 1) * SUBLANES, :] for g in range(groups)]
    right = [(lane == row + g * SUBLANES).astype(jnp.float32) for g in range(groups)]

    def over_rows(values, index):
        return jnp.broadcast_to(values[index : index + 1, :], (SUBLANES, LANES))

    for k in range(groups):
        later = range(k, groups)
        column = {
            g: [
                jnp.broadcast_to(
                    left[g][:, k * SUBLANES + q : k * SUBLANES + q + 1], (SUBLANES, LANES)
                )
                for q in range(SUBLANES)
            ]
            for g in later
        }
        for q in range(SUBLANES):
            scale = lax.rsqrt(over_rows(column[k][q], q))
            factor = {g: column[g][q] * scale for g in later}
            left_row = over_rows(left[k], q) * scale
            right_row = over_rows(right[k], q) * scale
            below = jnp.where(row > q, factor[k], 0.0)
            left[k] = jnp.where(row == q, left_row, left[k] - below * left_row)
            right[k] = jnp.where(row == q, right_row, right[k] - below * right_row)
            for other in range(q + 1, SUBLANES):
                weight = over_rows(factor[k], other)
                for g in later:
                    column[g][other] = column[g][other] - factor[g] * weight
            for g in range(k + 1, groups):
                left[g] = left[g] - factor[g] * left_row
                right[g] = right[g] - factor[g] * right_row
    return jnp.concatenate(right, axis=0)


def orthonormal_kernel(scale, block_ref, gram_ref, filtered_ref, out_ref, inverse):
    size = gram_ref.shape[0]
    count = size // LANES
    at = [slice(i * LANES, (i + 1) * LANES) for i in range(count)]
    lower = {}
    inverses = {}
    for i in range(count):
        diagonal = gram_ref[at[i], at[i]]
        for j in range(i):
            diagonal = diagonal - exact(lower[i, j], lower[i, j], ((1,), (1,)))
        inverses[i, i] = inverse_factor(diagonal)
        for k in range(i + 1, count):
            entry = gram_ref[at[k], at[i]]
            for j in range(i):
                entry = entry - exact(lower[k, j], lower[i, j], ((1,), (1,)))
            lower[k, i] = exact(entry, inverses[i, i], ((1,), (1,)))
    inverse[...] = jnp.zeros_like(inverse)
    for i in range(count):
        for j in range(i):
            entry = exact(lower[i, j], inverses[j, j], ((1,), (0,)))
            for m in range(j + 1, i):
                entry = entry + exact(lower[i, m], inverses[m, j], ((1,), (0,)))
            inverses[i, j] = -exact(inverses[i, i], entry, ((1,), (0,)))
            inverse[at[i], at[j]] = inverses[i, j] * scale
        inverse[at[i], at[i]] = inverses[i, i] * scale
    rows = out_ref.shape[0]
    mine = inverse[pl.ds(pl.multiple_of(block_ref[0] * rows, rows), rows), :]
    high = mine.astype(jnp.bfloat16)
    low = (mine - high.astype(jnp.float32)).astype(jnp.bfloat16)
    width = 512
    for first in range(0, out_ref.shape[1], width):
        part = filtered_ref[:, first : first + width]
        out_ref[:, first : first + width] = jnp.dot(
            high, part, preferred_element_type=jnp.float32
        ) + jnp.dot(low, part, preferred_element_type=jnp.float32)


def orthonormal(block, gram, filtered, rows, scale):
    size = gram.shape[0]
    return pl.pallas_call(
        functools.partial(orthonormal_kernel, scale),
        out_shape=jax.ShapeDtypeStruct((rows, filtered.shape[1]), jnp.float32),
        in_specs=[
            pl.BlockSpec(memory_space=pltpu.SMEM),
            pl.BlockSpec(memory_space=pltpu.VMEM),
            pl.BlockSpec(memory_space=pltpu.VMEM),
        ],
        out_specs=pl.BlockSpec(memory_space=pltpu.VMEM),
        scratch_shapes=[pltpu.VMEM((size, size), jnp.float32)],
        compiler_params=pltpu.CompilerParams(vmem_limit_bytes=16 * 1024 * 1024),
    )(block, gram, filtered)


def swap_pairs(count, first):
    pairs = []
    for low in range(first, count - 1, 2):
        pairs += [(low, low + 1), (low + 1, low)]
    return pairs


def sum_over(values, axis):
    count = lax.axis_size(axis)
    if count & (count - 1):
        return lax.psum(values.astype(jnp.bfloat16), axis).astype(jnp.float32)
    step = 1
    while step < count:
        sent = values.astype(jnp.bfloat16)
        got = lax.ppermute(sent, axis, [(i, i ^ step) for i in range(count)])
        values = sent.astype(jnp.float32) + got.astype(jnp.float32)
        step *= 2
    return values


def per_device(orbitals, cell_matrices, connectivity, face_lower, face_upper):
    own_count = orbitals.shape[1]
    face = face_lower.shape[0]
    ext_count = own_count + 2 * face
    slabs = lax.axis_size("slab")
    slab = lax.axis_index("slab")
    even = slab % 2 == 0

    has_lower = slab > 0
    has_upper = slab < slabs - 1
    has_a = jnp.where(even, has_upper, has_lower)
    has_b = jnp.where(even, has_lower, has_upper)
    ghost_lower = jnp.arange(face, dtype=jnp.int32)
    ghost_upper = ghost_lower + (face + own_count)
    face_a = jnp.where(even, face_upper, face_lower)
    face_b = jnp.where(even, face_lower, face_upper)
    ghost_a = jnp.where(even, ghost_upper, ghost_lower)
    ghost_b = jnp.where(even, ghost_lower, ghost_upper)

    lower_at = jnp.where(even, own_count + face, own_count)
    upper_at = jnp.where(even, own_count, own_count + face)
    places = jnp.where(
        connectivity < face,
        connectivity + lower_at,
        jnp.where(
            connectivity < face + own_count,
            connectivity - face,
            connectivity - (face + own_count) + upper_at,
        ),
    ).reshape(-1) * PITCH
    columns_b = jnp.concatenate([ghost_b, face_b + face])
    columns_a = jnp.concatenate([ghost_a, face_a + face])
    own_columns = jnp.arange(own_count, dtype=jnp.int32) + face
    nodes = jnp.broadcast_to(connectivity[:, :, None], connectivity.shape + (LANES,))

    face_nodes = jnp.concatenate([face_a, face_b])
    face_table = (
        face_nodes[:, None] == lax.broadcasted_iota(jnp.int32, (2 * face, own_count), 1)
    ).astype(jnp.bfloat16)

    pairs_a = swap_pairs(slabs, 0)
    pairs_b = swap_pairs(slabs, 1)

    def times(left, right):
        return jnp.dot(left, right, preferred_element_type=jnp.float32)

    rounded = orbitals.astype(jnp.bfloat16)
    own_start = lax.all_gather(rounded, "orb", axis=0, tiled=True)
    faces = lax.dot_general(
        rounded, face_table, (((1,), (1,)), ((), ())), preferred_element_type=jnp.float32
    ).astype(jnp.bfloat16)
    ghosts_b = lax.ppermute(faces[:, face:], "slab", pairs_b)
    ghosts_a = lax.ppermute(faces[:, :face], "slab", pairs_a)
    ghosts = jnp.concatenate([ghosts_a, ghosts_b], axis=1)
    ghost_start = lax.all_gather(ghosts, "orb", axis=0, tiled=True)

    matrix_b, matrix_a = assemble(
        places,
        jnp.concatenate([columns_b, columns_a]),
        nodes,
        cell_matrices,
        ((ext_count, 2 * face), (ext_count, 2 * face)),
        faces,
    )

    def assemble_own(first, after, partial):
        return assemble(
            places,
            own_columns[first : first + CHUNK],
            nodes,
            cell_matrices,
            ((ext_count, own_count),),
            after,
            first // CHUNK,
            partial,
        )[0]

    own_matrix = None
    for first in range(0, own_count - CHUNK, CHUNK):
        own_matrix = assemble_own(first, ghosts, own_matrix)

    def following(first_step, extended, previous, own_matrix):
        factor = 1.0 if first_step else 2.0
        part_b = times(extended, matrix_b)
        sent_b = part_b.astype(jnp.bfloat16)
        got_b = lax.ppermute(sent_b, "slab", pairs_b)
        part_a = times(extended, matrix_a)
        sent_a = part_a.astype(jnp.bfloat16)
        got_a = lax.ppermute(sent_a, "slab", pairs_a)
        if first_step:
            own_matrix = assemble_own(own_count - CHUNK, sent_a, own_matrix)
        own = own_part(first_step, extended, own_matrix, previous[0], (sent_a, sent_b))
        incoming = jnp.concatenate([got_a[:, :face], got_b[:, :face]], axis=1)
        own = own + factor * times(incoming, face_table)

        def ghosts_of(there, part, got, before):
            value = factor * (part[:, :face] + got[:, face:].astype(jnp.float32))
            if not first_step:
                value = value - before.astype(jnp.float32)
            return jnp.where(there, value, 0.0)

        at_a = ghosts_of(has_a, part_a, got_a, previous[1])
        at_b = ghosts_of(has_b, part_b, got_b, previous[2])
        return (own, at_a, at_b), own_matrix

    def extend(own, at_a, at_b):
        return jnp.concatenate([own, at_a, at_b], axis=1).astype(jnp.bfloat16)

    start = join(own_start, ghost_start)
    previous = (start, start[:, own_count : own_count + face], start[:, own_count + face :])
    current, own_matrix = following(True, start, previous, own_matrix)
    for degree_step in range(1, DEGREE):
        later, _ = following(False, extend(*current), previous, own_matrix)
        previous, current = current, later

    filtered = current[0].astype(jnp.bfloat16)
    gram = lax.dot_general(
        filtered, filtered, (((1,), (1,)), ((), ())), preferred_element_type=jnp.float32
    )
    total = sum_over(gram, "slab")
    block = lax.axis_index("orb").astype(jnp.int32).reshape(1)
    return orthonormal(block, total, filtered, orbitals.shape[0], math.sqrt(own_count * slabs))


def solution(mesh):
    in_specs = (P("orb", "slab"), P("slab", None, None), P("slab", None), P("slab"), P("slab"))
    out_specs = P("orb", "slab")
    return jax.shard_map(
        per_device, mesh=mesh, in_specs=in_specs, out_specs=out_specs, check_vma=False
    )
```

profile of v0, /device:TPU:0, one launch (start us, length us, event | category | flops | bytes accessed | tf_op | source)
XLA Modules:
  0.0 174.7 jit_solution(18074630998992821770)
XLA Ops:
  6.5 1.8 %convert_element_type.90 = bf16[64,2048]{1,0:T(8,128)(2,1)} convert(f32[64,2048]{1,0:T(8,128)} %param.5) | non-fusion elementwise | flops 131072 | bytes 786432 | tf_op jit(solution)/shard_map/convert_element_type | solution.py:367
  9.1 1.9 %fusion.14.refs_0_ = bf16[64,512]{1,0:T(8,128)(2,1)S(1)} fusion(bf16[64,2048]{1,0:T(8,128)(2,1)} %convert_element_type.90, s32[512]{0:T(512)S(1)} %pad_add_fusion.1), kind=kOutput, calls=%fused_computation.23 | convolution fusion | flops 135299072 | bytes 329728 | tf_op jit(solution)/shard_map/dot_general | solution.py:369
  12.9 2.9 %copy-done.6 = bf16[8,512,512]{2,1,0:T(8,128)(2,1)S(1)} copy-done((bf16[8,512,512]{2,1,0:T(8,128)(2,1)S(1)}, bf16[8,512,512]{2,1,0:T(8,128)(2,1)}, u32[]{:S(2)}) %copy-start.6) | copy-done | bytes 4194328
  15.8 14.1 %shard_map.56 = (bf16[2560,512]{1,0:T(8,128)(2,1)S(1)}, bf16[2560,512]{1,0:T(8,128)(2,1)S(1)}) custom-call(s32[4096]{0:T(1024)S(1)} %bitcast.22, s32[1,1024]{1,0:T(1,128)S(1)} %bitcast.25, s32[8,512,128]{2,1,0:T(8,128)S(1)} %broadcast_in_dim.26.nodes_ref, bf16[8,512,512]{2,1,0:T(8,128)(2,1)S(1)} %copy-done.6, bf16[64,512]{1,0:T(8,128)(2,1)S(1)} %fusion.14.refs_0_), custom_call_target="tpu_custom_call" | custom-call | flops 34359738368 | bytes 9437184 | tf_op jit(solution)/shard_map/pallas_call | solution.py:120
  29.9 1.6 copy-done
  31.6 1.6 copy-done.3
  33.2 2.2 %copy-done.7 = bf16[8,512,512]{2,1,0:T(8,128)(2,1)S(1)} copy-done((bf16[8,512,512]{2,1,0:T(8,128)(2,1)S(1)}, bf16[8,512,512]{2,1,0:T(8,128)(2,1)}, u32[]{:S(2)}) %copy-start.7) | copy-done | bytes 4194328
  35.4 14.5 %shard_map.57.refs_1_ = bf16[2560,2048]{1,0:T(8,128)(2,1)S(1)} custom-call(s32[4096]{0:T(1024)S(1)} %bitcast.23, s32[1,1024]{1,0:T(1,128)S(1)} %bitcast.27, s32[8,512,128]{2,1,0:T(8,128)S(1)} %copy-done.3, bf16[8,512,512]{2,1,0:T(8,128)(2,1)S(1)} %copy-done.7, bf16[64,512]{1,0:T(8,128)(2,1)S(1)} %constant_dynamic-update-slice_fusion.refs_0_), custom_call_target="tpu_custom_call" | custom-call | flops 34359738368 | bytes 9437184 | tf_op jit(solution)/shard_map/pallas_call | solution.py:120
  49.9 4.0 %copy-done.9 = bf16[2560,2048]{1,0:T(8,128)(2,1)} copy-done((bf16[2560,2048]{1,0:T(8,128)(2,1)}, bf16[2560,2048]{1,0:T(8,128)(2,1)S(1)}, u32[]{:S(2)}) %copy-start.9) | copy-done | bytes 10485784
  53.9 15.8 %all_gather.7.right_ref = bf16[256,512]{1,0:T(8,128)(2,1)S(1)} all-gather(bf16[64,512]{1,0:T(8,128)(2,1)S(1)} %constant_dynamic-update-slice_fusion.refs_0_), channel_id=1, replica_groups=mesh['slab'=8,'orb'=4] {'orb'}, dimensions={0}, use_global_device_ids=true | all-gather | bytes 327680 | tf_op jit(solution)/shard_map/all_gather | solution.py:375
  69.7 1.2 copy-done.5
  74.8 4.0 %copy-done.10 = bf16[2560,2048]{1,0:T(8,128)(2,1)S(1)} copy-done((bf16[2560,2048]{1,0:T(8,128)(2,1)S(1)}, bf16[2560,2048]{1,0:T(8,128)(2,1)}, u32[]{:S(2)}) %copy-start.10) | copy-done | bytes 10485784
  78.8 14.5 %shard_map.58.matrix_ref = bf16[2560,2048]{1,0:T(8,128)(2,1)S(1)} custom-call(s32[4096]{0:T(1024)S(1)} %bitcast.24, s32[1,1024]{1,0:T(1,128)S(1)} %bitcast.26, s32[8,512,128]{2,1,0:T(8,128)S(1)} %copy-done.4, bf16[8,512,512]{2,1,0:T(8,128)(2,1)S(1)} %copy-done.8, bf16[256,512]{1,0:T(8,128)(2,1)S(1)} %get-tuple-element.27.refs_0_, ...), custom_call_target="tpu_custom_call", output_to_operand_aliasing={{}: (5, {})} | custom-call | flops 34359738368 | bytes 9437184 | tf_op jit(solution)/shard_map/pallas_call | solution.py:120
  93.3 4.3 %shard_map.59 = f32[256,2048]{1,0:T(8,128)S(1)} custom-call(bf16[256,2560]{1,0:T(8,128)(2,1)S(1)} %shard_map.55.extended_ref.previous_ref, bf16[2560,2048]{1,0:T(8,128)(2,1)S(1)} %shard_map.58.matrix_ref, bf16[256,2560]{1,0:T(8,128)(2,1)S(1)} %shard_map.55.extended_ref.previous_ref, bf16[256,512]{1,0:T(8,128)(2,1)S(1)} %get-tuple-element.27.refs_0_, ...), custom_call_target="tpu_custom_call" | custom-call | flops 10737418240 | bytes 12582912 | tf_op jit(solution)/shard_map/pallas_call | solution.py:184
  97.6 1.0 fusion.3
  101.7 5.6 %collective-permute-start.4 = (bf16[256,512]{1,0:T(8,128)(2,1)S(1)}, bf16[256,512]{1,0:T(8,128)(2,1)S(1)}, u32[]{:S(2)}, u32[]{:S(2)}) collective-permute-start(bf16[256,512]{1,0:T(8,128)(2,1)S(1)} %get-tuple-element.29.refs_0_), channel_id=1, source_target_pairs={{0,4},{4,0},{8,12},{12,8},{16,20},{20,16},{24,28},{28,24},{1,5},{5... | collective-permute-start | bytes 786440 | tf_op jit(solution)/shard_map/ppermute | solution.py:409
  107.3 4.3 %shard_map.60 = f32[256,2048]{1,0:T(8,128)S(1)} custom-call(bf16[256,2560]{1,0:T(8,128)(2,1)S(1)} %pad_maximum_fusion.extended_ref, bf16[2560,2048]{1,0:T(8,128)(2,1)S(1)} %shard_map.58.matrix_ref, bf16[256,2560]{1,0:T(8,128)(2,1)S(1)} %shard_map.55.extended_ref.previous_ref, bf16[256,512]{1,0:T(8,128)(2,1)S(1)} %get-tuple-element.29.refs_0_, ...), custom_call_target="tpu_custom_call" | custom-call | flops 10737418240 | bytes 12582912 | tf_op jit(solution)/shard_map/pallas_call | solution.py:184
  111.7 1.1 fusion.5
  115.2 3.6 %collective-permute-start.6 = (bf16[256,512]{1,0:T(8,128)(2,1)S(1)}, bf16[256,512]{1,0:T(8,128)(2,1)S(1)}, u32[]{:S(2)}, u32[]{:S(2)}) collective-permute-start(bf16[256,512]{1,0:T(8,128)(2,1)S(1)} %get-tuple-element.35.refs_0_), channel_id=1, source_target_pairs={{0,4},{4,0},{8,12},{12,8},{16,20},{20,16},{24,28},{28,24},{1,5},{5... | collective-permute-start | bytes 786440 | tf_op jit(solution)/shard_map/ppermute | solution.py:409
  118.8 0.9 collective-permute-start.7
  119.7 4.3 %shard_map.61 = f32[256,2048]{1,0:T(8,128)S(1)} custom-call(bf16[256,2560]{1,0:T(8,128)(2,1)S(1)} %pad_maximum_fusion.1.extended_ref, bf16[2560,2048]{1,0:T(8,128)(2,1)S(1)} %shard_map.58.matrix_ref, f32[256,2048]{1,0:T(8,128)S(1)} %get-tuple-element.12.previous_ref, bf16[256,512]{1,0:T(8,128)(2,1)S(1)} %get-tuple-element.35.refs_0_, ...), custom_call_target="tpu_custom_call" | custom-call | flops 10737418240 | bytes 12582912 | tf_op jit(solution)/shard_map/pallas_call | solution.py:184
  124.1 1.1 fusion.6
  128.9 6.6 %collective-permute-start.8 = (bf16[256,512]{1,0:T(8,128)(2,1)S(1)}, bf16[256,512]{1,0:T(8,128)(2,1)S(1)}, u32[]{:S(2)}, u32[]{:S(2)}) collective-permute-start(bf16[256,512]{1,0:T(8,128)(2,1)S(1)} %convolution_convert_fusion.1.refs_0_), channel_id=1, source_target_pairs={{0,4},{4,0},{8,12},{12,8},{16,20},{20,16},{24,28},{28,24},{1,5},{5... | collective-permute-start | bytes 786440 | tf_op jit(solution)/shard_map/ppermute | solution.py:409
  135.5 4.3 %shard_map.62 = f32[256,2048]{1,0:T(8,128)S(1)} custom-call(bf16[256,2560]{1,0:T(8,128)(2,1)S(1)} %pad_maximum_fusion.2.extended_ref, bf16[2560,2048]{1,0:T(8,128)(2,1)S(1)} %shard_map.58.matrix_ref, f32[256,2048]{1,0:T(8,128)S(1)} %get-tuple-element.10.previous_ref, bf16[256,512]{1,0:T(8,128)(2,1)S(1)} %convolution_convert_fusion.1.refs_0_, ...), custom_call_target="tpu_custom_call" | custom-call | flops 10737418240 | bytes 12582912 | tf_op jit(solution)/shard_map/pallas_call | solution.py:184
  139.8 1.1 fusion.7
  141.8 2.5 %collective-permute-start.10 = (bf16[256,256]{1,0:T(8,128)(2,1)S(1)}, bf16[256,256]{1,0:T(8,128)(2,1)S(1)}, u32[]{:S(2)}, u32[]{:S(2)}) collective-permute-start(bf16[256,256]{1,0:T(8,128)(2,1)S(1)} %convolution_convert_fusion.2), channel_id=1, source_target_pairs={{0,4},{4,0},{8,12},{12,8},{16,20},{20,16},{24,28},{28,24},{1,5},{5... | collective-permute-start | bytes 393224 | tf_op jit(solution)/shard_map/ppermute | solution.py:315
  144.3 1.0 collective-permute-done.10
  145.3 2.3 %collective-permute-start.11 = (bf16[256,256]{1,0:T(8,128)(2,1)S(1)}, bf16[256,256]{1,0:T(8,128)(2,1)S(1)}, u32[]{:S(2)}, u32[]{:S(2)}) collective-permute-start(bf16[256,256]{1,0:T(8,128)(2,1)S(1)} %add_convert_fusion.3), channel_id=1, source_target_pairs={{0,8},{4,12},{8,0},{12,4},{16,24},{20,28},{24,16},{28,20},{1,9},{5... | collective-permute-start | bytes 393224 | tf_op jit(solution)/shard_map/ppermute | solution.py:315
  147.6 4.0 %collective-permute-done.11 = bf16[256,256]{1,0:T(8,128)(2,1)S(1)} collective-permute-done((bf16[256,256]{1,0:T(8,128)(2,1)S(1)}, bf16[256,256]{1,0:T(8,128)(2,1)S(1)}, u32[]{:S(2)}, u32[]{:S(2)}) %collective-permute-start.11) | collective-permute-done | bytes 131104 | tf_op jit(solution)/shard_map/ppermute | solution.py:315
  151.7 3.1 %collective-permute-start.12 = (bf16[256,256]{1,0:T(8,128)(2,1)S(1)}, bf16[256,256]{1,0:T(8,128)(2,1)S(1)}, u32[]{:S(2)}, u32[]{:S(2)}) collective-permute-start(bf16[256,256]{1,0:T(8,128)(2,1)S(1)} %add_convert_fusion.2), channel_id=1, source_target_pairs={{0,16},{4,20},{8,24},{12,28},{16,0},{20,4},{24,8},{28,12},{1,17},{... | collective-permute-start | bytes 393224 | tf_op jit(solution)/shard_map/ppermute | solution.py:315
  154.8 3.0 %collective-permute-done.12 = bf16[256,256]{1,0:T(8,128)(2,1)S(1)} collective-permute-done((bf16[256,256]{1,0:T(8,128)(2,1)S(1)}, bf16[256,256]{1,0:T(8,128)(2,1)S(1)}, u32[]{:S(2)}, u32[]{:S(2)}) %collective-permute-start.12) | collective-permute-done | bytes 131104 | tf_op jit(solution)/shard_map/ppermute | solution.py:315
  157.8 10.1 %shard_map.63 = f32[64,2048]{1,0:T(8,128)} custom-call(s32[1]{0:T(128)} %bitcast.block_ref, f32[256,256]{1,0:T(8,128)S(1)} %convert_add_fusion.gram_ref, bf16[256,2048]{1,0:T(8,128)(2,1)S(1)} %add_convert_fusion.filtered_ref), custom_call_target="tpu_custom_call" | custom-call | tf_op jit(solution)/shard_map/pallas_call | solution.py:287
  (85 shorter events, 16.4 us)
Async XLA Ops:
  6.5 5.7 %copy-start.13 = (s32[8,512]{1,0:T(8,128)S(1)}, s32[8,512]{1,0:T(8,128)}, u32[]{:S(2)}) copy-start(s32[8,512]{1,0:T(8,128)} %param.7) | copy-start | bytes 49156
  6.5 63.1 %all-gather.2.cloned.1.call-start = ((), (), s32[]{:S(2)}) async-start(), calls=%async_computation | async-start | bytes 1310720 | tf_op jit(solution)/shard_map/all_gather | solution.py:368
  11.0 20.5 %collective-permute-start = (bf16[64,256]{1,0:T(8,128)(2,1)S(1)}, bf16[64,256]{1,0:T(8,128)(2,1)S(1)}, u32[]{:S(2)}, u32[]{:S(2)}) collective-permute-start(bf16[64,256]{1,0:T(8,128)(2,1)S(1)} %get-tuple-element.20), channel_id=1, source_target_pairs={{0,4},{4,0},{8,12},{12,8},{16,20},{20,16},{24,28},{28,24},{1,5},{5... | collective-permute-start | bytes 98312 | tf_op jit(solution)/shard_map/ppermute | solution.py:373
  11.5 20.0 %collective-permute-start.1 = (bf16[64,256]{1,0:T(8,128)(2,1)S(1)}, bf16[64,256]{1,0:T(8,128)(2,1)S(1)}, u32[]{:S(2)}, u32[]{:S(2)}) collective-permute-start(bf16[64,256]{1,0:T(8,128)(2,1)S(1)} %get-tuple-element.19), channel_id=1, source_target_pairs={{4,8},{8,4},{12,16},{16,12},{20,24},{24,20},{5,9},{9,5},{13,17},{1... | collective-permute-start | bytes 98312 | tf_op jit(solution)/shard_map/ppermute | solution.py:372
  12.9 17.0 %copy-start.2 = (s32[8,512,128]{2,1,0:T(8,128)}, s32[8,512,128]{2,1,0:T(8,128)S(1)}, u32[]{:S(2)}) copy-start(s32[8,512,128]{2,1,0:T(8,128)S(1)} %broadcast_in_dim.26.nodes_ref) | copy-start | bytes 6291460
  12.9 2.9 %copy-start.6 = (bf16[8,512,512]{2,1,0:T(8,128)(2,1)S(1)}, bf16[8,512,512]{2,1,0:T(8,128)(2,1)}, u32[]{:S(2)}) copy-start(bf16[8,512,512]{2,1,0:T(8,128)(2,1)} %cells_ref.5) | copy-start | bytes 12582916
  29.9 1.6 copy-start
  31.6 1.6 copy-start.3
  33.2 2.2 %copy-start.7 = (bf16[8,512,512]{2,1,0:T(8,128)(2,1)S(1)}, bf16[8,512,512]{2,1,0:T(8,128)(2,1)}, u32[]{:S(2)}) copy-start(bf16[8,512,512]{2,1,0:T(8,128)(2,1)} %cells_ref.5) | copy-start | bytes 12582916
  49.9 4.0 %copy-start.9 = (bf16[2560,2048]{1,0:T(8,128)(2,1)}, bf16[2560,2048]{1,0:T(8,128)(2,1)S(1)}, u32[]{:S(2)}) copy-start(bf16[2560,2048]{1,0:T(8,128)(2,1)S(1)} %shard_map.57.refs_1_) | copy-start | bytes 31457284
  69.7 1.2 copy-start.5
  71.0 1.7 copy-start.1
  71.0 3.8 %copy-start.8 = (bf16[8,512,512]{2,1,0:T(8,128)(2,1)S(1)}, bf16[8,512,512]{2,1,0:T(8,128)(2,1)}, u32[]{:S(2)}) copy-start(bf16[8,512,512]{2,1,0:T(8,128)(2,1)} %cells_ref.5) | copy-start | bytes 12582916
  72.7 2.1 %copy-start.4 = (s32[8,512,128]{2,1,0:T(8,128)S(1)}, s32[8,512,128]{2,1,0:T(8,128)}, u32[]{:S(2)}) copy-start(s32[8,512,128]{2,1,0:T(8,128)} %copy-done.2) | copy-start | bytes 6291460
  73.6 24.0 %collective-permute-start.2 = (bf16[256,512]{1,0:T(8,128)(2,1)S(1)}, bf16[256,512]{1,0:T(8,128)(2,1)S(1)}, u32[]{:S(2)}, u32[]{:S(2)}) collective-permute-start(bf16[256,512]{1,0:T(8,128)(2,1)S(1)} %get-tuple-element.27.refs_0_), channel_id=1, source_target_pairs={{0,4},{4,0},{8,12},{12,8},{16,20},{20,16},{24,28},{28,24},{1,5},{5... | collective-permute-start | bytes 786440 | tf_op jit(solution)/shard_map/ppermute | solution.py:409
  73.9 23.7 %collective-permute-start.3 = (bf16[256,512]{1,0:T(8,128)(2,1)S(1)}, bf16[256,512]{1,0:T(8,128)(2,1)S(1)}, u32[]{:S(2)}, u32[]{:S(2)}) collective-permute-start(bf16[256,512]{1,0:T(8,128)(2,1)S(1)} %get-tuple-element.25.refs_1_), channel_id=1, source_target_pairs={{4,8},{8,4},{12,16},{16,12},{20,24},{24,20},{5,9},{9,5},{13,17},{1... | collective-permute-start | bytes 786440 | tf_op jit(solution)/shard_map/ppermute | solution.py:406
  74.8 4.0 %copy-start.10 = (bf16[2560,2048]{1,0:T(8,128)(2,1)S(1)}, bf16[2560,2048]{1,0:T(8,128)(2,1)}, u32[]{:S(2)}) copy-start(bf16[2560,2048]{1,0:T(8,128)(2,1)} %copy-done.9) | copy-start | bytes 31457284
  97.6 1.5 copy-start.11
  101.0 10.6 %collective-permute-start.5 = (bf16[256,512]{1,0:T(8,128)(2,1)S(1)}, bf16[256,512]{1,0:T(8,128)(2,1)S(1)}, u32[]{:S(2)}, u32[]{:S(2)}) collective-permute-start(bf16[256,512]{1,0:T(8,128)(2,1)S(1)} %get-tuple-element.31.refs_1_), channel_id=1, source_target_pairs={{4,8},{8,4},{12,16},{16,12},{20,24},{24,20},{5,9},{9,5},{13,17},{1... | collective-permute-start | bytes 786440 | tf_op jit(solution)/shard_map/ppermute | solution.py:406
  101.7 9.9 %collective-permute-start.4 = (bf16[256,512]{1,0:T(8,128)(2,1)S(1)}, bf16[256,512]{1,0:T(8,128)(2,1)S(1)}, u32[]{:S(2)}, u32[]{:S(2)}) collective-permute-start(bf16[256,512]{1,0:T(8,128)(2,1)S(1)} %get-tuple-element.29.refs_0_), channel_id=1, source_target_pairs={{0,4},{4,0},{8,12},{12,8},{16,20},{20,16},{24,28},{28,24},{1,5},{5... | collective-permute-start | bytes 786440 | tf_op jit(solution)/shard_map/ppermute | solution.py:409
  115.2 8.8 %collective-permute-start.6 = (bf16[256,512]{1,0:T(8,128)(2,1)S(1)}, bf16[256,512]{1,0:T(8,128)(2,1)S(1)}, u32[]{:S(2)}, u32[]{:S(2)}) collective-permute-start(bf16[256,512]{1,0:T(8,128)(2,1)S(1)} %get-tuple-element.35.refs_0_), channel_id=1, source_target_pairs={{0,4},{4,0},{8,12},{12,8},{16,20},{20,16},{24,28},{28,24},{1,5},{5... | collective-permute-start | bytes 786440 | tf_op jit(solution)/shard_map/ppermute | solution.py:409
  118.8 5.2 %collective-permute-start.7 = (bf16[256,512]{1,0:T(8,128)(2,1)S(1)}, bf16[256,512]{1,0:T(8,128)(2,1)S(1)}, u32[]{:S(2)}, u32[]{:S(2)}) collective-permute-start(bf16[256,512]{1,0:T(8,128)(2,1)S(1)} %get-tuple-element.33.refs_1_), channel_id=1, source_target_pairs={{4,8},{8,4},{12,16},{16,12},{20,24},{24,20},{5,9},{9,5},{13,17},{1... | collective-permute-start | bytes 786440 | tf_op jit(solution)/shard_map/ppermute | solution.py:406
  125.2 1.0 copy-start.12
  128.2 11.6 %collective-permute-start.9 = (bf16[256,512]{1,0:T(8,128)(2,1)S(1)}, bf16[256,512]{1,0:T(8,128)(2,1)S(1)}, u32[]{:S(2)}, u32[]{:S(2)}) collective-permute-start(bf16[256,512]{1,0:T(8,128)(2,1)S(1)} %convolution_convert_fusion.refs_1_), channel_id=1, source_target_pairs={{4,8},{8,4},{12,16},{16,12},{20,24},{24,20},{5,9},{9,5},{13,17},{1... | collective-permute-start | bytes 786440 | tf_op jit(solution)/shard_map/ppermute | solution.py:406
  128.9 10.9 %collective-permute-start.8 = (bf16[256,512]{1,0:T(8,128)(2,1)S(1)}, bf16[256,512]{1,0:T(8,128)(2,1)S(1)}, u32[]{:S(2)}, u32[]{:S(2)}) collective-permute-start(bf16[256,512]{1,0:T(8,128)(2,1)S(1)} %convolution_convert_fusion.1.refs_0_), channel_id=1, source_target_pairs={{0,4},{4,0},{8,12},{12,8},{16,20},{20,16},{24,28},{28,24},{1,5},{5... | collective-permute-start | bytes 786440 | tf_op jit(solution)/shard_map/ppermute | solution.py:409
  141.8 3.5 %collective-permute-start.10 = (bf16[256,256]{1,0:T(8,128)(2,1)S(1)}, bf16[256,256]{1,0:T(8,128)(2,1)S(1)}, u32[]{:S(2)}, u32[]{:S(2)}) collective-permute-start(bf16[256,256]{1,0:T(8,128)(2,1)S(1)} %convolution_convert_fusion.2), channel_id=1, source_target_pairs={{0,4},{4,0},{8,12},{12,8},{16,20},{20,16},{24,28},{28,24},{1,5},{5... | collective-permute-start | bytes 393224 | tf_op jit(solution)/shard_map/ppermute | solution.py:315
  145.3 6.3 %collective-permute-start.11 = (bf16[256,256]{1,0:T(8,128)(2,1)S(1)}, bf16[256,256]{1,0:T(8,128)(2,1)S(1)}, u32[]{:S(2)}, u32[]{:S(2)}) collective-permute-start(bf16[256,256]{1,0:T(8,128)(2,1)S(1)} %add_convert_fusion.3), channel_id=1, source_target_pairs={{0,8},{4,12},{8,0},{12,4},{16,24},{20,28},{24,16},{28,20},{1,9},{5... | collective-permute-start | bytes 393224 | tf_op jit(solution)/shard_map/ppermute | solution.py:315
  151.7 6.0 %collective-permute-start.12 = (bf16[256,256]{1,0:T(8,128)(2,1)S(1)}, bf16[256,256]{1,0:T(8,128)(2,1)S(1)}, u32[]{:S(2)}, u32[]{:S(2)}) collective-permute-start(bf16[256,256]{1,0:T(8,128)(2,1)S(1)} %add_convert_fusion.2), channel_id=1, source_target_pairs={{0,16},{4,20},{8,24},{12,28},{16,0},{20,4},{24,8},{28,12},{1,17},{... | collective-permute-start | bytes 393224 | tf_op jit(solution)/shard_map/ppermute | solution.py:315
Sparse Core Ops, SparseCore 0:
  8.9 30.6 all-gather.1
where the time goes:
time: 175 us
  Pallas kernels  70.4 us (40%)
  starting transfers between devices  28.3 us (16%)
  local copies, waits for them, and re-layouts  19.7 us (11%)
  blocking collectives  15.8 us (9%)
  between operations  14 us (8%)
  matrix products  13.6 us (8%)
  waiting for transfers between devices  8.02 us (5%)
  other arithmetic  4.89 us (3%)
    pallas_call x3, Pallas kernels, assemble(): pl.pallas_call(functools.partial(assemble_kernel, len(shapes)), out_shape...  43 us
    unnamed x30, local copies, waits for them, and re-layouts  19 us
    pallas_call x4, Pallas kernels, own_part(): pl.pallas_call(functools.partial(own_kernel, first_step), out_shape=jax.S...  17.2 us
    ppermute x4, starting transfers between devices, following(): got_a = lax.ppermute(sent_a, 'slab', pairs_a)  16.1 us
    all_gather x1, blocking collectives, per_device(): ghost_start = lax.all_gather(ghosts, 'orb', axis=0, tiled=True)  15.8 us
    dot_general x12, matrix products, times(): return jnp.dot(left, right, preferred_element_type=jnp.float32)  11.2 us
    pallas_call x1, Pallas kernels, orthonormal(): pl.pallas_call(functools.partial(orthonormal_kernel, scale), out_shape=ja...  10.1 us
    ppermute x3, waiting for transfers between devices, sum_over(): got = lax.ppermute(sent, axis, [(i, i ^ step) for i in range(count)])  7.98 us
  transfers between devices with their start and end apart: 14, of which 3 were waited for; matrix products, arithmetic and copies ran while one was open for 2% of the time, Pallas kernels for 34%

commit v1 on v0

--- a/solution.py
+++ b/solution.py
@@ -15,13 +15,15 @@
 PITCH = SUBLANES + 1
 
 
-def assemble_kernel(outputs, places_ref, column_ref, nodes_ref, cells_ref, *refs):
-    total, even_terms, odd_terms, fetched, arrived = refs[-5:]
-    out_refs = refs[-5 - outputs : -5]
-    cell = pl.program_id(0)
-    cells = pl.num_programs(0)
+def assemble_kernel(
+    places_ref, column_ref, nodes_ref, cells_ref, after_ref, shared_b_ref, shared_a_ref, own_ref,
+    total, even_terms, odd_terms, fetched, arrived,
+):
+    chunk = pl.program_id(0)
+    cell = pl.program_id(1)
+    cells = pl.num_programs(1)
     cell_nodes = fetched.shape[1]
-    ext_count = out_refs[0].shape[0]
+    ext_count = own_ref.shape[0]
     parts = CHUNK // 256
     part_rows = cell_nodes // parts
     group = 32
@@ -63,7 +65,10 @@
 
     @pl.when(cell == 0)
     def _():
-        fetch(0, 0).start()
+        @pl.when(chunk == 0)
+        def _():
+            fetch(0, 0).start()
+
         fetch(1, 1).start()
         total[...] = jnp.zeros_like(total)
         fetch(0, 0).wait()
@@ -74,9 +79,9 @@
 
         @pl.when((cell > 0) & (cell % 2 == parity))
         def _():
-            @pl.when(cell + 1 < cells)
+            @pl.when((cell + 1 < cells) | (chunk + 1 < pl.num_programs(0)))
             def _():
-                fetch(cell + 1, 1 - parity).start()
+                fetch(lax.rem(cell + 1, cells), 1 - parity).start()
 
             fetch(cell, parity).wait()
             spread = spread_part(0, parity)
@@ -94,9 +99,8 @@
 
             lax.fori_loop(0, parts, body, 0)
 
-    @pl.when(cell == cells - 1)
-    def _():
-        per_out = SUBLANES // outputs
+    def write_out(*out_refs):
+        per_out = SUBLANES // len(out_refs)
 
         def write_rows(step, carry):
             first = pl.multiple_of(step * 16, 16)
@@ -109,27 +113,43 @@
                 ).astype(jnp.bfloat16)
             return carry
 
-        lax.fori_loop(0, ext_count // 16, write_rows, 0, unroll=4)
-
-
-def assemble(places, columns, nodes, cell_matrices, shapes, after, at=0, partial=None):
+        lax.fori_loop(0, ext_count // 16, write_rows, 0, unroll=8)
+
+    @pl.when((cell == cells - 1) & (chunk == 0))
+    def _():
+        write_out(shared_b_ref, shared_a_ref)
+
+    @pl.when((cell == cells - 1) & (chunk > 0))
+    def _():
+        write_out(own_ref)
+
+
+def assemble(places, columns, nodes, cell_matrices, ext_count, after):
     cells, cell_nodes, _ = cell_matrices.shape
-    ext_count = shapes[0][0]
-    width = CHUNK // len(shapes)
-    extra = (after,) if partial is None else (after, partial)
+    assert cells % 2 == 0
+    count = columns.shape[0]
+    chunks = count // CHUNK
+    half = pl.BlockSpec((ext_count, CHUNK // 2), lambda q, c, places: (0, 0))
     return pl.pallas_call(
-        functools.partial(assemble_kernel, len(shapes)),
-        out_shape=tuple(jax.ShapeDtypeStruct(shape, jnp.bfloat16) for shape in shapes),
+        assemble_kernel,
+        out_shape=tuple(
+            jax.ShapeDtypeStruct((ext_count, width), jnp.bfloat16)
+            for width in (CHUNK // 2, CHUNK // 2, count - CHUNK)
+        ),
         grid_spec=pltpu.PrefetchScalarGridSpec(
             num_scalar_prefetch=1,
-            grid=(cells,),
+            grid=(chunks, cells),
             in_specs=[
-                pl.BlockSpec((1, CHUNK), lambda c, places: (0, 0)),
-                pl.BlockSpec((1, cell_nodes, LANES), lambda c, places: (c, 0, 0)),
+                pl.BlockSpec((1, CHUNK), lambda q, c, places: (0, q)),
+                pl.BlockSpec((1, cell_nodes, LANES), lambda q, c, places: (c, 0, 0)),
                 pl.BlockSpec(memory_space=pltpu.HBM),
-            ]
-            + [pl.BlockSpec(memory_space=pl.ANY)] * len(extra),
-            out_specs=tuple(pl.BlockSpec((ext_count, width), lambda c, places: (0, at)) for _ in shapes),
+                pl.BlockSpec(memory_space=pl.ANY),
+            ],
+            out_specs=(
+                half,
+                half,
+                pl.BlockSpec((ext_count, CHUNK), lambda q, c, places: (0, jnp.maximum(q - 1, 0))),
+            ),
             scratch_shapes=[
                 pltpu.VMEM((ext_count * PITCH, LANES), jnp.float32),
                 pltpu.VMEM((cell_nodes * PITCH, LANES), jnp.float32),
@@ -138,28 +158,25 @@
                 pltpu.SemaphoreType.DMA((2,)),
             ],
         ),
-        input_output_aliases={} if partial is None else {5: 0},
-        compiler_params=pltpu.CompilerParams(vmem_limit_bytes=32 * 1024 * 1024),
+        compiler_params=pltpu.CompilerParams(vmem_limit_bytes=42 * 1024 * 1024),
         cost_estimate=pl.CostEstimate(
-            flops=16 * cells * cell_nodes * cell_nodes * CHUNK,
-            bytes_accessed=cells * cell_nodes * cell_nodes * 2 + ext_count * CHUNK * 2,
+            flops=16 * cells * cell_nodes * cell_nodes * count,
+            bytes_accessed=chunks * cells * cell_nodes * cell_nodes * 2 + ext_count * count * 2,
             transcendentals=0,
         ),
-    )(places, columns[None, :], nodes, cell_matrices, *extra)
-
-
-def join_kernel(left_ref, right_ref, out_ref):
-    width = left_ref.shape[1]
-    out_ref[:, :width] = left_ref[...]
-    out_ref[:, width:] = right_ref[...]
-
-
-def join(left, right):
+    )(places, columns[None, :], nodes, cell_matrices, after)
+
+
+def hold_kernel(in_ref, out_ref):
+    out_ref[...] = in_ref[...]
+
+
+def hold(values):
     return pl.pallas_call(
-        join_kernel,
-        out_shape=jax.ShapeDtypeStruct((left.shape[0], left.shape[1] + right.shape[1]), left.dtype),
+        hold_kernel,
+        out_shape=jax.ShapeDtypeStruct(values.shape, values.dtype),
         compiler_params=pltpu.CompilerParams(vmem_limit_bytes=16 * 1024 * 1024),
-    )(left, right)
+    )(values)
 
 
 def own_kernel(first_step, extended_ref, matrix_ref, previous_ref, *refs):
@@ -365,41 +382,23 @@
         return jnp.dot(left, right, preferred_element_type=jnp.float32)
 
     rounded = orbitals.astype(jnp.bfloat16)
-    own_start = lax.all_gather(rounded, "orb", axis=0, tiled=True)
     faces = lax.dot_general(
         rounded, face_table, (((1,), (1,)), ((), ())), preferred_element_type=jnp.float32
     ).astype(jnp.bfloat16)
     ghosts_b = lax.ppermute(faces[:, face:], "slab", pairs_b)
     ghosts_a = lax.ppermute(faces[:, :face], "slab", pairs_a)
-    ghosts = jnp.concatenate([ghosts_a, ghosts_b], axis=1)
-    ghost_start = lax.all_gather(ghosts, "orb", axis=0, tiled=True)
-
-    matrix_b, matrix_a = assemble(
+    mine = jnp.concatenate([rounded, ghosts_a, ghosts_b], axis=1)
+    gathered = lax.all_gather(mine, "orb", axis=0, tiled=True)
+    matrix_b, matrix_a, own_matrix = assemble(
         places,
-        jnp.concatenate([columns_b, columns_a]),
+        jnp.concatenate([columns_b, columns_a, own_columns]),
         nodes,
         cell_matrices,
-        ((ext_count, 2 * face), (ext_count, 2 * face)),
-        faces,
+        ext_count,
+        mine,
     )
 
-    def assemble_own(first, after, partial):
-        return assemble(
-            places,
-            own_columns[first : first + CHUNK],
-            nodes,
-            cell_matrices,
-            ((ext_count, own_count),),
-            after,
-            first // CHUNK,
-            partial,
-        )[0]
-
-    own_matrix = None
-    for first in range(0, own_count - CHUNK, CHUNK):
-        own_matrix = assemble_own(first, ghosts, own_matrix)
-
-    def following(first_step, extended, previous, own_matrix):
+    def following(first_step, extended, previous):
         factor = 1.0 if first_step else 2.0
         part_b = times(extended, matrix_b)
         sent_b = part_b.astype(jnp.bfloat16)
@@ -407,8 +406,6 @@
         part_a = times(extended, matrix_a)
         sent_a = part_a.astype(jnp.bfloat16)
         got_a = lax.ppermute(sent_a, "slab", pairs_a)
-        if first_step:
-            own_matrix = assemble_own(own_count - CHUNK, sent_a, own_matrix)
         own = own_part(first_step, extended, own_matrix, previous[0], (sent_a, sent_b))
         incoming = jnp.concatenate([got_a[:, :face], got_b[:, :face]], axis=1)
         own = own + factor * times(incoming, face_table)
@@ -421,17 +418,16 @@
 
         at_a = ghosts_of(has_a, part_a, got_a, previous[1])
         at_b = ghosts_of(has_b, part_b, got_b, previous[2])
-        return (own, at_a, at_b), own_matrix
+        return own, at_a, at_b
 
     def extend(own, at_a, at_b):
         return jnp.concatenate([own, at_a, at_b], axis=1).astype(jnp.bfloat16)
 
-    start = join(own_start, ghost_start)
+    start = hold(gathered)
     previous = (start, start[:, own_count : own_count + face], start[:, own_count + face :])
-    current, own_matrix = following(True, start, previous, own_matrix)
+    current = following(True, start, previous)
     for degree_step in range(1, DEGREE):
-        later, _ = following(False, extend(*current), previous, own_matrix)
-        previous, current = current, later
+        previous, current = current, following(False, extend(*current), previous)
 
     filtered = current[0].astype(jnp.bfloat16)
     gram = lax.dot_general(

time: 175 us -> 157 us (0.90)
  blocking collectives: 15.8 us -> 0 us
  local copies, waits for them, and re-layouts: 19.7 us -> 11.8 us
  starting transfers between devices: 28.3 us -> 32.6 us
    all_gather x1 -> x0, blocking collectives: 15.8 us -> none  [per_device(): ghost_start = lax.all_gather(ghosts, 'orb', axis=0, tiled=True)]
    unnamed x30 -> x21, local copies, waits for them, and re-layouts: 19 us -> 11.1 us
    ppermute x4, starting transfers between devices: 16.1 us -> 20.6 us  [following(): got_a = lax.ppermute(sent_a, 'slab', pairs_a)]
    pallas_call x4 -> x2, Pallas kernels: 43.1 us -> 44.1 us  [the longest x1 44 us: assemble(): pl.pallas_call(assemble_kernel, out_shape=tuple((jax.ShapeDtypeStruct((ex...]
  transfers between devices with their start and end apart: 14 -> 14, of which waited for: 3 -> 4; matrix products, arithmetic and copies ran while one was open for 2% -> 1% of each run, Pallas kernels for 34% -> 39%
where the time goes in v1:
time: 157 us
  Pallas kernels  71.5 us (46%)
  starting transfers between devices  32.6 us (21%)
  between operations  14 us (9%)
  matrix products  12.5 us (8%)
  local copies, waits for them, and re-layouts  11.8 us (8%)
  waiting for transfers between devices  9.05 us (6%)
  other arithmetic  5.44 us (3%)
    pallas_call x1, Pallas kernels, assemble(): pl.pallas_call(assemble_kernel, out_shape=tuple((jax.ShapeDtypeStruct((ex...  44 us
    ppermute x4, starting transfers between devices, following(): got_a = lax.ppermute(sent_a, 'slab', pairs_a)  20.6 us
    pallas_call x4, Pallas kernels, own_part(): pl.pallas_call(functools.partial(own_kernel, first_step), out_shape=jax.S...  17.2 us
    dot_general x12, matrix products, times(): return jnp.dot(left, right, preferred_element_type=jnp.float32)  11.1 us
    unnamed x21, local copies, waits for them, and re-layouts  11.1 us
    pallas_call x1, Pallas kernels, orthonormal(): pl.pallas_call(functools.partial(orthonormal_kernel, scale), out_shape=ja...  10.1 us
    ppermute x3, waiting for transfers between devices, sum_over(): got = lax.ppermute(sent, axis, [(i, i ^ step) for i in range(count)])  8.89 us
    ppermute x3, starting transfers between devices, sum_over(): got = lax.ppermute(sent, axis, [(i, i ^ step) for i in range(count)])  7.7 us
  transfers between devices with their start and end apart: 14, of which 4 were waited for; matrix products, arithmetic and copies ran while one was open for 1% of the time, Pallas kernels for 39%

profile of v1, /device:TPU:0, one launch (start us, length us, event | category | flops | bytes accessed | tf_op | source)
XLA Modules:
  0.0 156.8 jit_solution(17878406387056139486)
XLA Ops:
  8.0 1.1 convert_element_type.91
  9.0 0.9 fusion.14
  13.1 2.2 %copy-done.4 = bf16[8,512,512]{2,1,0:T(8,128)(2,1)S(1)} copy-done((bf16[8,512,512]{2,1,0:T(8,128)(2,1)S(1)}, bf16[8,512,512]{2,1,0:T(8,128)(2,1)}, u32[]{:S(2)}) %copy-start.4) | copy-done | bytes 4194328
  15.3 44.0 %shard_map.56 = (bf16[2560,512]{1,0:T(8,128)(2,1)S(1)}, bf16[2560,512]{1,0:T(8,128)(2,1)S(1)}, bf16[2560,2048]{1,0:T(8,128)(2,1)}) custom-call(s32[4096]{0:T(1024)S(1)} %bitcast.20, s32[1,3072]{1,0:T(1,128)S(1)} %bitcast.21, s32[8,512,128]{2,1,0:T(8,128)S(1)} %broadcast_in_dim.20.nodes_ref, bf16[8,512,512]{2,1,0:T(8,128)(2,1)S(1)} %copy-done.4, ...), custom_call_target="tpu_custom_call" | custom-call | flops 103079215104 | bytes 28311552 | tf_op jit(solution)/shard_map/pallas_call | solution.py:133
  59.4 1.6 %copy-done = bf16[2560,512]{1,0:T(8,128)(2,1)} copy-done((bf16[2560,512]{1,0:T(8,128)(2,1)}, bf16[2560,512]{1,0:T(8,128)(2,1)S(1)}, u32[]{:S(2)}) %copy-start) | copy-done | bytes 2621464
  60.9 1.3 copy-done.2
  62.3 1.6 %copy-done.1 = bf16[2560,512]{1,0:T(8,128)(2,1)S(1)} copy-done((bf16[2560,512]{1,0:T(8,128)(2,1)S(1)}, bf16[2560,512]{1,0:T(8,128)(2,1)}, u32[]{:S(2)}) %copy-start.1) | copy-done | bytes 2621464
  64.8 5.3 %collective-permute-start.2 = (bf16[256,512]{1,0:T(8,128)(2,1)S(1)}, bf16[256,512]{1,0:T(8,128)(2,1)S(1)}, u32[]{:S(2)}, u32[]{:S(2)}) collective-permute-start(bf16[256,512]{1,0:T(8,128)(2,1)S(1)} %get-tuple-element.25.refs_0_), channel_id=1, source_target_pairs={{0,4},{4,0},{8,12},{12,8},{16,20},{20,16},{24,28},{28,24},{1,5},{5... | collective-permute-start | bytes 786440 | tf_op jit(solution)/shard_map/ppermute | solution.py:408
  71.7 4.0 %copy-done.5 = bf16[2560,2048]{1,0:T(8,128)(2,1)S(1)} copy-done((bf16[2560,2048]{1,0:T(8,128)(2,1)S(1)}, bf16[2560,2048]{1,0:T(8,128)(2,1)}, u32[]{:S(2)}) %copy-start.5) | copy-done | bytes 10485784
  75.7 4.3 %shard_map.57 = f32[256,2048]{1,0:T(8,128)S(1)} custom-call(bf16[256,2560]{1,0:T(8,128)(2,1)S(1)} %shard_map.55.extended_ref.previous_ref, bf16[2560,2048]{1,0:T(8,128)(2,1)S(1)} %copy-done.5, bf16[256,2560]{1,0:T(8,128)(2,1)S(1)} %shard_map.55.extended_ref.previous_ref, bf16[256,512]{1,0:T(8,128)(2,1)S(1)} %get-tuple-element.25.refs_0_, ...), custom_call_target="tpu_custom_call" | custom-call | flops 10737418240 | bytes 12582912 | tf_op jit(solution)/shard_map/pallas_call | solution.py:201
  80.0 1.0 fusion.3
  81.6 0.9 fusion.60
  82.4 0.8 fusion.61
  83.4 4.4 %collective-permute-start.4 = (bf16[256,512]{1,0:T(8,128)(2,1)S(1)}, bf16[256,512]{1,0:T(8,128)(2,1)S(1)}, u32[]{:S(2)}, u32[]{:S(2)}) collective-permute-start(bf16[256,512]{1,0:T(8,128)(2,1)S(1)} %get-tuple-element.27.refs_0_), channel_id=1, source_target_pairs={{0,4},{4,0},{8,12},{12,8},{16,20},{20,16},{24,28},{28,24},{1,5},{5... | collective-permute-start | bytes 786440 | tf_op jit(solution)/shard_map/ppermute | solution.py:408
  87.8 0.8 collective-permute-start.5
  88.6 4.3 %shard_map.58 = f32[256,2048]{1,0:T(8,128)S(1)} custom-call(bf16[256,2560]{1,0:T(8,128)(2,1)S(1)} %pad_maximum_fusion.extended_ref, bf16[2560,2048]{1,0:T(8,128)(2,1)S(1)} %bitcast.23, bf16[256,2560]{1,0:T(8,128)(2,1)S(1)} %shard_map.55.extended_ref.previous_ref, bf16[256,512]{1,0:T(8,128)(2,1)S(1)} %get-tuple-element.27.refs_0_, ...), custom_call_target="tpu_custom_call" | custom-call | flops 10737418240 | bytes 12582912 | tf_op jit(solution)/shard_map/pallas_call | solution.py:201
  93.0 1.1 fusion.5
  94.7 0.8 fusion.63
  96.5 5.3 %collective-permute-start.6 = (bf16[256,512]{1,0:T(8,128)(2,1)S(1)}, bf16[256,512]{1,0:T(8,128)(2,1)S(1)}, u32[]{:S(2)}, u32[]{:S(2)}) collective-permute-start(bf16[256,512]{1,0:T(8,128)(2,1)S(1)} %get-tuple-element.33.refs_0_), channel_id=1, source_target_pairs={{0,4},{4,0},{8,12},{12,8},{16,20},{20,16},{24,28},{28,24},{1,5},{5... | collective-permute-start | bytes 786440 | tf_op jit(solution)/shard_map/ppermute | solution.py:408
  102.4 4.3 %shard_map.59 = f32[256,2048]{1,0:T(8,128)S(1)} custom-call(bf16[256,2560]{1,0:T(8,128)(2,1)S(1)} %pad_maximum_fusion.1.extended_ref, bf16[2560,2048]{1,0:T(8,128)(2,1)S(1)} %bitcast.23, f32[256,2048]{1,0:T(8,128)S(1)} %get-tuple-element.14.previous_ref, bf16[256,512]{1,0:T(8,128)(2,1)S(1)} %get-tuple-element.33.refs_0_, ...), custom_call_target="tpu_custom_call" | custom-call | flops 10737418240 | bytes 12582912 | tf_op jit(solution)/shard_map/pallas_call | solution.py:201
  106.8 1.1 fusion.6
  110.3 0.9 collective-permute-start.9
  111.2 5.7 %collective-permute-start.8 = (bf16[256,512]{1,0:T(8,128)(2,1)S(1)}, bf16[256,512]{1,0:T(8,128)(2,1)S(1)}, u32[]{:S(2)}, u32[]{:S(2)}) collective-permute-start(bf16[256,512]{1,0:T(8,128)(2,1)S(1)} %convolution_convert_fusion.1.refs_0_), channel_id=1, source_target_pairs={{0,4},{4,0},{8,12},{12,8},{16,20},{20,16},{24,28},{28,24},{1,5},{5... | collective-permute-start | bytes 786440 | tf_op jit(solution)/shard_map/ppermute | solution.py:408
  116.8 4.3 %shard_map.60 = f32[256,2048]{1,0:T(8,128)S(1)} custom-call(bf16[256,2560]{1,0:T(8,128)(2,1)S(1)} %pad_maximum_fusion.2.extended_ref, bf16[2560,2048]{1,0:T(8,128)(2,1)S(1)} %bitcast.23, f32[256,2048]{1,0:T(8,128)S(1)} %get-tuple-element.12.previous_ref, bf16[256,512]{1,0:T(8,128)(2,1)S(1)} %convolution_convert_fusion.1.refs_0_, ...), custom_call_target="tpu_custom_call" | custom-call | flops 10737418240 | bytes 12582912 | tf_op jit(solution)/shard_map/pallas_call | solution.py:201
  121.2 1.1 fusion.7
  123.2 1.9 %collective-permute-start.10 = (bf16[256,256]{1,0:T(8,128)(2,1)S(1)}, bf16[256,256]{1,0:T(8,128)(2,1)S(1)}, u32[]{:S(2)}, u32[]{:S(2)}) collective-permute-start(bf16[256,256]{1,0:T(8,128)(2,1)S(1)} %convolution_convert_fusion.2), channel_id=1, source_target_pairs={{0,4},{4,0},{8,12},{12,8},{16,20},{20,16},{24,28},{28,24},{1,5},{5... | collective-permute-start | bytes 393224 | tf_op jit(solution)/shard_map/ppermute | solution.py:332
  125.1 1.0 collective-permute-done.10
  126.1 4.4 %collective-permute-start.11 = (bf16[256,256]{1,0:T(8,128)(2,1)S(1)}, bf16[256,256]{1,0:T(8,128)(2,1)S(1)}, u32[]{:S(2)}, u32[]{:S(2)}) collective-permute-start(bf16[256,256]{1,0:T(8,128)(2,1)S(1)} %add_convert_fusion.3), channel_id=1, source_target_pairs={{0,8},{4,12},{8,0},{12,4},{16,24},{20,28},{24,16},{28,20},{1,9},{5... | collective-permute-start | bytes 393224 | tf_op jit(solution)/shard_map/ppermute | solution.py:332
  130.5 4.0 %collective-permute-done.11 = bf16[256,256]{1,0:T(8,128)(2,1)S(1)} collective-permute-done((bf16[256,256]{1,0:T(8,128)(2,1)S(1)}, bf16[256,256]{1,0:T(8,128)(2,1)S(1)}, u32[]{:S(2)}, u32[]{:S(2)}) %collective-permute-start.11) | collective-permute-done | bytes 131104 | tf_op jit(solution)/shard_map/ppermute | solution.py:332
  134.6 1.4 collective-permute-start.12
  135.9 3.9 %collective-permute-done.12 = bf16[256,256]{1,0:T(8,128)(2,1)S(1)} collective-permute-done((bf16[256,256]{1,0:T(8,128)(2,1)S(1)}, bf16[256,256]{1,0:T(8,128)(2,1)S(1)}, u32[]{:S(2)}, u32[]{:S(2)}) %collective-permute-start.12) | collective-permute-done | bytes 131104 | tf_op jit(solution)/shard_map/ppermute | solution.py:332
  139.8 10.1 %shard_map.61 = f32[64,2048]{1,0:T(8,128)} custom-call(s32[1]{0:T(128)} %bitcast.block_ref, f32[256,256]{1,0:T(8,128)S(1)} %convert_add_fusion.gram_ref, bf16[256,2048]{1,0:T(8,128)(2,1)S(1)} %add_convert_fusion.filtered_ref), custom_call_target="tpu_custom_call" | custom-call | tf_op jit(solution)/shard_map/pallas_call | solution.py:304
  (75 shorter events, 12.9 us)
Async XLA Ops:
  6.5 4.7 %copy-start.6 = (s32[8,512]{1,0:T(8,128)S(1)}, s32[8,512]{1,0:T(8,128)}, u32[]{:S(2)}) copy-start(s32[8,512]{1,0:T(8,128)} %param.7) | copy-start | bytes 49156
  6.5 54.4 %all-gather.2.cloned.1.call-start = ((), (), s32[]{:S(2)}) async-start(), calls=%async_computation | async-start | bytes 1638400 | tf_op jit(solution)/shard_map/all_gather | solution.py:391
  10.0 1.4 collective-permute-start
  10.5 0.9 collective-permute-start.1
  12.1 1.0 copy-start.3
  13.1 2.2 %copy-start.4 = (bf16[8,512,512]{2,1,0:T(8,128)(2,1)S(1)}, bf16[8,512,512]{2,1,0:T(8,128)(2,1)}, u32[]{:S(2)}) copy-start(bf16[8,512,512]{2,1,0:T(8,128)(2,1)} %cells_ref.1) | copy-start | bytes 12582916
  59.3 1.6 %copy-start = (bf16[2560,512]{1,0:T(8,128)(2,1)}, bf16[2560,512]{1,0:T(8,128)(2,1)S(1)}, u32[]{:S(2)}) copy-start(bf16[2560,512]{1,0:T(8,128)(2,1)S(1)} %get-tuple-element.9) | copy-start | bytes 7864324
  60.9 1.3 copy-start.2
  62.3 1.7 %copy-start.1 = (bf16[2560,512]{1,0:T(8,128)(2,1)S(1)}, bf16[2560,512]{1,0:T(8,128)(2,1)}, u32[]{:S(2)}) copy-start(bf16[2560,512]{1,0:T(8,128)(2,1)} %copy-done) | copy-start | bytes 7864324
  64.8 15.1 %collective-permute-start.2 = (bf16[256,512]{1,0:T(8,128)(2,1)S(1)}, bf16[256,512]{1,0:T(8,128)(2,1)S(1)}, u32[]{:S(2)}, u32[]{:S(2)}) collective-permute-start(bf16[256,512]{1,0:T(8,128)(2,1)S(1)} %get-tuple-element.25.refs_0_), channel_id=1, source_target_pairs={{0,4},{4,0},{8,12},{12,8},{16,20},{20,16},{24,28},{28,24},{1,5},{5... | collective-permute-start | bytes 786440 | tf_op jit(solution)/shard_map/ppermute | solution.py:408
  71.0 9.0 %collective-permute-start.3 = (bf16[256,512]{1,0:T(8,128)(2,1)S(1)}, bf16[256,512]{1,0:T(8,128)(2,1)S(1)}, u32[]{:S(2)}, u32[]{:S(2)}) collective-permute-start(bf16[256,512]{1,0:T(8,128)(2,1)S(1)} %get-tuple-element.23.refs_1_), channel_id=1, source_target_pairs={{4,8},{8,4},{12,16},{16,12},{20,24},{24,20},{5,9},{9,5},{13,17},{1... | collective-permute-start | bytes 786440 | tf_op jit(solution)/shard_map/ppermute | solution.py:405
  71.7 4.0 %copy-start.5 = (bf16[2560,2048]{1,0:T(8,128)(2,1)S(1)}, bf16[2560,2048]{1,0:T(8,128)(2,1)}, u32[]{:S(2)}) copy-start(bf16[2560,2048]{1,0:T(8,128)(2,1)} %get-tuple-element.8.matrix_ref) | copy-start | bytes 31457284
  81.0 7.6 %slice-start = ((s8[10485760]{0:T(1024)(128)(4,1)}), s8[4194304]{0:T(1024)(128)(4,1)S(1)}, s32[]{:S(2)}) async-start(s8[10485760]{0:T(1024)(128)(4,1)} %bitcast.22), calls=%async_computation.1 | async-start | bytes 8388608
  81.5 7.1 %slice-start.1 = ((s8[10485760]{0:T(1024)(128)(4,1)}), s8[4194304]{0:T(1024)(128)(4,1)S(1)}, s32[]{:S(2)}) async-start(s8[10485760]{0:T(1024)(128)(4,1)} %bitcast.22), calls=%async_computation.2 | async-start | bytes 8388608
  82.4 6.2 %slice-start.2 = ((s8[10485760]{0:T(1024)(128)(4,1)}), s8[2097152]{0:T(1024)(128)(4,1)S(1)}, s32[]{:S(2)}) async-start(s8[10485760]{0:T(1024)(128)(4,1)} %bitcast.22), calls=%async_computation.3 | async-start | bytes 4194304
  83.4 9.6 %collective-permute-start.4 = (bf16[256,512]{1,0:T(8,128)(2,1)S(1)}, bf16[256,512]{1,0:T(8,128)(2,1)S(1)}, u32[]{:S(2)}, u32[]{:S(2)}) collective-permute-start(bf16[256,512]{1,0:T(8,128)(2,1)S(1)} %get-tuple-element.27.refs_0_), channel_id=1, source_target_pairs={{0,4},{4,0},{8,12},{12,8},{16,20},{20,16},{24,28},{28,24},{1,5},{5... | collective-permute-start | bytes 786440 | tf_op jit(solution)/shard_map/ppermute | solution.py:408
  87.8 5.2 %collective-permute-start.5 = (bf16[256,512]{1,0:T(8,128)(2,1)S(1)}, bf16[256,512]{1,0:T(8,128)(2,1)S(1)}, u32[]{:S(2)}, u32[]{:S(2)}) collective-permute-start(bf16[256,512]{1,0:T(8,128)(2,1)S(1)} %get-tuple-element.29.refs_1_), channel_id=1, source_target_pairs={{4,8},{8,4},{12,16},{16,12},{20,24},{24,20},{5,9},{9,5},{13,17},{1... | collective-permute-start | bytes 786440 | tf_op jit(solution)/shard_map/ppermute | solution.py:405
  96.5 10.3 %collective-permute-start.6 = (bf16[256,512]{1,0:T(8,128)(2,1)S(1)}, bf16[256,512]{1,0:T(8,128)(2,1)S(1)}, u32[]{:S(2)}, u32[]{:S(2)}) collective-permute-start(bf16[256,512]{1,0:T(8,128)(2,1)S(1)} %get-tuple-element.33.refs_0_), channel_id=1, source_target_pairs={{0,4},{4,0},{8,12},{12,8},{16,20},{20,16},{24,28},{28,24},{1,5},{5... | collective-permute-start | bytes 786440 | tf_op jit(solution)/shard_map/ppermute | solution.py:408
  101.8 5.0 %collective-permute-start.7 = (bf16[256,512]{1,0:T(8,128)(2,1)S(1)}, bf16[256,512]{1,0:T(8,128)(2,1)S(1)}, u32[]{:S(2)}, u32[]{:S(2)}) collective-permute-start(bf16[256,512]{1,0:T(8,128)(2,1)S(1)} %get-tuple-element.31.refs_1_), channel_id=1, source_target_pairs={{4,8},{8,4},{12,16},{16,12},{20,24},{24,20},{5,9},{9,5},{13,17},{1... | collective-permute-start | bytes 786440 | tf_op jit(solution)/shard_map/ppermute | solution.py:405
  110.3 10.9 %collective-permute-start.9 = (bf16[256,512]{1,0:T(8,128)(2,1)S(1)}, bf16[256,512]{1,0:T(8,128)(2,1)S(1)}, u32[]{:S(2)}, u32[]{:S(2)}) collective-permute-start(bf16[256,512]{1,0:T(8,128)(2,1)S(1)} %convolution_convert_fusion.refs_1_), channel_id=1, source_target_pairs={{4,8},{8,4},{12,16},{16,12},{20,24},{24,20},{5,9},{9,5},{13,17},{1... | collective-permute-start | bytes 786440 | tf_op jit(solution)/shard_map/ppermute | solution.py:405
  111.2 10.0 %collective-permute-start.8 = (bf16[256,512]{1,0:T(8,128)(2,1)S(1)}, bf16[256,512]{1,0:T(8,128)(2,1)S(1)}, u32[]{:S(2)}, u32[]{:S(2)}) collective-permute-start(bf16[256,512]{1,0:T(8,128)(2,1)S(1)} %convolution_convert_fusion.1.refs_0_), channel_id=1, source_target_pairs={{0,4},{4,0},{8,12},{12,8},{16,20},{20,16},{24,28},{28,24},{1,5},{5... | collective-permute-start | bytes 786440 | tf_op jit(solution)/shard_map/ppermute | solution.py:408
  123.2 2.9 %collective-permute-start.10 = (bf16[256,256]{1,0:T(8,128)(2,1)S(1)}, bf16[256,256]{1,0:T(8,128)(2,1)S(1)}, u32[]{:S(2)}, u32[]{:S(2)}) collective-permute-start(bf16[256,256]{1,0:T(8,128)(2,1)S(1)} %convolution_convert_fusion.2), channel_id=1, source_target_pairs={{0,4},{4,0},{8,12},{12,8},{16,20},{20,16},{24,28},{28,24},{1,5},{5... | collective-permute-start | bytes 393224 | tf_op jit(solution)/shard_map/ppermute | solution.py:332
  126.1 8.4 %collective-permute-start.11 = (bf16[256,256]{1,0:T(8,128)(2,1)S(1)}, bf16[256,256]{1,0:T(8,128)(2,1)S(1)}, u32[]{:S(2)}, u32[]{:S(2)}) collective-permute-start(bf16[256,256]{1,0:T(8,128)(2,1)S(1)} %add_convert_fusion.3), channel_id=1, source_target_pairs={{0,8},{4,12},{8,0},{12,4},{16,24},{20,28},{24,16},{28,20},{1,9},{5... | collective-permute-start | bytes 393224 | tf_op jit(solution)/shard_map/ppermute | solution.py:332
  134.6 5.3 %collective-permute-start.12 = (bf16[256,256]{1,0:T(8,128)(2,1)S(1)}, bf16[256,256]{1,0:T(8,128)(2,1)S(1)}, u32[]{:S(2)}, u32[]{:S(2)}) collective-permute-start(bf16[256,256]{1,0:T(8,128)(2,1)S(1)} %add_convert_fusion.2), channel_id=1, source_target_pairs={{0,16},{4,20},{8,24},{12,28},{16,0},{20,4},{24,8},{28,12},{1,17},{... | collective-permute-start | bytes 393224 | tf_op jit(solution)/shard_map/ppermute | solution.py:332
Sparse Core Ops, SparseCore 0:
  12.3 39.3 all-gather.1

commit v2 on v1

--- a/solution.py
+++ b/solution.py
@@ -16,22 +16,19 @@
 
 
 def assemble_kernel(
-    places_ref, column_ref, nodes_ref, cells_ref, after_ref, shared_b_ref, shared_a_ref, own_ref,
-    total, even_terms, odd_terms, fetched, arrived,
+    places_ref, column_ref, nodes_ref, cell_ref, after_ref, shared_b_ref, shared_a_ref, own_ref,
+    total, even_terms, odd_terms,
 ):
     chunk = pl.program_id(0)
     cell = pl.program_id(1)
     cells = pl.num_programs(1)
-    cell_nodes = fetched.shape[1]
+    cell_nodes = cell_ref.shape[1]
     ext_count = own_ref.shape[0]
     parts = CHUNK // 256
     part_rows = cell_nodes // parts
     group = 32
 
-    def fetch(index, slot):
-        return pltpu.make_async_copy(cells_ref.at[index], fetched.at[slot], arrived.at[slot])
-
-    def spread_part(part, slot):
+    def spread_part(part):
         columns = column_ref[:, part * 256 : (part + 1) * 256]
         picker = jnp.concatenate(
             [
@@ -42,7 +39,7 @@
             ],
             axis=1,
         )
-        return jnp.dot(fetched[slot], picker, preferred_element_type=jnp.float32)
+        return jnp.dot(cell_ref[0], picker, preferred_element_type=jnp.float32)
 
     def keep_part(part, spread, terms):
         for first in range(0, cell_nodes, SUBLANES):
@@ -65,28 +62,21 @@
 
     @pl.when(cell == 0)
     def _():
-        @pl.when(chunk == 0)
-        def _():
-            fetch(0, 0).start()
-
-        fetch(1, 1).start()
-        total[...] = jnp.zeros_like(total)
-        fetch(0, 0).wait()
+        zero_rows = total.shape[0] // parts
         for part in range(parts):
-            keep_part(part, spread_part(part, 0), even_terms)
+            spread = spread_part(part)
+            total[part * zero_rows : (part + 1) * zero_rows, :] = jnp.zeros(
+                (zero_rows, LANES), jnp.float32
+            )
+            keep_part(part, spread, even_terms)
 
     for parity, (before, now) in enumerate(((odd_terms, even_terms), (even_terms, odd_terms))):
 
         @pl.when((cell > 0) & (cell % 2 == parity))
         def _():
-            @pl.when((cell + 1 < cells) | (chunk + 1 < pl.num_programs(0)))
-            def _():
-                fetch(lax.rem(cell + 1, cells), 1 - parity).start()
-
-            fetch(cell, parity).wait()
-            spread = spread_part(0, parity)
+            spread = spread_part(0)
             for part in range(parts):
-                following = spread_part(part + 1, parity) if part + 1 < parts else None
+                following = spread_part(part + 1) if part + 1 < parts else None
                 add_part(part, cell - 1, before)
                 keep_part(part, spread, now)
                 spread = following
@@ -126,7 +116,6 @@
 
 def assemble(places, columns, nodes, cell_matrices, ext_count, after):
     cells, cell_nodes, _ = cell_matrices.shape
-    assert cells % 2 == 0
     count = columns.shape[0]
     chunks = count // CHUNK
     half = pl.BlockSpec((ext_count, CHUNK // 2), lambda q, c, places: (0, 0))
@@ -142,7 +131,7 @@
             in_specs=[
                 pl.BlockSpec((1, CHUNK), lambda q, c, places: (0, q)),
                 pl.BlockSpec((1, cell_nodes, LANES), lambda q, c, places: (c, 0, 0)),
-                pl.BlockSpec(memory_space=pltpu.HBM),
+                pl.BlockSpec((1, cell_nodes, cell_nodes), lambda q, c, places: (c, 0, 0)),
                 pl.BlockSpec(memory_space=pl.ANY),
             ],
             out_specs=(
@@ -154,11 +143,9 @@
                 pltpu.VMEM((ext_count * PITCH, LANES), jnp.float32),
                 pltpu.VMEM((cell_nodes * PITCH, LANES), jnp.float32),
                 pltpu.VMEM((cell_nodes * PITCH, LANES), jnp.float32),
-                pltpu.VMEM((2, cell_nodes, cell_nodes), jnp.bfloat16),
-                pltpu.SemaphoreType.DMA((2,)),
             ],
         ),
-        compiler_params=pltpu.CompilerParams(vmem_limit_bytes=42 * 1024 * 1024),
+        compiler_params=pltpu.CompilerParams(vmem_limit_bytes=57 * 1024 * 1024),
         cost_estimate=pl.CostEstimate(
             flops=16 * cells * cell_nodes * cell_nodes * count,
             bytes_accessed=chunks * cells * cell_nodes * cell_nodes * 2 + ext_count * count * 2,
@@ -180,30 +167,28 @@
 
 
 def own_kernel(first_step, extended_ref, matrix_ref, previous_ref, *refs):
-    out_ref = refs[-1]
-    width = 256
-
-    def body(step, carry):
-        at = pl.ds(pl.multiple_of(step * width, width), width)
-        product = jnp.dot(extended_ref[...], matrix_ref[:, at], preferred_element_type=jnp.float32)
-        if not first_step:
-            product = 2.0 * product - previous_ref[:, at].astype(jnp.float32)
-        out_ref[:, at] = product
-        return carry
-
-    lax.fori_loop(0, out_ref.shape[1] // width, body, 0)
+    product = jnp.dot(extended_ref[...], matrix_ref[...], preferred_element_type=jnp.float32)
+    if not first_step:
+        product = 2.0 * product - previous_ref[...].astype(jnp.float32)
+    refs[-1][...] = product
 
 
 def own_part(first_step, extended, matrix, previous, after):
     rows, depth = extended.shape
     columns = matrix.shape[1]
-    whole = pl.BlockSpec(memory_space=pltpu.VMEM)
+    width = 256
     return pl.pallas_call(
         functools.partial(own_kernel, first_step),
         out_shape=jax.ShapeDtypeStruct((rows, columns), jnp.float32),
-        in_specs=[whole] * 3 + [pl.BlockSpec(memory_space=pl.ANY)] * len(after),
-        out_specs=whole,
-        compiler_params=pltpu.CompilerParams(vmem_limit_bytes=16 * 1024 * 1024),
+        grid=(columns // width,),
+        in_specs=[
+            pl.BlockSpec((rows, depth), lambda t: (0, 0)),
+            pl.BlockSpec((depth, width), lambda t: (0, t)),
+            pl.BlockSpec((rows, width), lambda t: (0, t)),
+        ]
+        + [pl.BlockSpec(memory_space=pl.ANY)] * len(after),
+        out_specs=pl.BlockSpec((rows, width), lambda t: (0, t)),
+        compiler_params=pltpu.CompilerParams(vmem_limit_bytes=44 * 1024 * 1024),
         cost_estimate=pl.CostEstimate(
             flops=8 * rows * depth * columns,
             bytes_accessed=2 * depth * columns + 4 * rows * columns,
@@ -398,21 +383,24 @@
         mine,
     )
 
-    def following(first_step, extended, previous):
-        factor = 1.0 if first_step else 2.0
-        part_b = times(extended, matrix_b)
+    def following(step, extended, previous):
+        factor = 1.0 if step == 0 else 2.0
+        last = step == DEGREE - 1
+        part_b = times(extended, matrix_b[:, :face] if last else matrix_b)
         sent_b = part_b.astype(jnp.bfloat16)
         got_b = lax.ppermute(sent_b, "slab", pairs_b)
-        part_a = times(extended, matrix_a)
+        part_a = times(extended, matrix_a[:, :face] if last else matrix_a)
         sent_a = part_a.astype(jnp.bfloat16)
         got_a = lax.ppermute(sent_a, "slab", pairs_a)
-        own = own_part(first_step, extended, own_matrix, previous[0], (sent_a, sent_b))
+        own = own_part(step == 0, extended, own_matrix, previous[0], (sent_a, sent_b))
         incoming = jnp.concatenate([got_a[:, :face], got_b[:, :face]], axis=1)
         own = own + factor * times(incoming, face_table)
+        if last:
+            return (own,)
 
         def ghosts_of(there, part, got, before):
             value = factor * (part[:, :face] + got[:, face:].astype(jnp.float32))
-            if not first_step:
+            if step > 0:
                 value = value - before.astype(jnp.float32)
             return jnp.where(there, value, 0.0)
 
@@ -425,9 +413,9 @@
 
     start = hold(gathered)
     previous = (start, start[:, own_count : own_count + face], start[:, own_count + face :])
-    current = following(True, start, previous)
+    current = following(0, start, previous)
     for degree_step in range(1, DEGREE):
-        previous, current = current, following(False, extend(*current), previous)
+        previous, current = current, following(degree_step, extend(*current), previous)
 
     filtered = current[0].astype(jnp.bfloat16)
     gram = lax.dot_general(

time: 157 us -> 157 us (level)
  Pallas kernels: 71.5 us -> 85.9 us
  starting transfers between devices: 32.6 us -> 25.3 us
  local copies, waits for them, and re-layouts: 11.8 us -> 5.36 us
    pallas_call x4, Pallas kernels: 17.2 us -> 32.8 us  [own_part(): pl.pallas_call(functools.partial(own_kernel, first_step), out_shape=jax.S...]
    unnamed x21 -> x11, local copies, waits for them, and re-layouts: 11.1 us -> 3.59 us
    ppermute x4, starting transfers between devices: 20.6 us -> 16.8 us  [following(): got_a = lax.ppermute(sent_a, 'slab', pairs_a)]
    ppermute x3, starting transfers between devices: 7.7 us -> 4.21 us  [sum_over(): got = lax.ppermute(sent, axis, [(i, i ^ step) for i in range(count)])]
  transfers between devices with their start and end apart: 14 -> 14, of which waited for: 4 -> 3; matrix products, arithmetic and copies ran while one was open for 1% -> 2% of each run, Pallas kernels for 39% -> 48%
where the time goes in v2:
time: 157 us; the launch traced here: 156 us
  Pallas kernels  85.9 us (55%)
  starting transfers between devices  25.3 us (16%)
  between operations  13.9 us (9%)
  matrix products  11.9 us (8%)
  waiting for transfers between devices  8.62 us (5%)
  other arithmetic  5.43 us (3%)
  local copies, waits for them, and re-layouts  5.36 us (3%)
    pallas_call x1, Pallas kernels, assemble(): pl.pallas_call(assemble_kernel, out_shape=tuple((jax.ShapeDtypeStruct((ex...  42.9 us
    pallas_call x4, Pallas kernels, own_part(): pl.pallas_call(functools.partial(own_kernel, first_step), out_shape=jax.S...  32.8 us
    ppermute x4, starting transfers between devices, following(): got_a = lax.ppermute(sent_a, 'slab', pairs_a)  16.8 us
    dot_general x12, matrix products, times(): return jnp.dot(left, right, preferred_element_type=jnp.float32)  10.4 us
    pallas_call x1, Pallas kernels, orthonormal(): pl.pallas_call(functools.partial(orthonormal_kernel, scale), out_shape=ja...  10.1 us
    ppermute x3, waiting for transfers between devices, sum_over(): got = lax.ppermute(sent, axis, [(i, i ^ step) for i in range(count)])  8.57 us
    ppermute x3, starting transfers between devices, sum_over(): got = lax.ppermute(sent, axis, [(i, i ^ step) for i in range(count)])  4.21 us
    unnamed x11, local copies, waits for them, and re-layouts  3.59 us
  transfers between devices with their start and end apart: 14, of which 3 were waited for; matrix products, arithmetic and copies ran while one was open for 2% of the time, Pallas kernels for 48%

profile of v2, /device:TPU:0, one launch (start us, length us, event | category | flops | bytes accessed | tf_op | source)
XLA Modules:
  0.0 156.3 jit_solution(8444848571179624190)
XLA Ops:
  8.0 1.1 convert_element_type.91
  9.0 0.9 fusion.24
  12.6 1.7 %broadcast_in_dim.20.nodes_ref = s32[8,512,128]{2,1,0:T(8,128)} broadcast(s32[8,512]{1,0:T(8,128)S(1)} %copy-done.3), dimensions={0,1} | broadcast | bytes 2113536 | tf_op jit(solution)/shard_map/broadcast_in_dim | solution.py:356
  14.3 42.9 %shard_map.56 = (bf16[2560,512]{1,0:T(8,128)(2,1)}, bf16[2560,512]{1,0:T(8,128)(2,1)}, bf16[2560,2048]{1,0:T(8,128)(2,1)}) custom-call(s32[4096]{0:T(1024)} %bitcast.18, s32[1,3072]{1,0:T(1,128)} %bitcast.19, s32[8,512,128]{2,1,0:T(8,128)} %broadcast_in_dim.20.nodes_ref, bf16[8,512,512]{2,1,0:T(8,128)(2,1)} %cell_ref.1, ...), custom_call_target="tpu_custom_call" | custom-call | flops 103079215104 | bytes 28311552 | tf_op jit(solution)/shard_map/pallas_call | solution.py:122
  57.2 1.3 copy-done
  58.6 1.6 %copy-done.2 = bf16[2560,512]{1,0:T(8,128)(2,1)S(1)} copy-done((bf16[2560,512]{1,0:T(8,128)(2,1)S(1)}, bf16[2560,512]{1,0:T(8,128)(2,1)}, u32[]{:S(2)}) %copy-start.2) | copy-done | bytes 2621464
  60.3 0.8 fusion.69
  61.1 4.9 %collective-permute-start.2 = (bf16[256,512]{1,0:T(8,128)(2,1)S(1)}, bf16[256,512]{1,0:T(8,128)(2,1)S(1)}, u32[]{:S(2)}, u32[]{:S(2)}) collective-permute-start(bf16[256,512]{1,0:T(8,128)(2,1)S(1)} %get-tuple-element.25.refs_0_), channel_id=1, source_target_pairs={{0,4},{4,0},{8,12},{12,8},{16,20},{20,16},{24,28},{28,24},{1,5},{5... | collective-permute-start | bytes 786440 | tf_op jit(solution)/shard_map/ppermute | solution.py:394
  66.0 0.8 fusion.68
  67.5 8.2 %shard_map.57 = f32[256,2048]{1,0:T(8,128)S(1)} custom-call(bf16[256,2560]{1,0:T(8,128)(2,1)S(1)} %shard_map.55.extended_ref.previous_ref, bf16[2560,2048]{1,0:T(8,128)(2,1)} %get-tuple-element.8.matrix_ref, bf16[256,2560]{1,0:T(8,128)(2,1)S(1)} %shard_map.55.extended_ref.previous_ref, bf16[256,512]{1,0:T(8,128)(2,1)S(1)} %get-tuple-element.25.refs_0_, ...), custom_call_target="tpu_custom_call" | custom-call | flops 10737418240 | bytes 12582912 | tf_op jit(solution)/shard_map/pallas_call | solution.py:180
  75.8 1.0 fusion.3
  77.3 0.8 fusion.70
  78.1 0.8 fusion.71
  79.1 4.5 %collective-permute-start.4 = (bf16[256,512]{1,0:T(8,128)(2,1)S(1)}, bf16[256,512]{1,0:T(8,128)(2,1)S(1)}, u32[]{:S(2)}, u32[]{:S(2)}) collective-permute-start(bf16[256,512]{1,0:T(8,128)(2,1)S(1)} %get-tuple-element.27.refs_0_), channel_id=1, source_target_pairs={{0,4},{4,0},{8,12},{12,8},{16,20},{20,16},{24,28},{28,24},{1,5},{5... | collective-permute-start | bytes 786440 | tf_op jit(solution)/shard_map/ppermute | solution.py:394
  83.6 0.8 collective-permute-start.5
  84.4 8.2 %shard_map.58 = f32[256,2048]{1,0:T(8,128)S(1)} custom-call(bf16[256,2560]{1,0:T(8,128)(2,1)S(1)} %pad_maximum_fusion.extended_ref, bf16[2560,2048]{1,0:T(8,128)(2,1)} %get-tuple-element.8.matrix_ref, bf16[256,2560]{1,0:T(8,128)(2,1)S(1)} %shard_map.55.extended_ref.previous_ref, bf16[256,512]{1,0:T(8,128)(2,1)S(1)} %get-tuple-element.27.refs_0_, ...), custom_call_target="tpu_custom_call" | custom-call | flops 10737418240 | bytes 12582912 | tf_op jit(solution)/shard_map/pallas_call | solution.py:180
  92.7 1.1 fusion.5
  94.4 0.8 fusion.73
  95.2 0.8 fusion.72
  96.2 3.2 %collective-permute-start.6 = (bf16[256,512]{1,0:T(8,128)(2,1)S(1)}, bf16[256,512]{1,0:T(8,128)(2,1)S(1)}, u32[]{:S(2)}, u32[]{:S(2)}) collective-permute-start(bf16[256,512]{1,0:T(8,128)(2,1)S(1)} %get-tuple-element.33.refs_0_), channel_id=1, source_target_pairs={{0,4},{4,0},{8,12},{12,8},{16,20},{20,16},{24,28},{28,24},{1,5},{5... | collective-permute-start | bytes 786440 | tf_op jit(solution)/shard_map/ppermute | solution.py:394
  100.0 8.2 %shard_map.59 = f32[256,2048]{1,0:T(8,128)S(1)} custom-call(bf16[256,2560]{1,0:T(8,128)(2,1)S(1)} %pad_maximum_fusion.1.extended_ref, bf16[2560,2048]{1,0:T(8,128)(2,1)} %get-tuple-element.8.matrix_ref, f32[256,2048]{1,0:T(8,128)S(1)} %get-tuple-element.14.previous_ref, bf16[256,512]{1,0:T(8,128)(2,1)S(1)} %get-tuple-element.33.refs_0_, ...), custom_call_target="tpu_custom_call" | custom-call | flops 10737418240 | bytes 12582912 | tf_op jit(solution)/shard_map/pallas_call | solution.py:180
  108.3 1.1 fusion.6
  111.1 0.9 collective-permute-start.9
  112.0 4.3 %collective-permute-start.8 = (bf16[256,256]{1,0:T(8,128)(2,1)S(1)}, bf16[256,256]{1,0:T(8,128)(2,1)S(1)}, u32[]{:S(2)}, u32[]{:S(2)}) collective-permute-start(bf16[256,256]{1,0:T(8,128)(2,1)S(1)} %fusion.17.refs_0_), channel_id=1, source_target_pairs={{0,4},{4,0},{8,12},{12,8},{16,20},{20,16},{24,28},{28,24},{1,5},{5... | collective-permute-start | bytes 393224 | tf_op jit(solution)/shard_map/ppermute | solution.py:394
  116.3 8.2 %shard_map.60 = f32[256,2048]{1,0:T(8,128)S(1)} custom-call(bf16[256,2560]{1,0:T(8,128)(2,1)S(1)} %pad_maximum_fusion.2.extended_ref, bf16[2560,2048]{1,0:T(8,128)(2,1)} %get-tuple-element.8.matrix_ref, f32[256,2048]{1,0:T(8,128)S(1)} %get-tuple-element.12.previous_ref, bf16[256,256]{1,0:T(8,128)(2,1)S(1)} %fusion.17.refs_0_, ...), custom_call_target="tpu_custom_call" | custom-call | flops 10737418240 | bytes 12582912 | tf_op jit(solution)/shard_map/pallas_call | solution.py:180
  124.6 1.1 fusion.7
  126.6 1.3 collective-permute-done.10
  128.0 2.5 %collective-permute-start.11 = (bf16[256,256]{1,0:T(8,128)(2,1)S(1)}, bf16[256,256]{1,0:T(8,128)(2,1)S(1)}, u32[]{:S(2)}, u32[]{:S(2)}) collective-permute-start(bf16[256,256]{1,0:T(8,128)(2,1)S(1)} %add_convert_fusion.3), channel_id=1, source_target_pairs={{0,8},{4,12},{8,0},{12,4},{16,24},{20,28},{24,16},{28,20},{1,9},{5... | collective-permute-start | bytes 393224 | tf_op jit(solution)/shard_map/ppermute | solution.py:317
  130.4 3.8 %collective-permute-done.11 = bf16[256,256]{1,0:T(8,128)(2,1)S(1)} collective-permute-done((bf16[256,256]{1,0:T(8,128)(2,1)S(1)}, bf16[256,256]{1,0:T(8,128)(2,1)S(1)}, u32[]{:S(2)}, u32[]{:S(2)}) %collective-permute-start.11) | collective-permute-done | bytes 131104 | tf_op jit(solution)/shard_map/ppermute | solution.py:317
  134.3 1.7 %collective-permute-start.12 = (bf16[256,256]{1,0:T(8,128)(2,1)S(1)}, bf16[256,256]{1,0:T(8,128)(2,1)S(1)}, u32[]{:S(2)}, u32[]{:S(2)}) collective-permute-start(bf16[256,256]{1,0:T(8,128)(2,1)S(1)} %add_convert_fusion.2), channel_id=1, source_target_pairs={{0,16},{4,20},{8,24},{12,28},{16,0},{20,4},{24,8},{28,12},{1,17},{... | collective-permute-start | bytes 393224 | tf_op jit(solution)/shard_map/ppermute | solution.py:317
  135.9 3.4 %collective-permute-done.12 = bf16[256,256]{1,0:T(8,128)(2,1)S(1)} collective-permute-done((bf16[256,256]{1,0:T(8,128)(2,1)S(1)}, bf16[256,256]{1,0:T(8,128)(2,1)S(1)}, u32[]{:S(2)}, u32[]{:S(2)}) %collective-permute-start.12) | collective-permute-done | bytes 131104 | tf_op jit(solution)/shard_map/ppermute | solution.py:317
  139.4 10.1 %shard_map.61 = f32[64,2048]{1,0:T(8,128)} custom-call(s32[1]{0:T(128)} %bitcast.block_ref, f32[256,256]{1,0:T(8,128)S(1)} %convert_add_fusion.gram_ref, bf16[256,2048]{1,0:T(8,128)(2,1)S(1)} %add_convert_fusion.filtered_ref), custom_call_target="tpu_custom_call" | custom-call | tf_op jit(solution)/shard_map/pallas_call | solution.py:289
  (62 shorter events, 9.3 us)
Async XLA Ops:
  6.5 4.7 %copy-start.3 = (s32[8,512]{1,0:T(8,128)S(1)}, s32[8,512]{1,0:T(8,128)}, u32[]{:S(2)}) copy-start(s32[8,512]{1,0:T(8,128)} %param.7) | copy-start | bytes 49156
  6.5 50.7 %all-gather.2.cloned.1.call-start = ((), (), s32[]{:S(2)}) async-start(), calls=%async_computation | async-start | bytes 1638400 | tf_op jit(solution)/shard_map/all_gather | solution.py:376
  10.0 1.9 %collective-permute-start = (bf16[64,256]{1,0:T(8,128)(2,1)S(1)}, bf16[64,256]{1,0:T(8,128)(2,1)S(1)}, u32[]{:S(2)}, u32[]{:S(2)}) collective-permute-start(bf16[64,256]{1,0:T(8,128)(2,1)S(1)} %get-tuple-element.21), channel_id=1, source_target_pairs={{0,4},{4,0},{8,12},{12,8},{16,20},{20,16},{24,28},{28,24},{1,5},{5... | collective-permute-start | bytes 98312 | tf_op jit(solution)/shard_map/ppermute | solution.py:374
  10.5 1.3 collective-permute-start.1
  11.2 3.1 %copy-start.4 = (s32[3072]{0:T(1024)}, s32[3072]{0:T(1024)S(1)}, u32[]{:S(2)}) copy-start(s32[3072]{0:T(1024)S(1)} %add_dynamic-update-slice_fusion) | copy-start | bytes 36868
  57.2 1.3 copy-start
  58.5 1.7 %copy-start.2 = (bf16[2560,512]{1,0:T(8,128)(2,1)S(1)}, bf16[2560,512]{1,0:T(8,128)(2,1)}, u32[]{:S(2)}) copy-start(bf16[2560,512]{1,0:T(8,128)(2,1)} %get-tuple-element.9) | copy-start | bytes 7864324
  60.3 5.7 %copy-start.1 = (bf16[2560,512]{1,0:T(8,128)(2,1)S(1)}, bf16[2560,512]{1,0:T(8,128)(2,1)}, u32[]{:S(2)}) copy-start(bf16[2560,512]{1,0:T(8,128)(2,1)} %get-tuple-element.10) | copy-start | bytes 7864324
  61.1 14.6 %collective-permute-start.2 = (bf16[256,512]{1,0:T(8,128)(2,1)S(1)}, bf16[256,512]{1,0:T(8,128)(2,1)S(1)}, u32[]{:S(2)}, u32[]{:S(2)}) collective-permute-start(bf16[256,512]{1,0:T(8,128)(2,1)S(1)} %get-tuple-element.25.refs_0_), channel_id=1, source_target_pairs={{0,4},{4,0},{8,12},{12,8},{16,20},{20,16},{24,28},{28,24},{1,5},{5... | collective-permute-start | bytes 786440 | tf_op jit(solution)/shard_map/ppermute | solution.py:394
  66.8 8.9 %collective-permute-start.3 = (bf16[256,512]{1,0:T(8,128)(2,1)S(1)}, bf16[256,512]{1,0:T(8,128)(2,1)S(1)}, u32[]{:S(2)}, u32[]{:S(2)}) collective-permute-start(bf16[256,512]{1,0:T(8,128)(2,1)S(1)} %get-tuple-element.23.refs_1_), channel_id=1, source_target_pairs={{4,8},{8,4},{12,16},{16,12},{20,24},{24,20},{5,9},{9,5},{13,17},{1... | collective-permute-start | bytes 786440 | tf_op jit(solution)/shard_map/ppermute | solution.py:391
  79.1 13.6 %collective-permute-start.4 = (bf16[256,512]{1,0:T(8,128)(2,1)S(1)}, bf16[256,512]{1,0:T(8,128)(2,1)S(1)}, u32[]{:S(2)}, u32[]{:S(2)}) collective-permute-start(bf16[256,512]{1,0:T(8,128)(2,1)S(1)} %get-tuple-element.27.refs_0_), channel_id=1, source_target_pairs={{0,4},{4,0},{8,12},{12,8},{16,20},{20,16},{24,28},{28,24},{1,5},{5... | collective-permute-start | bytes 786440 | tf_op jit(solution)/shard_map/ppermute | solution.py:394
  83.6 9.1 %collective-permute-start.5 = (bf16[256,512]{1,0:T(8,128)(2,1)S(1)}, bf16[256,512]{1,0:T(8,128)(2,1)S(1)}, u32[]{:S(2)}, u32[]{:S(2)}) collective-permute-start(bf16[256,512]{1,0:T(8,128)(2,1)S(1)} %get-tuple-element.29.refs_1_), channel_id=1, source_target_pairs={{4,8},{8,4},{12,16},{16,12},{20,24},{24,20},{5,9},{9,5},{13,17},{1... | collective-permute-start | bytes 786440 | tf_op jit(solution)/shard_map/ppermute | solution.py:391
  96.2 12.1 %collective-permute-start.6 = (bf16[256,512]{1,0:T(8,128)(2,1)S(1)}, bf16[256,512]{1,0:T(8,128)(2,1)S(1)}, u32[]{:S(2)}, u32[]{:S(2)}) collective-permute-start(bf16[256,512]{1,0:T(8,128)(2,1)S(1)} %get-tuple-element.33.refs_0_), channel_id=1, source_target_pairs={{0,4},{4,0},{8,12},{12,8},{16,20},{20,16},{24,28},{28,24},{1,5},{5... | collective-permute-start | bytes 786440 | tf_op jit(solution)/shard_map/ppermute | solution.py:394
  99.4 8.9 %collective-permute-start.7 = (bf16[256,512]{1,0:T(8,128)(2,1)S(1)}, bf16[256,512]{1,0:T(8,128)(2,1)S(1)}, u32[]{:S(2)}, u32[]{:S(2)}) collective-permute-start(bf16[256,512]{1,0:T(8,128)(2,1)S(1)} %get-tuple-element.31.refs_1_), channel_id=1, source_target_pairs={{4,8},{8,4},{12,16},{16,12},{20,24},{24,20},{5,9},{9,5},{13,17},{1... | collective-permute-start | bytes 786440 | tf_op jit(solution)/shard_map/ppermute | solution.py:391
  111.1 13.4 %collective-permute-start.9 = (bf16[256,256]{1,0:T(8,128)(2,1)S(1)}, bf16[256,256]{1,0:T(8,128)(2,1)S(1)}, u32[]{:S(2)}, u32[]{:S(2)}) collective-permute-start(bf16[256,256]{1,0:T(8,128)(2,1)S(1)} %fusion.20.refs_1_), channel_id=1, source_target_pairs={{4,8},{8,4},{12,16},{16,12},{20,24},{24,20},{5,9},{9,5},{13,17},{1... | collective-permute-start | bytes 393224 | tf_op jit(solution)/shard_map/ppermute | solution.py:391
  112.0 12.5 %collective-permute-start.8 = (bf16[256,256]{1,0:T(8,128)(2,1)S(1)}, bf16[256,256]{1,0:T(8,128)(2,1)S(1)}, u32[]{:S(2)}, u32[]{:S(2)}) collective-permute-start(bf16[256,256]{1,0:T(8,128)(2,1)S(1)} %fusion.17.refs_0_), channel_id=1, source_target_pairs={{0,4},{4,0},{8,12},{12,8},{16,20},{20,16},{24,28},{28,24},{1,5},{5... | collective-permute-start | bytes 393224 | tf_op jit(solution)/shard_map/ppermute | solution.py:394
  126.5 1.4 collective-permute-start.10
  128.0 6.3 %collective-permute-start.11 = (bf16[256,256]{1,0:T(8,128)(2,1)S(1)}, bf16[256,256]{1,0:T(8,128)(2,1)S(1)}, u32[]{:S(2)}, u32[]{:S(2)}) collective-permute-start(bf16[256,256]{1,0:T(8,128)(2,1)S(1)} %add_convert_fusion.3), channel_id=1, source_target_pairs={{0,8},{4,12},{8,0},{12,4},{16,24},{20,28},{24,16},{28,20},{1,9},{5... | collective-permute-start | bytes 393224 | tf_op jit(solution)/shard_map/ppermute | solution.py:317
  134.3 5.1 %collective-permute-start.12 = (bf16[256,256]{1,0:T(8,128)(2,1)S(1)}, bf16[256,256]{1,0:T(8,128)(2,1)S(1)}, u32[]{:S(2)}, u32[]{:S(2)}) collective-permute-start(bf16[256,256]{1,0:T(8,128)(2,1)S(1)} %add_convert_fusion.2), channel_id=1, source_target_pairs={{0,16},{4,20},{8,24},{12,28},{16,0},{20,4},{24,8},{28,12},{1,17},{... | collective-permute-start | bytes 393224 | tf_op jit(solution)/shard_map/ppermute | solution.py:317
Sparse Core Ops, SparseCore 0:
  12.8 38.9 all-gather.1

commit v3 on v2

--- a/solution.py
+++ b/solution.py
@@ -13,23 +13,27 @@
 SUBLANES = 8
 CHUNK = LANES * SUBLANES
 PITCH = SUBLANES + 1
+TILE = 256
 
 
 def assemble_kernel(
     places_ref, column_ref, nodes_ref, cell_ref, after_ref, shared_b_ref, shared_a_ref, own_ref,
-    total, even_terms, odd_terms,
+    total, even_terms, odd_terms, rounded, sent,
 ):
     chunk = pl.program_id(0)
+    chunks = pl.num_programs(0)
     cell = pl.program_id(1)
     cells = pl.num_programs(1)
     cell_nodes = cell_ref.shape[1]
-    ext_count = own_ref.shape[0]
-    parts = CHUNK // 256
+    ext_count = own_ref.shape[1]
+    share = rounded.shape[1] // (places_ref.shape[0] // (2 * cell_nodes))
+    parts = CHUNK // TILE
     part_rows = cell_nodes // parts
     group = 32
+    table = chunk % 2 * (cells * cell_nodes)
 
     def spread_part(part):
-        columns = column_ref[:, part * 256 : (part + 1) * 256]
+        columns = column_ref[:, part * TILE : (part + 1) * TILE]
         picker = jnp.concatenate(
             [
                 (nodes_ref[0] == columns[:, half * LANES : (half + 1) * LANES])
@@ -51,7 +55,9 @@
     def add_part(part, of_cell, terms):
         first = part * part_rows
         for start in range(0, part_rows, group):
-            places = [places_ref[of_cell * cell_nodes + first + start + k] for k in range(group)]
+            places = [
+                places_ref[table + of_cell * cell_nodes + first + start + k] for k in range(group)
+            ]
             sums = [
                 total[pl.ds(places[k], SUBLANES), :]
                 + terms[pl.ds((first + start + k) * PITCH, SUBLANES), :]
@@ -60,14 +66,59 @@
             for k in range(group):
                 total[pl.ds(places[k], SUBLANES), :] = sums[k]
 
+    def round_rows(first, which, zero):
+        base = (which * ext_count + first) * PITCH
+        for block in range(SUBLANES):
+            upper = total[pl.ds(base + block, SUBLANES, stride=PITCH), :]
+            lower = total[pl.ds(base + SUBLANES * PITCH + block, SUBLANES, stride=PITCH), :]
+            rounded[
+                block // 2, pl.ds(first, 16), block % 2 * LANES : (block % 2 + 1) * LANES
+            ] = jnp.concatenate([upper, lower], axis=0).astype(jnp.bfloat16)
+        if zero:
+            total[pl.ds(pl.multiple_of(base, SUBLANES), 16 * PITCH), :] = jnp.zeros(
+                (16 * PITCH, LANES), jnp.float32
+            )
+
+    def round_part(part):
+        pieces = share // 16
+        for piece in range(part * pieces // parts, (part + 1) * pieces // parts):
+            round_rows(pl.multiple_of(cell * share + piece * 16, 16), 1 - chunk % 2, True)
+
+    def sends(index, of_chunk, to_own):
+        rows = pl.ds(pl.multiple_of(index * share, 16), share)
+        copies = []
+        for part in range(parts):
+            if to_own:
+                target = own_ref.at[(of_chunk - 1) * parts + part, rows]
+            else:
+                half = (shared_b_ref, shared_a_ref)[part // 2]
+                target = half.at[rows, part % 2 * TILE : (part % 2 + 1) * TILE]
+            copies.append(
+                pltpu.make_async_copy(rounded.at[part, rows], target, sent.at[index, part])
+            )
+        return copies
+
+    def wait_share(index):
+        for copy in sends(index, 1, True):
+            copy.wait()
+
+    @pl.when(chunk > 1)
+    def _():
+        wait_share(cell)
+
+    @pl.when((cell == 0) & (chunk == 0))
+    def _():
+        def zero(step, carry):
+            total[pl.ds(pl.multiple_of(step * 64, 64), 64), :] = jnp.zeros((64, LANES), jnp.float32)
+            return carry
+
+        lax.fori_loop(0, ext_count * PITCH // 64, zero, 0, unroll=4)
+
     @pl.when(cell == 0)
     def _():
-        zero_rows = total.shape[0] // parts
         for part in range(parts):
             spread = spread_part(part)
-            total[part * zero_rows : (part + 1) * zero_rows, :] = jnp.zeros(
-                (zero_rows, LANES), jnp.float32
-            )
+            round_part(part)
             keep_part(part, spread, even_terms)
 
     for parity, (before, now) in enumerate(((odd_terms, even_terms), (even_terms, odd_terms))):
@@ -78,6 +129,7 @@
             for part in range(parts):
                 following = spread_part(part + 1) if part + 1 < parts else None
                 add_part(part, cell - 1, before)
+                round_part(part)
                 keep_part(part, spread, now)
                 spread = following
 
@@ -89,41 +141,51 @@
 
             lax.fori_loop(0, parts, body, 0)
 
-    def write_out(*out_refs):
-        per_out = SUBLANES // len(out_refs)
-
-        def write_rows(step, carry):
-            first = pl.multiple_of(step * 16, 16)
-            for block in range(SUBLANES):
-                upper = total[pl.ds(first * PITCH + block, SUBLANES, stride=PITCH), :]
-                lower = total[pl.ds((first + 8) * PITCH + block, SUBLANES, stride=PITCH), :]
-                at = block % per_out * LANES
-                out_refs[block // per_out][pl.ds(first, 16), at : at + LANES] = jnp.concatenate(
-                    [upper, lower], axis=0
-                ).astype(jnp.bfloat16)
+    @pl.when(chunk == 1)
+    def _():
+        for copy in sends(cell, 0, False):
+            copy.start()
+
+    @pl.when(chunk > 1)
+    def _():
+        for copy in sends(cell, chunk - 1, True):
+            copy.start()
+
+    @pl.when((cell == cells - 1) & (chunk == chunks - 1))
+    def _():
+        def last_share(index, carry):
+            wait_share(index)
+
+            def last_rows(piece, inner):
+                round_rows(pl.multiple_of(index * share + piece * 16, 16), chunk % 2, False)
+                return inner
+
+            lax.fori_loop(0, share // 16, last_rows, 0, unroll=4)
+            for copy in sends(index, chunk, True):
+                copy.start()
             return carry
 
-        lax.fori_loop(0, ext_count // 16, write_rows, 0, unroll=8)
-
-    @pl.when((cell == cells - 1) & (chunk == 0))
-    def _():
-        write_out(shared_b_ref, shared_a_ref)
-
-    @pl.when((cell == cells - 1) & (chunk > 0))
-    def _():
-        write_out(own_ref)
+        lax.fori_loop(0, cells, last_share, 0)
+
+        def settle(index, carry):
+            wait_share(index)
+            return carry
+
+        lax.fori_loop(0, cells, settle, 0)
 
 
 def assemble(places, columns, nodes, cell_matrices, ext_count, after):
     cells, cell_nodes, _ = cell_matrices.shape
     count = columns.shape[0]
     chunks = count // CHUNK
-    half = pl.BlockSpec((ext_count, CHUNK // 2), lambda q, c, places: (0, 0))
+    assert chunks > 1 and ext_count % (16 * cells) == 0
+    half = jax.ShapeDtypeStruct((ext_count, CHUNK // 2), jnp.bfloat16)
     return pl.pallas_call(
         assemble_kernel,
-        out_shape=tuple(
-            jax.ShapeDtypeStruct((ext_count, width), jnp.bfloat16)
-            for width in (CHUNK // 2, CHUNK // 2, count - CHUNK)
+        out_shape=(
+            half,
+            half,
+            jax.ShapeDtypeStruct(((count - CHUNK) // TILE, ext_count, TILE), jnp.bfloat16),
         ),
         grid_spec=pltpu.PrefetchScalarGridSpec(
             num_scalar_prefetch=1,
@@ -134,15 +196,13 @@
                 pl.BlockSpec((1, cell_nodes, cell_nodes), lambda q, c, places: (c, 0, 0)),
                 pl.BlockSpec(memory_space=pl.ANY),
             ],
-            out_specs=(
-                half,
-                half,
-                pl.BlockSpec((ext_count, CHUNK), lambda q, c, places: (0, jnp.maximum(q - 1, 0))),
-            ),
+            out_specs=(pl.BlockSpec(memory_space=pl.ANY),) * 3,
             scratch_shapes=[
-                pltpu.VMEM((ext_count * PITCH, LANES), jnp.float32),
+                pltpu.VMEM((2 * ext_count * PITCH, LANES), jnp.float32),
                 pltpu.VMEM((cell_nodes * PITCH, LANES), jnp.float32),
                 pltpu.VMEM((cell_nodes * PITCH, LANES), jnp.float32),
+                pltpu.VMEM((CHUNK // TILE, ext_count, TILE), jnp.bfloat16),
+                pltpu.SemaphoreType.DMA((cells, CHUNK // TILE)),
             ],
         ),
         compiler_params=pltpu.CompilerParams(vmem_limit_bytes=57 * 1024 * 1024),
@@ -151,7 +211,13 @@
             bytes_accessed=chunks * cells * cell_nodes * cell_nodes * 2 + ext_count * count * 2,
             transcendentals=0,
         ),
-    )(places, columns[None, :], nodes, cell_matrices, after)
+    )(
+        jnp.concatenate([places, places + ext_count * PITCH]),
+        columns[None, :],
+        nodes,
+        cell_matrices,
+        after,
+    )
 
 
 def hold_kernel(in_ref, out_ref):
@@ -167,7 +233,7 @@
 
 
 def own_kernel(first_step, extended_ref, matrix_ref, previous_ref, *refs):
-    product = jnp.dot(extended_ref[...], matrix_ref[...], preferred_element_type=jnp.float32)
+    product = jnp.dot(extended_ref[...], matrix_ref[0], preferred_element_type=jnp.float32)
     if not first_step:
         product = 2.0 * product - previous_ref[...].astype(jnp.float32)
     refs[-1][...] = product
@@ -175,15 +241,15 @@
 
 def own_part(first_step, extended, matrix, previous, after):
     rows, depth = extended.shape
-    columns = matrix.shape[1]
-    width = 256
+    tiles, _, width = matrix.shape
+    columns = tiles * width
     return pl.pallas_call(
         functools.partial(own_kernel, first_step),
         out_shape=jax.ShapeDtypeStruct((rows, columns), jnp.float32),
-        grid=(columns // width,),
+        grid=(tiles,),
         in_specs=[
             pl.BlockSpec((rows, depth), lambda t: (0, 0)),
-            pl.BlockSpec((depth, width), lambda t: (0, t)),
+            pl.BlockSpec((1, depth, width), lambda t: (t, 0, 0)),
             pl.BlockSpec((rows, width), lambda t: (0, t)),
         ]
         + [pl.BlockSpec(memory_space=pl.ANY)] * len(after),

time: 157 us -> 156 us (level)
  Pallas kernels: 85.9 us -> 84.2 us
    pallas_call x1, Pallas kernels: 42.9 us -> 41.1 us  [assemble(): pl.pallas_call(assemble_kernel, out_shape=(half, half, jax.ShapeDtypeStru...]
where the time goes in v3:
time: 156 us; the launch traced here: 155 us
  Pallas kernels  84.2 us (54%)
  starting transfers between devices  25.3 us (16%)
  between operations  13.9 us (9%)
  matrix products  11.9 us (8%)
  waiting for transfers between devices  8.64 us (6%)
  other arithmetic  6.04 us (4%)
  local copies, waits for them, and re-layouts  4.75 us (3%)
    pallas_call x1, Pallas kernels, assemble(): pl.pallas_call(assemble_kernel, out_shape=(half, half, jax.ShapeDtypeStru...  41.1 us
    pallas_call x4, Pallas kernels, own_part(): pl.pallas_call(functools.partial(own_kernel, first_step), out_shape=jax.S...  32.8 us
    ppermute x4, starting transfers between devices, following(): got_a = lax.ppermute(sent_a, 'slab', pairs_a)  16.8 us
    dot_general x12, matrix products, times(): return jnp.dot(left, right, preferred_element_type=jnp.float32)  10.4 us
    pallas_call x1, Pallas kernels, orthonormal(): pl.pallas_call(functools.partial(orthonormal_kernel, scale), out_shape=ja...  10.1 us
    ppermute x3, waiting for transfers between devices, sum_over(): got = lax.ppermute(sent, axis, [(i, i ^ step) for i in range(count)])  8.57 us
    ppermute x3, starting transfers between devices, sum_over(): got = lax.ppermute(sent, axis, [(i, i ^ step) for i in range(count)])  4.21 us
  transfers between devices with their start and end apart: 14, of which 3 were waited for; matrix products, arithmetic and copies ran while one was open for 2% of the time, Pallas kernels for 48%

profile of v3, /device:TPU:0, one launch (start us, length us, event | category | flops | bytes accessed | tf_op | source)
XLA Modules:
  0.0 154.6 jit_solution(13834929804512626338)
XLA Ops:
  8.0 1.1 convert_element_type.91
  9.0 0.9 fusion.24
  12.6 1.7 %broadcast_in_dim.20.nodes_ref = s32[8,512,128]{2,1,0:T(8,128)} broadcast(s32[8,512]{1,0:T(8,128)S(1)} %copy-done.3), dimensions={0,1} | broadcast | bytes 2113536 | tf_op jit(solution)/shard_map/broadcast_in_dim | solution.py:422
  14.3 41.1 %shard_map.56 = (bf16[2560,512]{1,0:T(8,128)(2,1)}, bf16[2560,512]{1,0:T(8,128)(2,1)}, bf16[8,2560,256]{2,1,0:T(8,128)(2,1)}) custom-call(s32[8192]{0:T(1024)} %pad_add_fusion.places_ref, s32[1,3072]{1,0:T(1,128)} %bitcast.20, s32[8,512,128]{2,1,0:T(8,128)} %broadcast_in_dim.20.nodes_ref, bf16[8,512,512]{2,1,0:T(8,128)(2,1)} %cell_ref.1, ...), custom_call_target="tpu_custom_call" | custom-call | flops 103079215104 | bytes 28311552 | tf_op jit(solution)/shard_map/pallas_call | solution.py:183
  55.5 1.3 copy-done
  56.9 1.6 %copy-done.2 = bf16[2560,512]{1,0:T(8,128)(2,1)S(1)} copy-done((bf16[2560,512]{1,0:T(8,128)(2,1)S(1)}, bf16[2560,512]{1,0:T(8,128)(2,1)}, u32[]{:S(2)}) %copy-start.2) | copy-done | bytes 2621464
  58.6 0.8 fusion.69
  59.4 4.9 %collective-permute-start.2 = (bf16[256,512]{1,0:T(8,128)(2,1)S(1)}, bf16[256,512]{1,0:T(8,128)(2,1)S(1)}, u32[]{:S(2)}, u32[]{:S(2)}) collective-permute-start(bf16[256,512]{1,0:T(8,128)(2,1)S(1)} %get-tuple-element.25.refs_0_), channel_id=1, source_target_pairs={{0,4},{4,0},{8,12},{12,8},{16,20},{20,16},{24,28},{28,24},{1,5},{5... | collective-permute-start | bytes 786440 | tf_op jit(solution)/shard_map/ppermute | solution.py:460
  64.3 0.8 fusion.68
  65.8 8.2 %shard_map.57 = f32[256,2048]{1,0:T(8,128)S(1)} custom-call(bf16[256,2560]{1,0:T(8,128)(2,1)S(1)} %shard_map.55.extended_ref.previous_ref, bf16[8,2560,256]{2,1,0:T(8,128)(2,1)} %get-tuple-element.8.matrix_ref, bf16[256,2560]{1,0:T(8,128)(2,1)S(1)} %shard_map.55.extended_ref.previous_ref, bf16[256,512]{1,0:T(8,128)(2,1)S(1)} %get-tuple-element.25.refs_0_, ...), custom_call_target="tpu_custom_call" | custom-call | flops 10737418240 | bytes 12582912 | tf_op jit(solution)/shard_map/pallas_call | solution.py:246
  74.0 1.0 fusion.3
  75.6 0.8 fusion.70
  76.4 0.8 fusion.71
  77.4 4.5 %collective-permute-start.4 = (bf16[256,512]{1,0:T(8,128)(2,1)S(1)}, bf16[256,512]{1,0:T(8,128)(2,1)S(1)}, u32[]{:S(2)}, u32[]{:S(2)}) collective-permute-start(bf16[256,512]{1,0:T(8,128)(2,1)S(1)} %get-tuple-element.27.refs_0_), channel_id=1, source_target_pairs={{0,4},{4,0},{8,12},{12,8},{16,20},{20,16},{24,28},{28,24},{1,5},{5... | collective-permute-start | bytes 786440 | tf_op jit(solution)/shard_map/ppermute | solution.py:460
  81.9 0.8 collective-permute-start.5
  82.7 8.2 %shard_map.58 = f32[256,2048]{1,0:T(8,128)S(1)} custom-call(bf16[256,2560]{1,0:T(8,128)(2,1)S(1)} %pad_maximum_fusion.extended_ref, bf16[8,2560,256]{2,1,0:T(8,128)(2,1)} %get-tuple-element.8.matrix_ref, bf16[256,2560]{1,0:T(8,128)(2,1)S(1)} %shard_map.55.extended_ref.previous_ref, bf16[256,512]{1,0:T(8,128)(2,1)S(1)} %get-tuple-element.27.refs_0_, ...), custom_call_target="tpu_custom_call" | custom-call | flops 10737418240 | bytes 12582912 | tf_op jit(solution)/shard_map/pallas_call | solution.py:246
  91.0 1.1 fusion.5
  92.7 0.8 fusion.73
  93.5 0.8 fusion.72
  94.5 3.2 %collective-permute-start.6 = (bf16[256,512]{1,0:T(8,128)(2,1)S(1)}, bf16[256,512]{1,0:T(8,128)(2,1)S(1)}, u32[]{:S(2)}, u32[]{:S(2)}) collective-permute-start(bf16[256,512]{1,0:T(8,128)(2,1)S(1)} %get-tuple-element.33.refs_0_), channel_id=1, source_target_pairs={{0,4},{4,0},{8,12},{12,8},{16,20},{20,16},{24,28},{28,24},{1,5},{5... | collective-permute-start | bytes 786440 | tf_op jit(solution)/shard_map/ppermute | solution.py:460
  98.3 8.2 %shard_map.59 = f32[256,2048]{1,0:T(8,128)S(1)} custom-call(bf16[256,2560]{1,0:T(8,128)(2,1)S(1)} %pad_maximum_fusion.1.extended_ref, bf16[8,2560,256]{2,1,0:T(8,128)(2,1)} %get-tuple-element.8.matrix_ref, f32[256,2048]{1,0:T(8,128)S(1)} %get-tuple-element.14.previous_ref, bf16[256,512]{1,0:T(8,128)(2,1)S(1)} %get-tuple-element.33.refs_0_, ...), custom_call_target="tpu_custom_call" | custom-call | flops 10737418240 | bytes 12582912 | tf_op jit(solution)/shard_map/pallas_call | solution.py:246
  106.6 1.1 fusion.6
  109.4 0.9 collective-permute-start.9
  110.3 4.3 %collective-permute-start.8 = (bf16[256,256]{1,0:T(8,128)(2,1)S(1)}, bf16[256,256]{1,0:T(8,128)(2,1)S(1)}, u32[]{:S(2)}, u32[]{:S(2)}) collective-permute-start(bf16[256,256]{1,0:T(8,128)(2,1)S(1)} %fusion.17.refs_0_), channel_id=1, source_target_pairs={{0,4},{4,0},{8,12},{12,8},{16,20},{20,16},{24,28},{28,24},{1,5},{5... | collective-permute-start | bytes 393224 | tf_op jit(solution)/shard_map/ppermute | solution.py:460
  114.6 8.2 %shard_map.60 = f32[256,2048]{1,0:T(8,128)S(1)} custom-call(bf16[256,2560]{1,0:T(8,128)(2,1)S(1)} %pad_maximum_fusion.2.extended_ref, bf16[8,2560,256]{2,1,0:T(8,128)(2,1)} %get-tuple-element.8.matrix_ref, f32[256,2048]{1,0:T(8,128)S(1)} %get-tuple-element.12.previous_ref, bf16[256,256]{1,0:T(8,128)(2,1)S(1)} %fusion.17.refs_0_, ...), custom_call_target="tpu_custom_call" | custom-call | flops 10737418240 | bytes 12582912 | tf_op jit(solution)/shard_map/pallas_call | solution.py:246
  122.8 1.1 fusion.7
  124.9 1.3 collective-permute-done.10
  126.2 2.5 %collective-permute-start.11 = (bf16[256,256]{1,0:T(8,128)(2,1)S(1)}, bf16[256,256]{1,0:T(8,128)(2,1)S(1)}, u32[]{:S(2)}, u32[]{:S(2)}) collective-permute-start(bf16[256,256]{1,0:T(8,128)(2,1)S(1)} %add_convert_fusion.3), channel_id=1, source_target_pairs={{0,8},{4,12},{8,0},{12,4},{16,24},{20,28},{24,16},{28,20},{1,9},{5... | collective-permute-start | bytes 393224 | tf_op jit(solution)/shard_map/ppermute | solution.py:383
  128.7 3.8 %collective-permute-done.11 = bf16[256,256]{1,0:T(8,128)(2,1)S(1)} collective-permute-done((bf16[256,256]{1,0:T(8,128)(2,1)S(1)}, bf16[256,256]{1,0:T(8,128)(2,1)S(1)}, u32[]{:S(2)}, u32[]{:S(2)}) %collective-permute-start.11) | collective-permute-done | bytes 131104 | tf_op jit(solution)/shard_map/ppermute | solution.py:383
  132.5 1.7 %collective-permute-start.12 = (bf16[256,256]{1,0:T(8,128)(2,1)S(1)}, bf16[256,256]{1,0:T(8,128)(2,1)S(1)}, u32[]{:S(2)}, u32[]{:S(2)}) collective-permute-start(bf16[256,256]{1,0:T(8,128)(2,1)S(1)} %add_convert_fusion.2), channel_id=1, source_target_pairs={{0,16},{4,20},{8,24},{12,28},{16,0},{20,4},{24,8},{28,12},{1,17},{... | collective-permute-start | bytes 393224 | tf_op jit(solution)/shard_map/ppermute | solution.py:383
  134.2 3.4 %collective-permute-done.12 = bf16[256,256]{1,0:T(8,128)(2,1)S(1)} collective-permute-done((bf16[256,256]{1,0:T(8,128)(2,1)S(1)}, bf16[256,256]{1,0:T(8,128)(2,1)S(1)}, u32[]{:S(2)}, u32[]{:S(2)}) %collective-permute-start.12) | collective-permute-done | bytes 131104 | tf_op jit(solution)/shard_map/ppermute | solution.py:383
  137.7 10.1 %shard_map.61 = f32[64,2048]{1,0:T(8,128)} custom-call(s32[1]{0:T(128)} %bitcast.block_ref, f32[256,256]{1,0:T(8,128)S(1)} %convert_add_fusion.gram_ref, bf16[256,2048]{1,0:T(8,128)(2,1)S(1)} %add_convert_fusion.filtered_ref), custom_call_target="tpu_custom_call" | custom-call | tf_op jit(solution)/shard_map/pallas_call | solution.py:355
  (64 shorter events, 9.3 us)
Async XLA Ops:
  6.5 4.7 %copy-start.3 = (s32[8,512]{1,0:T(8,128)S(1)}, s32[8,512]{1,0:T(8,128)}, u32[]{:S(2)}) copy-start(s32[8,512]{1,0:T(8,128)} %param.7) | copy-start | bytes 49156
  6.5 49.0 %all-gather.2.cloned.1.call-start = ((), (), s32[]{:S(2)}) async-start(), calls=%async_computation | async-start | bytes 1638400 | tf_op jit(solution)/shard_map/all_gather | solution.py:442
  10.0 1.9 %collective-permute-start = (bf16[64,256]{1,0:T(8,128)(2,1)S(1)}, bf16[64,256]{1,0:T(8,128)(2,1)S(1)}, u32[]{:S(2)}, u32[]{:S(2)}) collective-permute-start(bf16[64,256]{1,0:T(8,128)(2,1)S(1)} %get-tuple-element.21), channel_id=1, source_target_pairs={{0,4},{4,0},{8,12},{12,8},{16,20},{20,16},{24,28},{28,24},{1,5},{5... | collective-permute-start | bytes 98312 | tf_op jit(solution)/shard_map/ppermute | solution.py:440
  10.5 1.3 collective-permute-start.1
  11.9 2.5 %copy-start.4 = (s32[3072]{0:T(1024)}, s32[3072]{0:T(1024)S(1)}, u32[]{:S(2)}) copy-start(s32[3072]{0:T(1024)S(1)} %add_dynamic-update-slice_fusion) | copy-start | bytes 36868
  55.5 1.3 copy-start
  56.8 1.7 %copy-start.2 = (bf16[2560,512]{1,0:T(8,128)(2,1)S(1)}, bf16[2560,512]{1,0:T(8,128)(2,1)}, u32[]{:S(2)}) copy-start(bf16[2560,512]{1,0:T(8,128)(2,1)} %get-tuple-element.9) | copy-start | bytes 7864324
  58.6 5.7 %copy-start.1 = (bf16[2560,512]{1,0:T(8,128)(2,1)S(1)}, bf16[2560,512]{1,0:T(8,128)(2,1)}, u32[]{:S(2)}) copy-start(bf16[2560,512]{1,0:T(8,128)(2,1)} %get-tuple-element.10) | copy-start | bytes 7864324
  59.4 14.6 %collective-permute-start.2 = (bf16[256,512]{1,0:T(8,128)(2,1)S(1)}, bf16[256,512]{1,0:T(8,128)(2,1)S(1)}, u32[]{:S(2)}, u32[]{:S(2)}) collective-permute-start(bf16[256,512]{1,0:T(8,128)(2,1)S(1)} %get-tuple-element.25.refs_0_), channel_id=1, source_target_pairs={{0,4},{4,0},{8,12},{12,8},{16,20},{20,16},{24,28},{28,24},{1,5},{5... | collective-permute-start | bytes 786440 | tf_op jit(solution)/shard_map/ppermute | solution.py:460
  65.1 8.9 %collective-permute-start.3 = (bf16[256,512]{1,0:T(8,128)(2,1)S(1)}, bf16[256,512]{1,0:T(8,128)(2,1)S(1)}, u32[]{:S(2)}, u32[]{:S(2)}) collective-permute-start(bf16[256,512]{1,0:T(8,128)(2,1)S(1)} %get-tuple-element.23.refs_1_), channel_id=1, source_target_pairs={{4,8},{8,4},{12,16},{16,12},{20,24},{24,20},{5,9},{9,5},{13,17},{1... | collective-permute-start | bytes 786440 | tf_op jit(solution)/shard_map/ppermute | solution.py:457
  77.4 13.6 %collective-permute-start.4 = (bf16[256,512]{1,0:T(8,128)(2,1)S(1)}, bf16[256,512]{1,0:T(8,128)(2,1)S(1)}, u32[]{:S(2)}, u32[]{:S(2)}) collective-permute-start(bf16[256,512]{1,0:T(8,128)(2,1)S(1)} %get-tuple-element.27.refs_0_), channel_id=1, source_target_pairs={{0,4},{4,0},{8,12},{12,8},{16,20},{20,16},{24,28},{28,24},{1,5},{5... | collective-permute-start | bytes 786440 | tf_op jit(solution)/shard_map/ppermute | solution.py:460
  81.9 9.1 %collective-permute-start.5 = (bf16[256,512]{1,0:T(8,128)(2,1)S(1)}, bf16[256,512]{1,0:T(8,128)(2,1)S(1)}, u32[]{:S(2)}, u32[]{:S(2)}) collective-permute-start(bf16[256,512]{1,0:T(8,128)(2,1)S(1)} %get-tuple-element.29.refs_1_), channel_id=1, source_target_pairs={{4,8},{8,4},{12,16},{16,12},{20,24},{24,20},{5,9},{9,5},{13,17},{1... | collective-permute-start | bytes 786440 | tf_op jit(solution)/shard_map/ppermute | solution.py:457
  94.5 12.1 %collective-permute-start.6 = (bf16[256,512]{1,0:T(8,128)(2,1)S(1)}, bf16[256,512]{1,0:T(8,128)(2,1)S(1)}, u32[]{:S(2)}, u32[]{:S(2)}) collective-permute-start(bf16[256,512]{1,0:T(8,128)(2,1)S(1)} %get-tuple-element.33.refs_0_), channel_id=1, source_target_pairs={{0,4},{4,0},{8,12},{12,8},{16,20},{20,16},{24,28},{28,24},{1,5},{5... | collective-permute-start | bytes 786440 | tf_op jit(solution)/shard_map/ppermute | solution.py:460
  97.6 8.9 %collective-permute-start.7 = (bf16[256,512]{1,0:T(8,128)(2,1)S(1)}, bf16[256,512]{1,0:T(8,128)(2,1)S(1)}, u32[]{:S(2)}, u32[]{:S(2)}) collective-permute-start(bf16[256,512]{1,0:T(8,128)(2,1)S(1)} %get-tuple-element.31.refs_1_), channel_id=1, source_target_pairs={{4,8},{8,4},{12,16},{16,12},{20,24},{24,20},{5,9},{9,5},{13,17},{1... | collective-permute-start | bytes 786440 | tf_op jit(solution)/shard_map/ppermute | solution.py:457
  109.4 13.4 %collective-permute-start.9 = (bf16[256,256]{1,0:T(8,128)(2,1)S(1)}, bf16[256,256]{1,0:T(8,128)(2,1)S(1)}, u32[]{:S(2)}, u32[]{:S(2)}) collective-permute-start(bf16[256,256]{1,0:T(8,128)(2,1)S(1)} %fusion.20.refs_1_), channel_id=1, source_target_pairs={{4,8},{8,4},{12,16},{16,12},{20,24},{24,20},{5,9},{9,5},{13,17},{1... | collective-permute-start | bytes 393224 | tf_op jit(solution)/shard_map/ppermute | solution.py:457
  110.3 12.5 %collective-permute-start.8 = (bf16[256,256]{1,0:T(8,128)(2,1)S(1)}, bf16[256,256]{1,0:T(8,128)(2,1)S(1)}, u32[]{:S(2)}, u32[]{:S(2)}) collective-permute-start(bf16[256,256]{1,0:T(8,128)(2,1)S(1)} %fusion.17.refs_0_), channel_id=1, source_target_pairs={{0,4},{4,0},{8,12},{12,8},{16,20},{20,16},{24,28},{28,24},{1,5},{5... | collective-permute-start | bytes 393224 | tf_op jit(solution)/shard_map/ppermute | solution.py:460
  124.8 1.4 collective-permute-start.10
  126.2 6.3 %collective-permute-start.11 = (bf16[256,256]{1,0:T(8,128)(2,1)S(1)}, bf16[256,256]{1,0:T(8,128)(2,1)S(1)}, u32[]{:S(2)}, u32[]{:S(2)}) collective-permute-start(bf16[256,256]{1,0:T(8,128)(2,1)S(1)} %add_convert_fusion.3), channel_id=1, source_target_pairs={{0,8},{4,12},{8,0},{12,4},{16,24},{20,28},{24,16},{28,20},{1,9},{5... | collective-permute-start | bytes 393224 | tf_op jit(solution)/shard_map/ppermute | solution.py:383
  132.5 5.1 %collective-permute-start.12 = (bf16[256,256]{1,0:T(8,128)(2,1)S(1)}, bf16[256,256]{1,0:T(8,128)(2,1)S(1)}, u32[]{:S(2)}, u32[]{:S(2)}) collective-permute-start(bf16[256,256]{1,0:T(8,128)(2,1)S(1)} %add_convert_fusion.2), channel_id=1, source_target_pairs={{0,16},{4,20},{8,24},{12,28},{16,0},{20,4},{24,8},{28,12},{1,17},{... | collective-permute-start | bytes 393224 | tf_op jit(solution)/shard_map/ppermute | solution.py:383
Sparse Core Ops, SparseCore 0:
  12.8 38.9 all-gather.1

commit v4 on v3

--- a/solution.py
+++ b/solution.py
@@ -12,8 +12,23 @@
 LANES = 128
 SUBLANES = 8
 CHUNK = LANES * SUBLANES
-PITCH = SUBLANES + 1
 TILE = 256
+
+
+def turn(tiles):
+    row = lax.broadcasted_iota(jnp.int32, (SUBLANES, LANES), 0)
+    tiles = [pltpu.roll(tile, i, 0) if i else tile for i, tile in enumerate(tiles)]
+    step = 1
+    while step < SUBLANES:
+        far = (row & step) != 0
+        tiles = [
+            jnp.where(far, tiles[(i + step) % SUBLANES], tiles[i]) for i in range(SUBLANES)
+        ]
+        step *= 2
+    tiles = [tiles[-i % SUBLANES] for i in range(SUBLANES)]
+    return [
+        pltpu.roll(tile, SUBLANES - i, 0) if i else tile for i, tile in enumerate(tiles)
+    ]
 
 
 def assemble_kernel(
@@ -46,38 +61,44 @@
         return jnp.dot(cell_ref[0], picker, preferred_element_type=jnp.float32)
 
     def keep_part(part, spread, terms):
-        for first in range(0, cell_nodes, SUBLANES):
-            for half in range(2):
-                terms[pl.ds(first * PITCH + 2 * part + half, SUBLANES, stride=PITCH), :] = spread[
-                    first : first + SUBLANES, half * LANES : (half + 1) * LANES
-                ]
+        for half in range(2):
+            terms[2 * part + half] = spread[:, half * LANES : (half + 1) * LANES]
 
     def add_part(part, of_cell, terms):
-        first = part * part_rows
+        first = part * part_rows if isinstance(part, int) else pl.multiple_of(part * part_rows, part_rows)
         for start in range(0, part_rows, group):
             places = [
-                places_ref[table + of_cell * cell_nodes + first + start + k] for k in range(group)
-            ]
-            sums = [
-                total[pl.ds(places[k], SUBLANES), :]
-                + terms[pl.ds((first + start + k) * PITCH, SUBLANES), :]
+                pl.multiple_of(
+                    places_ref[table + of_cell * cell_nodes + first + start + k], SUBLANES
+                )
                 for k in range(group)
             ]
+            added = []
+            for inner in range(0, group, SUBLANES):
+                added += turn(
+                    [terms[b, pl.ds(first + start + inner, SUBLANES), :] for b in range(SUBLANES)]
+                )
+            sums = [total[pl.ds(places[k], SUBLANES), :] + added[k] for k in range(group)]
             for k in range(group):
                 total[pl.ds(places[k], SUBLANES), :] = sums[k]
 
     def round_rows(first, which, zero):
-        base = (which * ext_count + first) * PITCH
+        base = pl.multiple_of((which * ext_count + first) * SUBLANES, 16 * SUBLANES)
+        upper, lower = (
+            turn(
+                [
+                    total[pl.ds(base + (start + i) * SUBLANES, SUBLANES), :]
+                    for i in range(SUBLANES)
+                ]
+            )
+            for start in (0, SUBLANES)
+        )
         for block in range(SUBLANES):
-            upper = total[pl.ds(base + block, SUBLANES, stride=PITCH), :]
-            lower = total[pl.ds(base + SUBLANES * PITCH + block, SUBLANES, stride=PITCH), :]
             rounded[
                 block // 2, pl.ds(first, 16), block % 2 * LANES : (block % 2 + 1) * LANES
-            ] = jnp.concatenate([upper, lower], axis=0).astype(jnp.bfloat16)
+            ] = jnp.concatenate([upper[block], lower[block]], axis=0).astype(jnp.bfloat16)
         if zero:
-            total[pl.ds(pl.multiple_of(base, SUBLANES), 16 * PITCH), :] = jnp.zeros(
-                (16 * PITCH, LANES), jnp.float32
-            )
+            total[pl.ds(base, 16 * SUBLANES), :] = jnp.zeros((16 * SUBLANES, LANES), jnp.float32)
 
     def round_part(part):
         pieces = share // 16
@@ -112,7 +133,7 @@
             total[pl.ds(pl.multiple_of(step * 64, 64), 64), :] = jnp.zeros((64, LANES), jnp.float32)
             return carry
 
-        lax.fori_loop(0, ext_count * PITCH // 64, zero, 0, unroll=4)
+        lax.fori_loop(0, ext_count * SUBLANES // 64, zero, 0, unroll=4)
 
     @pl.when(cell == 0)
     def _():
@@ -198,9 +219,9 @@
             ],
             out_specs=(pl.BlockSpec(memory_space=pl.ANY),) * 3,
             scratch_shapes=[
-                pltpu.VMEM((2 * ext_count * PITCH, LANES), jnp.float32),
-                pltpu.VMEM((cell_nodes * PITCH, LANES), jnp.float32),
-                pltpu.VMEM((cell_nodes * PITCH, LANES), jnp.float32),
+                pltpu.VMEM((2 * ext_count * SUBLANES, LANES), jnp.float32),
+                pltpu.VMEM((SUBLANES, cell_nodes, LANES), jnp.float32),
+                pltpu.VMEM((SUBLANES, cell_nodes, LANES), jnp.float32),
                 pltpu.VMEM((CHUNK // TILE, ext_count, TILE), jnp.bfloat16),
                 pltpu.SemaphoreType.DMA((cells, CHUNK // TILE)),
             ],
@@ -212,7 +233,7 @@
             transcendentals=0,
         ),
     )(
-        jnp.concatenate([places, places + ext_count * PITCH]),
+        jnp.concatenate([places, places + ext_count * SUBLANES]),
         columns[None, :],
         nodes,
         cell_matrices,
@@ -233,28 +254,30 @@
 
 
 def own_kernel(first_step, extended_ref, matrix_ref, previous_ref, *refs):
-    product = jnp.dot(extended_ref[...], matrix_ref[0], preferred_element_type=jnp.float32)
-    if not first_step:
-        product = 2.0 * product - previous_ref[...].astype(jnp.float32)
-    refs[-1][...] = product
+    out_ref = refs[-1]
+
+    def body(tile, carry):
+        at = pl.ds(pl.multiple_of(tile * TILE, TILE), TILE)
+        product = jnp.dot(extended_ref[...], matrix_ref[tile], preferred_element_type=jnp.float32)
+        if not first_step:
+            product = 2.0 * product - previous_ref[:, at].astype(jnp.float32)
+        out_ref[:, at] = product
+        return carry
+
+    lax.fori_loop(0, matrix_ref.shape[0], body, 0)
 
 
 def own_part(first_step, extended, matrix, previous, after):
     rows, depth = extended.shape
     tiles, _, width = matrix.shape
     columns = tiles * width
+    whole = pl.BlockSpec(memory_space=pltpu.VMEM)
     return pl.pallas_call(
         functools.partial(own_kernel, first_step),
         out_shape=jax.ShapeDtypeStruct((rows, columns), jnp.float32),
-        grid=(tiles,),
-        in_specs=[
-            pl.BlockSpec((rows, depth), lambda t: (0, 0)),
-            pl.BlockSpec((1, depth, width), lambda t: (t, 0, 0)),
-            pl.BlockSpec((rows, width), lambda t: (0, t)),
-        ]
-        + [pl.BlockSpec(memory_space=pl.ANY)] * len(after),
-        out_specs=pl.BlockSpec((rows, width), lambda t: (0, t)),
-        compiler_params=pltpu.CompilerParams(vmem_limit_bytes=44 * 1024 * 1024),
+        in_specs=[whole] * 3 + [pl.BlockSpec(memory_space=pl.ANY)] * len(after),
+        out_specs=whole,
+        compiler_params=pltpu.CompilerParams(vmem_limit_bytes=16 * 1024 * 1024),
         cost_estimate=pl.CostEstimate(
             flops=8 * rows * depth * columns,
             bytes_accessed=2 * depth * columns + 4 * rows * columns,
@@ -415,7 +438,7 @@
             connectivity - face,
             connectivity - (face + own_count) + upper_at,
         ),
-    ).reshape(-1) * PITCH
+    ).reshape(-1) * SUBLANES
     columns_b = jnp.concatenate([ghost_b, face_b + face])
     columns_a = jnp.concatenate([ghost_a, face_a + face])
     own_columns = jnp.arange(own_count, dtype=jnp.int32) + face

time: 156 us -> 156 us (level)
  Pallas kernels: 84.2 us -> 72 us
  starting transfers between devices: 25.3 us -> 33.5 us
  matrix products: 11.9 us -> 15.5 us
    pallas_call x4, Pallas kernels: 32.8 us -> 16.3 us  [own_part(): pl.pallas_call(functools.partial(own_kernel, first_step), out_shape=jax.S...]
    ppermute x4, starting transfers between devices: 16.8 us -> 23.2 us  [following(): got_a = lax.ppermute(sent_a, 'slab', pairs_a)]
    pallas_call x1, Pallas kernels: 41.1 us -> 45.5 us  [assemble(): pl.pallas_call(assemble_kernel, out_shape=(half, half, jax.ShapeDtypeStru...]
    dot_general x12, matrix products: 10.4 us -> 14.1 us  [times(): return jnp.dot(left, right, preferred_element_type=jnp.float32)]
    ppermute x3, starting transfers between devices: 4.21 us -> 6.06 us  [sum_over(): got = lax.ppermute(sent, axis, [(i, i ^ step) for i in range(count)])]
    unnamed x11 -> x13, local copies, waits for them, and re-layouts: 2.98 us -> 3.41 us
  transfers between devices with their start and end apart: 14 -> 14, of which waited for: 3 -> 3; matrix products, arithmetic and copies ran while one was open for 2% -> 3% of each run, Pallas kernels for 48% -> 40%
where the time goes in v4:
time: 156 us; the launch traced here: 155 us
  Pallas kernels  72 us (46%)
  starting transfers between devices  33.5 us (21%)
  matrix products  15.5 us (10%)
  between operations  13.9 us (9%)
  waiting for transfers between devices  8.69 us (6%)
  other arithmetic  6.09 us (4%)
  local copies, waits for them, and re-layouts  5.2 us (3%)
    pallas_call x1, Pallas kernels, assemble(): pl.pallas_call(assemble_kernel, out_shape=(half, half, jax.ShapeDtypeStru...  45.5 us
    ppermute x4, starting transfers between devices, following(): got_a = lax.ppermute(sent_a, 'slab', pairs_a)  23.2 us
    pallas_call x4, Pallas kernels, own_part(): pl.pallas_call(functools.partial(own_kernel, first_step), out_shape=jax.S...  16.3 us
    dot_general x12, matrix products, times(): return jnp.dot(left, right, preferred_element_type=jnp.float32)  14.1 us
    pallas_call x1, Pallas kernels, orthonormal(): pl.pallas_call(functools.partial(orthonormal_kernel, scale), out_shape=ja...  10.1 us
    ppermute x3, waiting for transfers between devices, sum_over(): got = lax.ppermute(sent, axis, [(i, i ^ step) for i in range(count)])  8.62 us
    ppermute x3, starting transfers between devices, sum_over(): got = lax.ppermute(sent, axis, [(i, i ^ step) for i in range(count)])  6.06 us
    unnamed x13, local copies, waits for them, and re-layouts  3.41 us
  transfers between devices with their start and end apart: 14, of which 3 were waited for; matrix products, arithmetic and copies ran while one was open for 3% of the time, Pallas kernels for 40%

profile of v4, /device:TPU:0, one launch (start us, length us, event | category | flops | bytes accessed | tf_op | source)
XLA Modules:
  0.0 154.9 jit_solution(1867290376186010011)
XLA Ops:
  8.0 1.1 convert_element_type.91
  9.0 0.9 fusion.24
  12.6 1.7 %broadcast_in_dim.20.nodes_ref = s32[8,512,128]{2,1,0:T(8,128)} broadcast(s32[8,512]{1,0:T(8,128)S(1)} %copy-done.4), dimensions={0,1} | broadcast | bytes 2113536 | tf_op jit(solution)/shard_map/broadcast_in_dim | solution.py:445
  14.4 45.5 %shard_map.56 = (bf16[2560,512]{1,0:T(8,128)(2,1)}, bf16[2560,512]{1,0:T(8,128)(2,1)}, bf16[8,2560,256]{2,1,0:T(8,128)(2,1)}) custom-call(s32[8192]{0:T(1024)} %pad_add_fusion.places_ref, s32[1,3072]{1,0:T(1,128)} %bitcast.20, s32[8,512,128]{2,1,0:T(8,128)} %broadcast_in_dim.20.nodes_ref, bf16[8,512,512]{2,1,0:T(8,128)(2,1)} %cell_ref.1, ...), custom_call_target="tpu_custom_call" | custom-call | flops 103079215104 | bytes 28311552 | tf_op jit(solution)/shard_map/pallas_call | solution.py:204
  59.9 1.3 copy-done
  61.3 2.7 %fusion.69 = (bf16[256,512]{1,0:T(8,128)(2,1)S(1)}, f32[256,512]{1,0:T(8,128)S(1)}) fusion(bf16[256,2560]{1,0:T(8,128)(2,1)S(1)} %shard_map.55.extended_ref.previous_ref, bf16[2560,512]{1,0:T(8,128)(2,1)} %get-tuple-element.9), kind=kOutput, calls=%fused_computation.94 | convolution fusion | flops 671219712 | bytes 4718592 | tf_op jit(solution)/shard_map/dot_general | solution.py:456
  64.1 4.8 %collective-permute-start.2 = (bf16[256,512]{1,0:T(8,128)(2,1)S(1)}, bf16[256,512]{1,0:T(8,128)(2,1)S(1)}, u32[]{:S(2)}, u32[]{:S(2)}) collective-permute-start(bf16[256,512]{1,0:T(8,128)(2,1)S(1)} %get-tuple-element.25.refs_0_), channel_id=1, source_target_pairs={{0,4},{4,0},{8,12},{12,8},{16,20},{20,16},{24,28},{28,24},{1,5},{5... | collective-permute-start | bytes 786440 | tf_op jit(solution)/shard_map/ppermute | solution.py:483
  68.9 2.6 %fusion.68 = (bf16[256,512]{1,0:T(8,128)(2,1)S(1)}, f32[256,512]{1,0:T(8,128)S(1)}) fusion(bf16[256,2560]{1,0:T(8,128)(2,1)S(1)} %shard_map.55.extended_ref.previous_ref, bf16[2560,512]{1,0:T(8,128)(2,1)} %get-tuple-element.10), kind=kOutput, calls=%fused_computation.93 | convolution fusion | flops 671219712 | bytes 4718592 | tf_op jit(solution)/shard_map/dot_general | solution.py:456
  72.2 4.1 %shard_map.57 = f32[256,2048]{1,0:T(8,128)S(1)} custom-call(bf16[256,2560]{1,0:T(8,128)(2,1)S(1)} %shard_map.55.extended_ref.previous_ref, bf16[8,2560,256]{2,1,0:T(8,128)(2,1)S(1)} %copy-done.1, bf16[256,2560]{1,0:T(8,128)(2,1)S(1)} %shard_map.55.extended_ref.previous_ref, bf16[256,512]{1,0:T(8,128)(2,1)S(1)} %get-tuple-element.25.refs_0_, ...), custom_call_target="tpu_custom_call" | custom-call | flops 10737418240 | bytes 12582912 | tf_op jit(solution)/shard_map/pallas_call | solution.py:275
  76.3 1.0 fusion.3
  77.9 1.2 copy-done.3
  79.9 0.9 copy-done.2
  80.8 0.8 fusion.71
  81.8 6.3 %collective-permute-start.4 = (bf16[256,512]{1,0:T(8,128)(2,1)S(1)}, bf16[256,512]{1,0:T(8,128)(2,1)S(1)}, u32[]{:S(2)}, u32[]{:S(2)}) collective-permute-start(bf16[256,512]{1,0:T(8,128)(2,1)S(1)} %get-tuple-element.27.refs_0_), channel_id=1, source_target_pairs={{0,4},{4,0},{8,12},{12,8},{16,20},{20,16},{24,28},{28,24},{1,5},{5... | collective-permute-start | bytes 786440 | tf_op jit(solution)/shard_map/ppermute | solution.py:483
  88.1 0.8 collective-permute-start.5
  88.9 4.1 %shard_map.58 = f32[256,2048]{1,0:T(8,128)S(1)} custom-call(bf16[256,2560]{1,0:T(8,128)(2,1)S(1)} %pad_maximum_fusion.extended_ref, bf16[8,2560,256]{2,1,0:T(8,128)(2,1)S(1)} %copy-done.1, bf16[256,2560]{1,0:T(8,128)(2,1)S(1)} %shard_map.55.extended_ref.previous_ref, bf16[256,512]{1,0:T(8,128)(2,1)S(1)} %get-tuple-element.27.refs_0_, ...), custom_call_target="tpu_custom_call" | custom-call | flops 10737418240 | bytes 12582912 | tf_op jit(solution)/shard_map/pallas_call | solution.py:275
  93.0 1.1 fusion.5
  94.7 0.8 fusion.73
  95.6 0.8 fusion.72
  96.5 5.6 %collective-permute-start.6 = (bf16[256,512]{1,0:T(8,128)(2,1)S(1)}, bf16[256,512]{1,0:T(8,128)(2,1)S(1)}, u32[]{:S(2)}, u32[]{:S(2)}) collective-permute-start(bf16[256,512]{1,0:T(8,128)(2,1)S(1)} %get-tuple-element.33.refs_0_), channel_id=1, source_target_pairs={{0,4},{4,0},{8,12},{12,8},{16,20},{20,16},{24,28},{28,24},{1,5},{5... | collective-permute-start | bytes 786440 | tf_op jit(solution)/shard_map/ppermute | solution.py:483
  102.8 4.1 %shard_map.59 = f32[256,2048]{1,0:T(8,128)S(1)} custom-call(bf16[256,2560]{1,0:T(8,128)(2,1)S(1)} %pad_maximum_fusion.1.extended_ref, bf16[8,2560,256]{2,1,0:T(8,128)(2,1)S(1)} %copy-done.1, f32[256,2048]{1,0:T(8,128)S(1)} %get-tuple-element.14.previous_ref, bf16[256,512]{1,0:T(8,128)(2,1)S(1)} %get-tuple-element.33.refs_0_, ...), custom_call_target="tpu_custom_call" | custom-call | flops 10737418240 | bytes 12582912 | tf_op jit(solution)/shard_map/pallas_call | solution.py:275
  106.9 1.1 fusion.6
  109.7 0.9 collective-permute-start.9
  110.6 6.5 %collective-permute-start.8 = (bf16[256,256]{1,0:T(8,128)(2,1)S(1)}, bf16[256,256]{1,0:T(8,128)(2,1)S(1)}, u32[]{:S(2)}, u32[]{:S(2)}) collective-permute-start(bf16[256,256]{1,0:T(8,128)(2,1)S(1)} %fusion.17.refs_0_), channel_id=1, source_target_pairs={{0,4},{4,0},{8,12},{12,8},{16,20},{20,16},{24,28},{28,24},{1,5},{5... | collective-permute-start | bytes 393224 | tf_op jit(solution)/shard_map/ppermute | solution.py:483
  117.1 4.1 %shard_map.60 = f32[256,2048]{1,0:T(8,128)S(1)} custom-call(bf16[256,2560]{1,0:T(8,128)(2,1)S(1)} %pad_maximum_fusion.2.extended_ref, bf16[8,2560,256]{2,1,0:T(8,128)(2,1)S(1)} %copy-done.1, f32[256,2048]{1,0:T(8,128)S(1)} %get-tuple-element.12.previous_ref, bf16[256,256]{1,0:T(8,128)(2,1)S(1)} %fusion.17.refs_0_, bf16[256,256]{1,0:T(8,128)(2,1)S(1)} %fusion.20.refs_1_), custom_call_target="tpu_custom_call" | custom-call | flops 10737418240 | bytes 12582912 | tf_op jit(solution)/shard_map/pallas_call | solution.py:275
  121.2 1.1 fusion.7
  123.2 1.3 collective-permute-done.10
  124.6 4.4 %collective-permute-start.11 = (bf16[256,256]{1,0:T(8,128)(2,1)S(1)}, bf16[256,256]{1,0:T(8,128)(2,1)S(1)}, u32[]{:S(2)}, u32[]{:S(2)}) collective-permute-start(bf16[256,256]{1,0:T(8,128)(2,1)S(1)} %add_convert_fusion.3), channel_id=1, source_target_pairs={{0,8},{4,12},{8,0},{12,4},{16,24},{20,28},{24,16},{28,20},{1,9},{5... | collective-permute-start | bytes 393224 | tf_op jit(solution)/shard_map/ppermute | solution.py:406
  129.0 3.8 %collective-permute-done.11 = bf16[256,256]{1,0:T(8,128)(2,1)S(1)} collective-permute-done((bf16[256,256]{1,0:T(8,128)(2,1)S(1)}, bf16[256,256]{1,0:T(8,128)(2,1)S(1)}, u32[]{:S(2)}, u32[]{:S(2)}) %collective-permute-start.11) | collective-permute-done | bytes 131104 | tf_op jit(solution)/shard_map/ppermute | solution.py:406
  132.8 1.6 %collective-permute-start.12 = (bf16[256,256]{1,0:T(8,128)(2,1)S(1)}, bf16[256,256]{1,0:T(8,128)(2,1)S(1)}, u32[]{:S(2)}, u32[]{:S(2)}) collective-permute-start(bf16[256,256]{1,0:T(8,128)(2,1)S(1)} %add_convert_fusion.2), channel_id=1, source_target_pairs={{0,16},{4,20},{8,24},{12,28},{16,0},{20,4},{24,8},{28,12},{1,17},{... | collective-permute-start | bytes 393224 | tf_op jit(solution)/shard_map/ppermute | solution.py:406
  134.4 3.5 %collective-permute-done.12 = bf16[256,256]{1,0:T(8,128)(2,1)S(1)} collective-permute-done((bf16[256,256]{1,0:T(8,128)(2,1)S(1)}, bf16[256,256]{1,0:T(8,128)(2,1)S(1)}, u32[]{:S(2)}, u32[]{:S(2)}) %collective-permute-start.12) | collective-permute-done | bytes 131104 | tf_op jit(solution)/shard_map/ppermute | solution.py:406
  138.0 10.1 %shard_map.61 = f32[64,2048]{1,0:T(8,128)} custom-call(s32[1]{0:T(128)} %bitcast.block_ref, f32[256,256]{1,0:T(8,128)S(1)} %convert_add_fusion.gram_ref, bf16[256,2048]{1,0:T(8,128)(2,1)S(1)} %add_convert_fusion.filtered_ref), custom_call_target="tpu_custom_call" | custom-call | tf_op jit(solution)/shard_map/pallas_call | solution.py:378
  (66 shorter events, 10.2 us)
Async XLA Ops:
  6.5 4.7 %copy-start.4 = (s32[8,512]{1,0:T(8,128)S(1)}, s32[8,512]{1,0:T(8,128)}, u32[]{:S(2)}) copy-start(s32[8,512]{1,0:T(8,128)} %param.7) | copy-start | bytes 49156
  6.5 53.4 %all-gather.2.cloned.1.call-start = ((), (), s32[]{:S(2)}) async-start(), calls=%async_computation | async-start | bytes 1638400 | tf_op jit(solution)/shard_map/all_gather | solution.py:465
  10.0 1.9 %collective-permute-start = (bf16[64,256]{1,0:T(8,128)(2,1)S(1)}, bf16[64,256]{1,0:T(8,128)(2,1)S(1)}, u32[]{:S(2)}, u32[]{:S(2)}) collective-permute-start(bf16[64,256]{1,0:T(8,128)(2,1)S(1)} %get-tuple-element.21), channel_id=1, source_target_pairs={{0,4},{4,0},{8,12},{12,8},{16,20},{20,16},{24,28},{28,24},{1,5},{5... | collective-permute-start | bytes 98312 | tf_op jit(solution)/shard_map/ppermute | solution.py:463
  10.5 1.3 collective-permute-start.1
  11.9 2.5 %copy-start.5 = (s32[3072]{0:T(1024)}, s32[3072]{0:T(1024)S(1)}, u32[]{:S(2)}) copy-start(s32[3072]{0:T(1024)S(1)} %add_dynamic-update-slice_fusion) | copy-start | bytes 36868
  59.9 1.3 copy-start
  61.3 10.9 %copy-start.1 = (bf16[8,2560,256]{2,1,0:T(8,128)(2,1)S(1)}, bf16[8,2560,256]{2,1,0:T(8,128)(2,1)}, u32[]{:S(2)}) copy-start(bf16[8,2560,256]{2,1,0:T(8,128)(2,1)} %get-tuple-element.8.matrix_ref) | copy-start | bytes 31457284
  64.1 12.2 %collective-permute-start.2 = (bf16[256,512]{1,0:T(8,128)(2,1)S(1)}, bf16[256,512]{1,0:T(8,128)(2,1)S(1)}, u32[]{:S(2)}, u32[]{:S(2)}) collective-permute-start(bf16[256,512]{1,0:T(8,128)(2,1)S(1)} %get-tuple-element.25.refs_0_), channel_id=1, source_target_pairs={{0,4},{4,0},{8,12},{12,8},{16,20},{20,16},{24,28},{28,24},{1,5},{5... | collective-permute-start | bytes 786440 | tf_op jit(solution)/shard_map/ppermute | solution.py:483
  71.5 4.8 %collective-permute-start.3 = (bf16[256,512]{1,0:T(8,128)(2,1)S(1)}, bf16[256,512]{1,0:T(8,128)(2,1)S(1)}, u32[]{:S(2)}, u32[]{:S(2)}) collective-permute-start(bf16[256,512]{1,0:T(8,128)(2,1)S(1)} %get-tuple-element.23.refs_1_), channel_id=1, source_target_pairs={{4,8},{8,4},{12,16},{16,12},{20,24},{24,20},{5,9},{9,5},{13,17},{1... | collective-permute-start | bytes 786440 | tf_op jit(solution)/shard_map/ppermute | solution.py:480
  77.3 1.7 %copy-start.3 = (bf16[2560,512]{1,0:T(8,128)(2,1)S(1)}, bf16[2560,512]{1,0:T(8,128)(2,1)}, u32[]{:S(2)}) copy-start(bf16[2560,512]{1,0:T(8,128)(2,1)} %get-tuple-element.9) | copy-start | bytes 7864324
  79.1 1.7 %copy-start.2 = (bf16[2560,512]{1,0:T(8,128)(2,1)S(1)}, bf16[2560,512]{1,0:T(8,128)(2,1)}, u32[]{:S(2)}) copy-start(bf16[2560,512]{1,0:T(8,128)(2,1)} %get-tuple-element.10) | copy-start | bytes 7864324
  81.8 11.2 %collective-permute-start.4 = (bf16[256,512]{1,0:T(8,128)(2,1)S(1)}, bf16[256,512]{1,0:T(8,128)(2,1)S(1)}, u32[]{:S(2)}, u32[]{:S(2)}) collective-permute-start(bf16[256,512]{1,0:T(8,128)(2,1)S(1)} %get-tuple-element.27.refs_0_), channel_id=1, source_target_pairs={{0,4},{4,0},{8,12},{12,8},{16,20},{20,16},{24,28},{28,24},{1,5},{5... | collective-permute-start | bytes 786440 | tf_op jit(solution)/shard_map/ppermute | solution.py:483
  88.1 5.0 %collective-permute-start.5 = (bf16[256,512]{1,0:T(8,128)(2,1)S(1)}, bf16[256,512]{1,0:T(8,128)(2,1)S(1)}, u32[]{:S(2)}, u32[]{:S(2)}) collective-permute-start(bf16[256,512]{1,0:T(8,128)(2,1)S(1)} %get-tuple-element.29.refs_1_), channel_id=1, source_target_pairs={{4,8},{8,4},{12,16},{16,12},{20,24},{24,20},{5,9},{9,5},{13,17},{1... | collective-permute-start | bytes 786440 | tf_op jit(solution)/shard_map/ppermute | solution.py:480
  96.5 10.3 %collective-permute-start.6 = (bf16[256,512]{1,0:T(8,128)(2,1)S(1)}, bf16[256,512]{1,0:T(8,128)(2,1)S(1)}, u32[]{:S(2)}, u32[]{:S(2)}) collective-permute-start(bf16[256,512]{1,0:T(8,128)(2,1)S(1)} %get-tuple-element.33.refs_0_), channel_id=1, source_target_pairs={{0,4},{4,0},{8,12},{12,8},{16,20},{20,16},{24,28},{28,24},{1,5},{5... | collective-permute-start | bytes 786440 | tf_op jit(solution)/shard_map/ppermute | solution.py:483
  102.1 4.8 %collective-permute-start.7 = (bf16[256,512]{1,0:T(8,128)(2,1)S(1)}, bf16[256,512]{1,0:T(8,128)(2,1)S(1)}, u32[]{:S(2)}, u32[]{:S(2)}) collective-permute-start(bf16[256,512]{1,0:T(8,128)(2,1)S(1)} %get-tuple-element.31.refs_1_), channel_id=1, source_target_pairs={{4,8},{8,4},{12,16},{16,12},{20,24},{24,20},{5,9},{9,5},{13,17},{1... | collective-permute-start | bytes 786440 | tf_op jit(solution)/shard_map/ppermute | solution.py:480
  109.7 11.5 %collective-permute-start.9 = (bf16[256,256]{1,0:T(8,128)(2,1)S(1)}, bf16[256,256]{1,0:T(8,128)(2,1)S(1)}, u32[]{:S(2)}, u32[]{:S(2)}) collective-permute-start(bf16[256,256]{1,0:T(8,128)(2,1)S(1)} %fusion.20.refs_1_), channel_id=1, source_target_pairs={{4,8},{8,4},{12,16},{16,12},{20,24},{24,20},{5,9},{9,5},{13,17},{1... | collective-permute-start | bytes 393224 | tf_op jit(solution)/shard_map/ppermute | solution.py:480
  110.6 10.6 %collective-permute-start.8 = (bf16[256,256]{1,0:T(8,128)(2,1)S(1)}, bf16[256,256]{1,0:T(8,128)(2,1)S(1)}, u32[]{:S(2)}, u32[]{:S(2)}) collective-permute-start(bf16[256,256]{1,0:T(8,128)(2,1)S(1)} %fusion.17.refs_0_), channel_id=1, source_target_pairs={{0,4},{4,0},{8,12},{12,8},{16,20},{20,16},{24,28},{28,24},{1,5},{5... | collective-permute-start | bytes 393224 | tf_op jit(solution)/shard_map/ppermute | solution.py:483
  123.2 1.4 collective-permute-start.10
  124.6 8.2 %collective-permute-start.11 = (bf16[256,256]{1,0:T(8,128)(2,1)S(1)}, bf16[256,256]{1,0:T(8,128)(2,1)S(1)}, u32[]{:S(2)}, u32[]{:S(2)}) collective-permute-start(bf16[256,256]{1,0:T(8,128)(2,1)S(1)} %add_convert_fusion.3), channel_id=1, source_target_pairs={{0,8},{4,12},{8,0},{12,4},{16,24},{20,28},{24,16},{28,20},{1,9},{5... | collective-permute-start | bytes 393224 | tf_op jit(solution)/shard_map/ppermute | solution.py:406
  132.8 5.1 %collective-permute-start.12 = (bf16[256,256]{1,0:T(8,128)(2,1)S(1)}, bf16[256,256]{1,0:T(8,128)(2,1)S(1)}, u32[]{:S(2)}, u32[]{:S(2)}) collective-permute-start(bf16[256,256]{1,0:T(8,128)(2,1)S(1)} %add_convert_fusion.2), channel_id=1, source_target_pairs={{0,16},{4,20},{8,24},{12,28},{16,0},{20,4},{24,8},{28,12},{1,17},{... | collective-permute-start | bytes 393224 | tf_op jit(solution)/shard_map/ppermute | solution.py:406
Sparse Core Ops, SparseCore 0:
  12.8 38.9 all-gather.1

commit v5 on v3

--- a/solution.py
+++ b/solution.py
@@ -117,21 +117,17 @@
     @pl.when(cell == 0)
     def _():
         for part in range(parts):
-            spread = spread_part(part)
+            keep_part(part, spread_part(part), even_terms)
             round_part(part)
-            keep_part(part, spread, even_terms)
 
     for parity, (before, now) in enumerate(((odd_terms, even_terms), (even_terms, odd_terms))):
 
         @pl.when((cell > 0) & (cell % 2 == parity))
         def _():
-            spread = spread_part(0)
             for part in range(parts):
-                following = spread_part(part + 1) if part + 1 < parts else None
+                keep_part(part, spread_part(part), now)
                 add_part(part, cell - 1, before)
                 round_part(part)
-                keep_part(part, spread, now)
-                spread = following
 
         @pl.when((cell == cells - 1) & (cell % 2 == parity))
         def _():
@@ -232,35 +228,90 @@
     )(values)
 
 
-def own_kernel(first_step, extended_ref, matrix_ref, previous_ref, *refs):
-    product = jnp.dot(extended_ref[...], matrix_ref[0], preferred_element_type=jnp.float32)
-    if not first_step:
-        product = 2.0 * product - previous_ref[...].astype(jnp.float32)
-    refs[-1][...] = product
-
-
-def own_part(first_step, extended, matrix, previous, after):
+def arrived(got_a_ref, got_b_ref, table_ref, at):
+    incoming = jnp.concatenate(
+        [ref[:, : table_ref.shape[0] // 2] for ref in (got_a_ref, got_b_ref)], axis=1
+    )
+    return jnp.dot(incoming, table_ref[:, at], preferred_element_type=jnp.float32)
+
+
+def own_kernel(step, extended_ref, matrix_ref, *refs):
+    out_ref = refs[-1]
+
+    def body(tile, carry):
+        at = pl.ds(pl.multiple_of(tile * TILE, TILE), TILE)
+        product = jnp.dot(extended_ref[...], matrix_ref[tile], preferred_element_type=jnp.float32)
+        if step == 1:
+            product = 2.0 * product - refs[0][:, at].astype(jnp.float32)
+        if step > 1:
+            factor = 1.0 if step == 2 else 2.0
+            product = 2.0 * product - (refs[0][:, at] + factor * arrived(*refs[1:4], at))
+        out_ref[:, at] = product
+        return carry
+
+    lax.fori_loop(0, matrix_ref.shape[0], body, 0)
+
+
+def own_part(step, extended, matrix, before, after):
     rows, depth = extended.shape
     tiles, _, width = matrix.shape
     columns = tiles * width
+    whole = pl.BlockSpec(memory_space=pltpu.VMEM)
+    operands = (extended, matrix) + before
     return pl.pallas_call(
-        functools.partial(own_kernel, first_step),
+        functools.partial(own_kernel, step),
         out_shape=jax.ShapeDtypeStruct((rows, columns), jnp.float32),
-        grid=(tiles,),
-        in_specs=[
-            pl.BlockSpec((rows, depth), lambda t: (0, 0)),
-            pl.BlockSpec((1, depth, width), lambda t: (t, 0, 0)),
-            pl.BlockSpec((rows, width), lambda t: (0, t)),
-        ]
-        + [pl.BlockSpec(memory_space=pl.ANY)] * len(after),
-        out_specs=pl.BlockSpec((rows, width), lambda t: (0, t)),
-        compiler_params=pltpu.CompilerParams(vmem_limit_bytes=44 * 1024 * 1024),
+        in_specs=[whole] * len(operands) + [pl.BlockSpec(memory_space=pl.ANY)] * len(after),
+        out_specs=whole,
+        compiler_params=pltpu.CompilerParams(vmem_limit_bytes=16 * 1024 * 1024),
         cost_estimate=pl.CostEstimate(
             flops=8 * rows * depth * columns,
             bytes_accessed=2 * depth * columns + 4 * rows * columns,
             transcendentals=0,
         ),
-    )(extended, matrix, previous, *after)
+    )(*operands, *after)
+
+
+def combine_kernel(step, there_ref, own_ref, got_a_ref, got_b_ref, table_ref, *refs):
+    factor = 1.0 if step == 0 else 2.0
+    columns, face = own_ref.shape[1], table_ref.shape[0] // 2
+    ghosts_ref = refs[-1]
+    field_ref = refs[-2] if len(refs) > 1 else refs[-1]
+    for first in range(0, columns, TILE):
+        at = slice(first, first + TILE)
+        field_ref[:, at] = (
+            own_ref[:, at] + factor * arrived(got_a_ref, got_b_ref, table_ref, at)
+        ).astype(jnp.bfloat16)
+    if len(refs) == 1:
+        return
+    for side, got_ref in enumerate((got_a_ref, got_b_ref)):
+        at = slice(side * face, (side + 1) * face)
+        value = factor * (refs[side][:, :face] + got_ref[:, face:].astype(jnp.float32))
+        if step > 0:
+            value = value - refs[2][:, at].astype(jnp.float32)
+        value = jnp.where(there_ref[side] != 0, value, 0.0)
+        ghosts_ref[:, at] = value
+        field_ref[:, columns + side * face : columns + (side + 1) * face] = value.astype(jnp.bfloat16)
+
+
+def combine(step, there, own, got_a, got_b, table, ghost_operands):
+    rows, columns = own.shape
+    whole = pl.BlockSpec(memory_space=pltpu.VMEM)
+    face = table.shape[0] // 2
+    if ghost_operands:
+        out_shape = (
+            jax.ShapeDtypeStruct((rows, columns + 2 * face), jnp.bfloat16),
+            jax.ShapeDtypeStruct((rows, 2 * face), jnp.float32),
+        )
+    else:
+        out_shape = (jax.ShapeDtypeStruct((rows, columns), jnp.bfloat16),)
+    return pl.pallas_call(
+        functools.partial(combine_kernel, step),
+        out_shape=out_shape,
+        in_specs=[pl.BlockSpec(memory_space=pltpu.SMEM)] + [whole] * (4 + len(ghost_operands)),
+        out_specs=(whole,) * len(out_shape),
+        compiler_params=pltpu.CompilerParams(vmem_limit_bytes=16 * 1024 * 1024),
+    )(there, own, got_a, got_b, table, *ghost_operands)
 
 
 def exact(left, right, contract):
@@ -449,41 +500,31 @@
         mine,
     )
 
-    def following(step, extended, previous):
-        factor = 1.0 if step == 0 else 2.0
+    there = jnp.stack([has_a, has_b]).astype(jnp.int32)
+    field = hold(gathered)
+    ghosts = [field[:, own_count:]]
+    before = ()
+    for step in range(DEGREE):
         last = step == DEGREE - 1
-        part_b = times(extended, matrix_b[:, :face] if last else matrix_b)
+        part_b = times(field, matrix_b[:, :face] if last else matrix_b)
         sent_b = part_b.astype(jnp.bfloat16)
         got_b = lax.ppermute(sent_b, "slab", pairs_b)
-        part_a = times(extended, matrix_a[:, :face] if last else matrix_a)
+        part_a = times(field, matrix_a[:, :face] if last else matrix_a)
         sent_a = part_a.astype(jnp.bfloat16)
         got_a = lax.ppermute(sent_a, "slab", pairs_a)
-        own = own_part(step == 0, extended, own_matrix, previous[0], (sent_a, sent_b))
-        incoming = jnp.concatenate([got_a[:, :face], got_b[:, :face]], axis=1)
-        own = own + factor * times(incoming, face_table)
+        own = own_part(step, field, own_matrix, before, (sent_a, sent_b))
+        if step == 0:
+            before = (field,)
+        else:
+            before = arrivals
+        arrivals = (own, got_a, got_b, face_table)
         if last:
-            return (own,)
-
-        def ghosts_of(there, part, got, before):
-            value = factor * (part[:, :face] + got[:, face:].astype(jnp.float32))
-            if step > 0:
-                value = value - before.astype(jnp.float32)
-            return jnp.where(there, value, 0.0)
-
-        at_a = ghosts_of(has_a, part_a, got_a, previous[1])
-        at_b = ghosts_of(has_b, part_b, got_b, previous[2])
-        return own, at_a, at_b
-
-    def extend(own, at_a, at_b):
-        return jnp.concatenate([own, at_a, at_b], axis=1).astype(jnp.bfloat16)
-
-    start = hold(gathered)
-    previous = (start, start[:, own_count : own_count + face], start[:, own_count + face :])
-    current = following(0, start, previous)
-    for degree_step in range(1, DEGREE):
-        previous, current = current, following(degree_step, extend(*current), previous)
-
-    filtered = current[0].astype(jnp.bfloat16)
+            (filtered,) = combine(step, there, own, got_a, got_b, face_table, ())
+        else:
+            operands = (part_a, part_b) + ((ghosts[-2],) if step else ())
+            field, new_ghosts = combine(step, there, own, got_a, got_b, face_table, operands)
+            ghosts.append(new_ghosts)
+
     gram = lax.dot_general(
         filtered, filtered, (((1,), (1,)), ((), ())), preferred_element_type=jnp.float32
     )

time: 156 us -> 148 us (0.949)
  Pallas kernels: 84.2 us -> 76.4 us
  starting transfers between devices: 25.3 us -> 28.1 us
  other arithmetic: 6.04 us -> 4.43 us
    pallas_call x4 -> x8, Pallas kernels: 32.8 us -> 24.4 us  [the longest x4 17.5 us: own_part(): pl.pallas_call(functools.partial(own_kernel, step), out_shape=jax.ShapeDt...]
    ppermute x8, starting transfers between devices: 19.9 us -> 22.7 us  [the longest x4 19.8 us: per_device(): got_a = lax.ppermute(sent_a, 'slab', pairs_a)]
    dot_general x12 -> x8, matrix products: 10.4 us -> 10.3 us  [times(): return jnp.dot(left, right, preferred_element_type=jnp.float32)]
  transfers between devices with their start and end apart: 14 -> 14, of which waited for: 3 -> 3; matrix products, arithmetic and copies ran while one was open for 2% -> 2% of each run, Pallas kernels for 48% -> 40%
where the time goes in v5:
time: 148 us
  Pallas kernels  76.4 us (52%)
  starting transfers between devices  28.1 us (19%)
  between operations  13.8 us (9%)
  matrix products  11.7 us (8%)
  waiting for transfers between devices  8.69 us (6%)
  other arithmetic  4.43 us (3%)
  local copies, waits for them, and re-layouts  4.38 us (3%)
    pallas_call x1, Pallas kernels, assemble(): pl.pallas_call(assemble_kernel, out_shape=(half, half, jax.ShapeDtypeStru...  41.8 us
    ppermute x4, starting transfers between devices, per_device(): got_a = lax.ppermute(sent_a, 'slab', pairs_a)  19.8 us
    pallas_call x4, Pallas kernels, own_part(): pl.pallas_call(functools.partial(own_kernel, step), out_shape=jax.ShapeDt...  17.5 us
    dot_general x8, matrix products, times(): return jnp.dot(left, right, preferred_element_type=jnp.float32)  10.3 us
    pallas_call x1, Pallas kernels, orthonormal(): pl.pallas_call(functools.partial(orthonormal_kernel, scale), out_shape=ja...  10.1 us
    ppermute x3, waiting for transfers between devices, sum_over(): got = lax.ppermute(sent, axis, [(i, i ^ step) for i in range(count)])  8.62 us
    pallas_call x4, Pallas kernels, combine(): pl.pallas_call(functools.partial(combine_kernel, step), out_shape=out_sha...  6.94 us
    ppermute x3, starting transfers between devices, sum_over(): got = lax.ppermute(sent, axis, [(i, i ^ step) for i in range(count)])  4.29 us
  transfers between devices with their start and end apart: 14, of which 3 were waited for; matrix products, arithmetic and copies ran while one was open for 2% of the time, Pallas kernels for 40%

profile of v5, /device:TPU:0, one launch (start us, length us, event | category | flops | bytes accessed | tf_op | source)
XLA Modules:
  0.0 147.5 jit_solution(6050968878906863745)
XLA Ops:
  7.9 1.1 convert_element_type.67
  9.0 0.9 fusion.14
  12.4 0.7 pad_maximum_fusion.after_ref
  13.1 1.7 %broadcast_in_dim.5.nodes_ref = s32[8,512,128]{2,1,0:T(8,128)} broadcast(s32[8,512]{1,0:T(8,128)S(1)} %copy-done.4), dimensions={0,1} | broadcast | bytes 2113536 | tf_op jit(solution)/shard_map/broadcast_in_dim | solution.py:473
  14.9 41.8 %shard_map.56 = (bf16[2560,512]{1,0:T(8,128)(2,1)}, bf16[2560,512]{1,0:T(8,128)(2,1)}, bf16[8,2560,256]{2,1,0:T(8,128)(2,1)}) custom-call(s32[8192]{0:T(1024)} %pad_add_fusion.places_ref, s32[1,3072]{1,0:T(1,128)} %bitcast.28, s32[8,512,128]{2,1,0:T(8,128)} %broadcast_in_dim.5.nodes_ref, bf16[8,512,512]{2,1,0:T(8,128)(2,1)} %cell_ref.1, ...), custom_call_target="tpu_custom_call" | custom-call | flops 103079215104 | bytes 28311552 | tf_op jit(solution)/shard_map/pallas_call | solution.py:179
  56.8 1.3 copy-done
  58.2 2.7 %fusion.17 = (bf16[256,512]{1,0:T(8,128)(2,1)S(1)}, f32[256,512]{1,0:T(8,128)S(1)}) fusion(bf16[256,2560]{1,0:T(8,128)(2,1)S(1)} %shard_map.55.extended_ref.refs_0_, bf16[2560,512]{1,0:T(8,128)(2,1)} %get-tuple-element.14), kind=kOutput, calls=%fused_computation.32 | convolution fusion | flops 671219712 | bytes 4718592 | tf_op jit(solution)/shard_map/dot_general | solution.py:484
  60.9 3.2 %fusion.16 = (bf16[256,512]{1,0:T(8,128)(2,1)S(1)}, f32[256,512]{1,0:T(8,128)S(1)}) fusion(bf16[256,2560]{1,0:T(8,128)(2,1)S(1)} %shard_map.55.extended_ref.refs_0_, bf16[2560,512]{1,0:T(8,128)(2,1)} %get-tuple-element.13), kind=kOutput, calls=%fused_computation.31 | convolution fusion | flops 671219712 | bytes 4718592 | tf_op jit(solution)/shard_map/dot_general | solution.py:484
  64.8 7.3 %collective-permute-start.2 = (bf16[256,512]{1,0:T(8,128)(2,1)S(1)}, bf16[256,512]{1,0:T(8,128)(2,1)S(1)}, u32[]{:S(2)}, u32[]{:S(2)}) collective-permute-start(bf16[256,512]{1,0:T(8,128)(2,1)S(1)} %get-tuple-element.25.refs_0_), channel_id=1, source_target_pairs={{0,4},{4,0},{8,12},{12,8},{16,20},{20,16},{24,28},{28,24},{1,5},{5... | collective-permute-start | bytes 786440 | tf_op jit(solution)/shard_map/ppermute | solution.py:514
  72.1 4.1 %shard_map.57.own_ref.refs_0_ = f32[256,2048]{1,0:T(8,128)S(1)} custom-call(bf16[256,2560]{1,0:T(8,128)(2,1)S(1)} %shard_map.55.extended_ref.refs_0_, bf16[8,2560,256]{2,1,0:T(8,128)(2,1)S(1)} %copy-done.1, bf16[256,512]{1,0:T(8,128)(2,1)S(1)} %get-tuple-element.25.refs_0_, bf16[256,512]{1,0:T(8,128)(2,1)S(1)} %get-tuple-element.27.refs_1_), custom_call_target="tpu_custom_call" | custom-call | flops 10737418240 | bytes 12582912 | tf_op jit(solution)/shard_map/pallas_call | solution.py:261
  76.2 1.3 shard_map.58
  77.9 0.8 fusion.19
  78.7 0.9 copy-done.2
  79.6 0.8 fusion.18
  81.2 3.8 %collective-permute-start.4 = (bf16[256,512]{1,0:T(8,128)(2,1)S(1)}, bf16[256,512]{1,0:T(8,128)(2,1)S(1)}, u32[]{:S(2)}, u32[]{:S(2)}) collective-permute-start(bf16[256,512]{1,0:T(8,128)(2,1)S(1)} %get-tuple-element.29.refs_1_), channel_id=1, source_target_pairs={{0,4},{4,0},{8,12},{12,8},{16,20},{20,16},{24,28},{28,24},{1,5},{5... | collective-permute-start | bytes 786440 | tf_op jit(solution)/shard_map/ppermute | solution.py:514
  85.0 4.1 %shard_map.59.own_ref.refs_0_ = f32[256,2048]{1,0:T(8,128)S(1)} custom-call(bf16[256,2560]{1,0:T(8,128)(2,1)S(1)} %get-tuple-element.15.extended_ref, bf16[8,2560,256]{2,1,0:T(8,128)(2,1)S(1)} %copy-done.1, bf16[256,2560]{1,0:T(8,128)(2,1)S(1)} %shard_map.55.extended_ref.refs_0_, bf16[256,512]{1,0:T(8,128)(2,1)S(1)} %get-tuple-element.29.refs_1_, ...), custom_call_target="tpu_custom_call" | custom-call | flops 10737418240 | bytes 12582912 | tf_op jit(solution)/shard_map/pallas_call | solution.py:261
  89.1 2.2 %shard_map.60 = (bf16[256,2560]{1,0:T(8,128)(2,1)S(1)}, f32[256,512]{1,0:T(8,128)}) custom-call(s32[2]{0:T(128)S(1)} %add_convert_fusion.2.there_ref, f32[256,2048]{1,0:T(8,128)S(1)} %shard_map.59.own_ref.refs_0_, bf16[256,512]{1,0:T(8,128)(2,1)S(1)} %collective-permute-done.4.got_a_ref.refs_1_, ...), custom_call_target="tpu_custom_call" | custom-call | tf_op jit(solution)/shard_map/pallas_call | solution.py:308
  91.3 0.8 fusion.21
  92.1 0.8 fusion.20
  93.0 0.9 collective-permute-start.7
  93.8 4.8 %collective-permute-start.6 = (bf16[256,512]{1,0:T(8,128)(2,1)S(1)}, bf16[256,512]{1,0:T(8,128)(2,1)S(1)}, u32[]{:S(2)}, u32[]{:S(2)}) collective-permute-start(bf16[256,512]{1,0:T(8,128)(2,1)S(1)} %get-tuple-element.33.refs_4_), channel_id=1, source_target_pairs={{0,4},{4,0},{8,12},{12,8},{16,20},{20,16},{24,28},{28,24},{1,5},{5... | collective-permute-start | bytes 786440 | tf_op jit(solution)/shard_map/ppermute | solution.py:514
  98.7 4.7 %shard_map.61.own_ref = f32[256,2048]{1,0:T(8,128)S(1)} custom-call(bf16[256,2560]{1,0:T(8,128)(2,1)S(1)} %get-tuple-element.16.extended_ref, bf16[8,2560,256]{2,1,0:T(8,128)(2,1)S(1)} %copy-done.1, f32[256,2048]{1,0:T(8,128)S(1)} %shard_map.57.own_ref.refs_0_, bf16[256,512]{1,0:T(8,128)(2,1)S(1)} %collective-permute-done.2.got_a_ref.refs_1_, ...), custom_call_target="tpu_custom_call" | custom-call | flops 10737418240 | bytes 12582912 | tf_op jit(solution)/shard_map/pallas_call | solution.py:261
  103.4 2.2 %shard_map.62 = (bf16[256,2560]{1,0:T(8,128)(2,1)S(1)}, f32[256,512]{1,0:T(8,128)}) custom-call(s32[2]{0:T(128)S(1)} %add_convert_fusion.2.there_ref, f32[256,2048]{1,0:T(8,128)S(1)} %shard_map.61.own_ref, bf16[256,512]{1,0:T(8,128)(2,1)S(1)} %collective-permute-done.6.got_a_ref, bf16[256,512]{1,0:T(8,128)(2,1)S(1)} %collective-permute-done.7.got_b_ref, ...), custom_call_target="tpu_custom_call" | custom-call | tf_op jit(solution)/shard_map/pallas_call | solution.py:308
  107.2 3.9 %collective-permute-start.8 = (bf16[256,256]{1,0:T(8,128)(2,1)S(1)}, bf16[256,256]{1,0:T(8,128)(2,1)S(1)}, u32[]{:S(2)}, u32[]{:S(2)}) collective-permute-start(bf16[256,256]{1,0:T(8,128)(2,1)S(1)} %fusion.7.refs_4_), channel_id=1, source_target_pairs={{0,4},{4,0},{8,12},{12,8},{16,20},{20,16},{24,28},{28,24},{1,5},{5... | collective-permute-start | bytes 393224 | tf_op jit(solution)/shard_map/ppermute | solution.py:514
  111.1 4.7 %shard_map.63.own_ref = f32[256,2048]{1,0:T(8,128)S(1)} custom-call(bf16[256,2560]{1,0:T(8,128)(2,1)S(1)} %get-tuple-element.18.extended_ref, bf16[8,2560,256]{2,1,0:T(8,128)(2,1)S(1)} %copy-done.1, f32[256,2048]{1,0:T(8,128)S(1)} %shard_map.59.own_ref.refs_0_, bf16[256,512]{1,0:T(8,128)(2,1)S(1)} %collective-permute-done.4.got_a_ref.refs_1_, ...), custom_call_target="tpu_custom_call" | custom-call | flops 10737418240 | bytes 12582912 | tf_op jit(solution)/shard_map/pallas_call | solution.py:261
  115.8 1.3 shard_map.64.filtered_ref
  117.6 1.3 collective-permute-done.10
  119.0 2.6 %collective-permute-start.11 = (bf16[256,256]{1,0:T(8,128)(2,1)S(1)}, bf16[256,256]{1,0:T(8,128)(2,1)S(1)}, u32[]{:S(2)}, u32[]{:S(2)}) collective-permute-start(bf16[256,256]{1,0:T(8,128)(2,1)S(1)} %add_convert_fusion.1), channel_id=1, source_target_pairs={{0,8},{4,12},{8,0},{12,4},{16,24},{20,28},{24,16},{28,20},{1,9},{5... | collective-permute-start | bytes 393224 | tf_op jit(solution)/shard_map/ppermute | solution.py:434
  121.6 3.8 %collective-permute-done.11 = bf16[256,256]{1,0:T(8,128)(2,1)S(1)} collective-permute-done((bf16[256,256]{1,0:T(8,128)(2,1)S(1)}, bf16[256,256]{1,0:T(8,128)(2,1)S(1)}, u32[]{:S(2)}, u32[]{:S(2)}) %collective-permute-start.11) | collective-permute-done | bytes 131104 | tf_op jit(solution)/shard_map/ppermute | solution.py:434
  125.4 1.6 %collective-permute-start.12 = (bf16[256,256]{1,0:T(8,128)(2,1)S(1)}, bf16[256,256]{1,0:T(8,128)(2,1)S(1)}, u32[]{:S(2)}, u32[]{:S(2)}) collective-permute-start(bf16[256,256]{1,0:T(8,128)(2,1)S(1)} %add_convert_fusion), channel_id=1, source_target_pairs={{0,16},{4,20},{8,24},{12,28},{16,0},{20,4},{24,8},{28,12},{1,17},{... | collective-permute-start | bytes 393224 | tf_op jit(solution)/shard_map/ppermute | solution.py:434
  127.1 3.5 %collective-permute-done.12 = bf16[256,256]{1,0:T(8,128)(2,1)S(1)} collective-permute-done((bf16[256,256]{1,0:T(8,128)(2,1)S(1)}, bf16[256,256]{1,0:T(8,128)(2,1)S(1)}, u32[]{:S(2)}, u32[]{:S(2)}) %collective-permute-start.12) | collective-permute-done | bytes 131104 | tf_op jit(solution)/shard_map/ppermute | solution.py:434
  130.6 10.1 %shard_map.65 = f32[64,2048]{1,0:T(8,128)} custom-call(s32[1]{0:T(128)} %bitcast.block_ref, f32[256,256]{1,0:T(8,128)S(1)} %convert_add_fusion.gram_ref, bf16[256,2048]{1,0:T(8,128)(2,1)S(1)} %shard_map.64.filtered_ref), custom_call_target="tpu_custom_call" | custom-call | tf_op jit(solution)/shard_map/pallas_call | solution.py:406
  (51 shorter events, 8.0 us)
Async XLA Ops:
  6.5 50.2 %all-gather.2.cloned.1.call-start = ((), (), s32[]{:S(2)}) async-start(), calls=%async_computation | async-start | bytes 1638400 | tf_op jit(solution)/shard_map/all_gather | solution.py:493
  9.0 2.6 %copy-start.4 = (s32[8,512]{1,0:T(8,128)S(1)}, s32[8,512]{1,0:T(8,128)}, u32[]{:S(2)}) copy-start(s32[8,512]{1,0:T(8,128)} %param.7) | copy-start | bytes 49156
  10.0 2.4 %collective-permute-start = (bf16[64,256]{1,0:T(8,128)(2,1)S(1)}, bf16[64,256]{1,0:T(8,128)(2,1)S(1)}, u32[]{:S(2)}, u32[]{:S(2)}) collective-permute-start(bf16[64,256]{1,0:T(8,128)(2,1)S(1)} %get-tuple-element.23), channel_id=1, source_target_pairs={{0,4},{4,0},{8,12},{12,8},{16,20},{20,16},{24,28},{28,24},{1,5},{5... | collective-permute-start | bytes 98312 | tf_op jit(solution)/shard_map/ppermute | solution.py:491
  10.5 1.8 %collective-permute-start.1 = (bf16[64,256]{1,0:T(8,128)(2,1)S(1)}, bf16[64,256]{1,0:T(8,128)(2,1)S(1)}, u32[]{:S(2)}, u32[]{:S(2)}) collective-permute-start(bf16[64,256]{1,0:T(8,128)(2,1)S(1)} %get-tuple-element.24), channel_id=1, source_target_pairs={{4,8},{8,4},{12,16},{16,12},{20,24},{24,20},{5,9},{9,5},{13,17},{1... | collective-permute-start | bytes 98312 | tf_op jit(solution)/shard_map/ppermute | solution.py:490
  12.3 2.6 %copy-start.5 = (s32[3072]{0:T(1024)}, s32[3072]{0:T(1024)S(1)}, u32[]{:S(2)}) copy-start(s32[3072]{0:T(1024)S(1)} %add_dynamic-update-slice_fusion) | copy-start | bytes 36868
  56.7 1.3 copy-start
  58.1 14.0 %copy-start.1 = (bf16[8,2560,256]{2,1,0:T(8,128)(2,1)S(1)}, bf16[8,2560,256]{2,1,0:T(8,128)(2,1)}, u32[]{:S(2)}) copy-start(bf16[8,2560,256]{2,1,0:T(8,128)(2,1)} %get-tuple-element.12.matrix_ref) | copy-start | bytes 31457284
  64.1 12.1 %collective-permute-start.3 = (bf16[256,512]{1,0:T(8,128)(2,1)S(1)}, bf16[256,512]{1,0:T(8,128)(2,1)S(1)}, u32[]{:S(2)}, u32[]{:S(2)}) collective-permute-start(bf16[256,512]{1,0:T(8,128)(2,1)S(1)} %get-tuple-element.27.refs_1_), channel_id=1, source_target_pairs={{4,8},{8,4},{12,16},{16,12},{20,24},{24,20},{5,9},{9,5},{13,17},{1... | collective-permute-start | bytes 786440 | tf_op jit(solution)/shard_map/ppermute | solution.py:511
  64.8 11.4 %collective-permute-start.2 = (bf16[256,512]{1,0:T(8,128)(2,1)S(1)}, bf16[256,512]{1,0:T(8,128)(2,1)S(1)}, u32[]{:S(2)}, u32[]{:S(2)}) collective-permute-start(bf16[256,512]{1,0:T(8,128)(2,1)S(1)} %get-tuple-element.25.refs_0_), channel_id=1, source_target_pairs={{0,4},{4,0},{8,12},{12,8},{16,20},{20,16},{24,28},{28,24},{1,5},{5... | collective-permute-start | bytes 786440 | tf_op jit(solution)/shard_map/ppermute | solution.py:514
  76.2 1.7 %copy-start.3 = (bf16[2560,512]{1,0:T(8,128)(2,1)S(1)}, bf16[2560,512]{1,0:T(8,128)(2,1)}, u32[]{:S(2)}) copy-start(bf16[2560,512]{1,0:T(8,128)(2,1)} %get-tuple-element.14) | copy-start | bytes 7864324
  77.9 1.7 %copy-start.2 = (bf16[2560,512]{1,0:T(8,128)(2,1)S(1)}, bf16[2560,512]{1,0:T(8,128)(2,1)}, u32[]{:S(2)}) copy-start(bf16[2560,512]{1,0:T(8,128)(2,1)} %get-tuple-element.13) | copy-start | bytes 7864324
  80.5 8.6 %collective-permute-start.5 = (bf16[256,512]{1,0:T(8,128)(2,1)S(1)}, bf16[256,512]{1,0:T(8,128)(2,1)S(1)}, u32[]{:S(2)}, u32[]{:S(2)}) collective-permute-start(bf16[256,512]{1,0:T(8,128)(2,1)S(1)} %get-tuple-element.31.refs_2_), channel_id=1, source_target_pairs={{4,8},{8,4},{12,16},{16,12},{20,24},{24,20},{5,9},{9,5},{13,17},{1... | collective-permute-start | bytes 786440 | tf_op jit(solution)/shard_map/ppermute | solution.py:511
  81.2 7.9 %collective-permute-start.4 = (bf16[256,512]{1,0:T(8,128)(2,1)S(1)}, bf16[256,512]{1,0:T(8,128)(2,1)S(1)}, u32[]{:S(2)}, u32[]{:S(2)}) collective-permute-start(bf16[256,512]{1,0:T(8,128)(2,1)S(1)} %get-tuple-element.29.refs_1_), channel_id=1, source_target_pairs={{0,4},{4,0},{8,12},{12,8},{16,20},{20,16},{24,28},{28,24},{1,5},{5... | collective-permute-start | bytes 786440 | tf_op jit(solution)/shard_map/ppermute | solution.py:514
  93.0 10.4 %collective-permute-start.7 = (bf16[256,512]{1,0:T(8,128)(2,1)S(1)}, bf16[256,512]{1,0:T(8,128)(2,1)S(1)}, u32[]{:S(2)}, u32[]{:S(2)}) collective-permute-start(bf16[256,512]{1,0:T(8,128)(2,1)S(1)} %get-tuple-element.35.refs_5_), channel_id=1, source_target_pairs={{4,8},{8,4},{12,16},{16,12},{20,24},{24,20},{5,9},{9,5},{13,17},{1... | collective-permute-start | bytes 786440 | tf_op jit(solution)/shard_map/ppermute | solution.py:511
  93.8 9.5 %collective-permute-start.6 = (bf16[256,512]{1,0:T(8,128)(2,1)S(1)}, bf16[256,512]{1,0:T(8,128)(2,1)S(1)}, u32[]{:S(2)}, u32[]{:S(2)}) collective-permute-start(bf16[256,512]{1,0:T(8,128)(2,1)S(1)} %get-tuple-element.33.refs_4_), channel_id=1, source_target_pairs={{0,4},{4,0},{8,12},{12,8},{16,20},{20,16},{24,28},{28,24},{1,5},{5... | collective-permute-start | bytes 786440 | tf_op jit(solution)/shard_map/ppermute | solution.py:514
  106.6 9.2 %collective-permute-start.9 = (bf16[256,256]{1,0:T(8,128)(2,1)S(1)}, bf16[256,256]{1,0:T(8,128)(2,1)S(1)}, u32[]{:S(2)}, u32[]{:S(2)}) collective-permute-start(bf16[256,256]{1,0:T(8,128)(2,1)S(1)} %fusion.10.refs_5_), channel_id=1, source_target_pairs={{4,8},{8,4},{12,16},{16,12},{20,24},{24,20},{5,9},{9,5},{13,17},{1... | collective-permute-start | bytes 393224 | tf_op jit(solution)/shard_map/ppermute | solution.py:511
  107.2 8.6 %collective-permute-start.8 = (bf16[256,256]{1,0:T(8,128)(2,1)S(1)}, bf16[256,256]{1,0:T(8,128)(2,1)S(1)}, u32[]{:S(2)}, u32[]{:S(2)}) collective-permute-start(bf16[256,256]{1,0:T(8,128)(2,1)S(1)} %fusion.7.refs_4_), channel_id=1, source_target_pairs={{0,4},{4,0},{8,12},{12,8},{16,20},{20,16},{24,28},{28,24},{1,5},{5... | collective-permute-start | bytes 393224 | tf_op jit(solution)/shard_map/ppermute | solution.py:514
  117.6 1.4 collective-permute-start.10
  119.0 6.4 %collective-permute-start.11 = (bf16[256,256]{1,0:T(8,128)(2,1)S(1)}, bf16[256,256]{1,0:T(8,128)(2,1)S(1)}, u32[]{:S(2)}, u32[]{:S(2)}) collective-permute-start(bf16[256,256]{1,0:T(8,128)(2,1)S(1)} %add_convert_fusion.1), channel_id=1, source_target_pairs={{0,8},{4,12},{8,0},{12,4},{16,24},{20,28},{24,16},{28,20},{1,9},{5... | collective-permute-start | bytes 393224 | tf_op jit(solution)/shard_map/ppermute | solution.py:434
  125.4 5.1 %collective-permute-start.12 = (bf16[256,256]{1,0:T(8,128)(2,1)S(1)}, bf16[256,256]{1,0:T(8,128)(2,1)S(1)}, u32[]{:S(2)}, u32[]{:S(2)}) collective-permute-start(bf16[256,256]{1,0:T(8,128)(2,1)S(1)} %add_convert_fusion), channel_id=1, source_target_pairs={{0,16},{4,20},{8,24},{12,28},{16,0},{20,4},{24,8},{28,12},{1,17},{... | collective-permute-start | bytes 393224 | tf_op jit(solution)/shard_map/ppermute | solution.py:434
Sparse Core Ops, SparseCore 0:
  13.3 38.4 all-gather.1

commit v6 on v5

--- a/solution.py
+++ b/solution.py
@@ -14,6 +14,22 @@
 CHUNK = LANES * SUBLANES
 PITCH = SUBLANES + 1
 TILE = 256
+
+
+def turn(tiles):
+    row = lax.broadcasted_iota(jnp.int32, (SUBLANES, LANES), 0)
+    tiles = [pltpu.roll(tile, i, 0) if i else tile for i, tile in enumerate(tiles)]
+    step = 1
+    while step < SUBLANES:
+        far = (row & step) != 0
+        tiles = [
+            jnp.where(far, tiles[(i + step) % SUBLANES], tiles[i]) for i in range(SUBLANES)
+        ]
+        step *= 2
+    tiles = [tiles[-i % SUBLANES] for i in range(SUBLANES)]
+    return [
+        pltpu.roll(tile, SUBLANES - i, 0) if i else tile for i, tile in enumerate(tiles)
+    ]
 
 
 def assemble_kernel(
@@ -56,7 +72,10 @@
         first = part * part_rows
         for start in range(0, part_rows, group):
             places = [
-                places_ref[table + of_cell * cell_nodes + first + start + k] for k in range(group)
+                pl.multiple_of(
+                    places_ref[table + of_cell * cell_nodes + first + start + k], SUBLANES
+                )
+                for k in range(group)
             ]
             sums = [
                 total[pl.ds(places[k], SUBLANES), :]
@@ -67,17 +86,22 @@
                 total[pl.ds(places[k], SUBLANES), :] = sums[k]
 
     def round_rows(first, which, zero):
-        base = (which * ext_count + first) * PITCH
+        base = pl.multiple_of((which * ext_count + first) * SUBLANES, 16 * SUBLANES)
+        upper, lower = (
+            turn(
+                [
+                    total[pl.ds(base + (start + i) * SUBLANES, SUBLANES), :]
+                    for i in range(SUBLANES)
+                ]
+            )
+            for start in (0, SUBLANES)
+        )
         for block in range(SUBLANES):
-            upper = total[pl.ds(base + block, SUBLANES, stride=PITCH), :]
-            lower = total[pl.ds(base + SUBLANES * PITCH + block, SUBLANES, stride=PITCH), :]
             rounded[
                 block // 2, pl.ds(first, 16), block % 2 * LANES : (block % 2 + 1) * LANES
-            ] = jnp.concatenate([upper, lower], axis=0).astype(jnp.bfloat16)
+            ] = jnp.concatenate([upper[block], lower[block]], axis=0).astype(jnp.bfloat16)
         if zero:
-            total[pl.ds(pl.multiple_of(base, SUBLANES), 16 * PITCH), :] = jnp.zeros(
-                (16 * PITCH, LANES), jnp.float32
-            )
+            total[pl.ds(base, 16 * SUBLANES), :] = jnp.zeros((16 * SUBLANES, LANES), jnp.float32)
 
     def round_part(part):
         pieces = share // 16
@@ -112,7 +136,7 @@
             total[pl.ds(pl.multiple_of(step * 64, 64), 64), :] = jnp.zeros((64, LANES), jnp.float32)
             return carry
 
-        lax.fori_loop(0, ext_count * PITCH // 64, zero, 0, unroll=4)
+        lax.fori_loop(0, ext_count * SUBLANES // 64, zero, 0, unroll=4)
 
     @pl.when(cell == 0)
     def _():
@@ -194,21 +218,21 @@
             ],
             out_specs=(pl.BlockSpec(memory_space=pl.ANY),) * 3,
             scratch_shapes=[
-                pltpu.VMEM((2 * ext_count * PITCH, LANES), jnp.float32),
+                pltpu.VMEM((2 * ext_count * SUBLANES, LANES), jnp.float32),
                 pltpu.VMEM((cell_nodes * PITCH, LANES), jnp.float32),
                 pltpu.VMEM((cell_nodes * PITCH, LANES), jnp.float32),
                 pltpu.VMEM((CHUNK // TILE, ext_count, TILE), jnp.bfloat16),
                 pltpu.SemaphoreType.DMA((cells, CHUNK // TILE)),
             ],
         ),
-        compiler_params=pltpu.CompilerParams(vmem_limit_bytes=57 * 1024 * 1024),
+        compiler_params=pltpu.CompilerParams(vmem_limit_bytes=38 * 1024 * 1024),
         cost_estimate=pl.CostEstimate(
             flops=16 * cells * cell_nodes * cell_nodes * count,
             bytes_accessed=chunks * cells * cell_nodes * cell_nodes * 2 + ext_count * count * 2,
             transcendentals=0,
         ),
     )(
-        jnp.concatenate([places, places + ext_count * PITCH]),
+        jnp.concatenate([places, places + ext_count * SUBLANES]),
         columns[None, :],
         nodes,
         cell_matrices,
@@ -249,7 +273,7 @@
         out_ref[:, at] = product
         return carry
 
-    lax.fori_loop(0, matrix_ref.shape[0], body, 0)
+    lax.fori_loop(0, matrix_ref.shape[0], body, 0, unroll=4)
 
 
 def own_part(step, extended, matrix, before, after):
@@ -466,7 +490,7 @@
             connectivity - face,
             connectivity - (face + own_count) + upper_at,
         ),
-    ).reshape(-1) * PITCH
+    ).reshape(-1) * SUBLANES
     columns_b = jnp.concatenate([ghost_b, face_b + face])
     columns_a = jnp.concatenate([ghost_a, face_a + face])
     own_columns = jnp.arange(own_count, dtype=jnp.int32) + face

time: 148 us -> 150 us (1.014)
  local copies, waits for them, and re-layouts: 4.38 us -> 14.1 us
  Pallas kernels: 76.4 us -> 71.1 us
  matrix products: 11.7 us -> 7.44 us
  starting transfers between devices: 28.1 us -> 31.1 us
    unnamed x13 -> x21, local copies, waits for them, and re-layouts: 2.63 us -> 13.4 us
    dot_general x8, matrix products: 10.3 us -> 6.03 us  [times(): return jnp.dot(left, right, preferred_element_type=jnp.float32)]
    pallas_call x4, Pallas kernels: 17.5 us -> 13.5 us  [own_part(): pl.pallas_call(functools.partial(own_kernel, step), out_shape=jax.ShapeDt...]
  transfers between devices with their start and end apart: 14 -> 14, of which waited for: 3 -> 3; matrix products, arithmetic and copies ran while one was open for 2% -> 1% of each run, Pallas kernels for 40% -> 36%
where the time goes in v6:
time: 150 us
  Pallas kernels  71.1 us (47%)
  starting transfers between devices  31.1 us (21%)
  local copies, waits for them, and re-layouts  14.1 us (9%)
  between operations  13.8 us (9%)
  waiting for transfers between devices  8.74 us (6%)
  matrix products  7.44 us (5%)
  other arithmetic  3.83 us (3%)
    pallas_call x1, Pallas kernels, assemble(): pl.pallas_call(assemble_kernel, out_shape=(half, half, jax.ShapeDtypeStru...  40.5 us
    ppermute x4, starting transfers between devices, per_device(): got_a = lax.ppermute(sent_a, 'slab', pairs_a)  21.1 us
    pallas_call x4, Pallas kernels, own_part(): pl.pallas_call(functools.partial(own_kernel, step), out_shape=jax.ShapeDt...  13.5 us
    unnamed x21, local copies, waits for them, and re-layouts  13.4 us
    pallas_call x1, Pallas kernels, orthonormal(): pl.pallas_call(functools.partial(orthonormal_kernel, scale), out_shape=ja...  10.1 us
    ppermute x3, waiting for transfers between devices, sum_over(): got = lax.ppermute(sent, axis, [(i, i ^ step) for i in range(count)])  8.7 us
    pallas_call x4, Pallas kernels, combine(): pl.pallas_call(functools.partial(combine_kernel, step), out_shape=out_sha...  6.94 us
    dot_general x8, matrix products, times(): return jnp.dot(left, right, preferred_element_type=jnp.float32)  6.03 us
  transfers between devices with their start and end apart: 14, of which 3 were waited for; matrix products, arithmetic and copies ran while one was open for 1% of the time, Pallas kernels for 36%

profile of v6, /device:TPU:0, one launch (start us, length us, event | category | flops | bytes accessed | tf_op | source)
XLA Modules:
  0.0 150.1 jit_solution(15059186444939000820)
XLA Ops:
  7.9 1.1 convert_element_type.67
  9.0 0.9 fusion.14
  13.5 2.2 %copy-done.6 = bf16[8,512,512]{2,1,0:T(8,128)(2,1)S(1)} copy-done((bf16[8,512,512]{2,1,0:T(8,128)(2,1)S(1)}, bf16[8,512,512]{2,1,0:T(8,128)(2,1)}, u32[]{:S(2)}) %copy-start.6) | copy-done | bytes 4194328
  15.7 40.5 %shard_map.56 = (bf16[2560,512]{1,0:T(8,128)(2,1)S(1)}, bf16[2560,512]{1,0:T(8,128)(2,1)S(1)}, bf16[8,2560,256]{2,1,0:T(8,128)(2,1)}) custom-call(s32[8192]{0:T(1024)S(1)} %pad_add_fusion.places_ref, s32[1,3072]{1,0:T(1,128)S(1)} %bitcast.26, s32[8,512,128]{2,1,0:T(8,128)S(1)} %broadcast_in_dim.5.nodes_ref, bf16[8,512,512]{2,1,0:T(8,128)(2,1)S(1)} %copy-done.6, ...), custom_call_target="tpu_custom_call" | custom-call | flops 103079215104 | bytes 28311552 | tf_op jit(solution)/shard_map/pallas_call | solution.py:203
  56.2 1.6 %copy-done = bf16[2560,512]{1,0:T(8,128)(2,1)} copy-done((bf16[2560,512]{1,0:T(8,128)(2,1)}, bf16[2560,512]{1,0:T(8,128)(2,1)S(1)}, u32[]{:S(2)}) %copy-start) | copy-done | bytes 2621464
  57.8 1.5 copy-done.2
  59.3 1.3 copy-done.4
  60.7 1.6 %copy-done.3 = bf16[2560,512]{1,0:T(8,128)(2,1)S(1)} copy-done((bf16[2560,512]{1,0:T(8,128)(2,1)S(1)}, bf16[2560,512]{1,0:T(8,128)(2,1)}, u32[]{:S(2)}) %copy-start.3) | copy-done | bytes 2621464
  63.2 0.9 copy-done.1
  65.6 7.9 %collective-permute-start.2 = (bf16[256,512]{1,0:T(8,128)(2,1)S(1)}, bf16[256,512]{1,0:T(8,128)(2,1)S(1)}, u32[]{:S(2)}, u32[]{:S(2)}) collective-permute-start(bf16[256,512]{1,0:T(8,128)(2,1)S(1)} %get-tuple-element.25.refs_0_), channel_id=1, source_target_pairs={{0,4},{4,0},{8,12},{12,8},{16,20},{20,16},{24,28},{28,24},{1,5},{5... | collective-permute-start | bytes 786440 | tf_op jit(solution)/shard_map/ppermute | solution.py:538
  73.5 4.0 %copy-done.7 = bf16[8,2560,256]{2,1,0:T(8,128)(2,1)S(1)} copy-done((bf16[8,2560,256]{2,1,0:T(8,128)(2,1)S(1)}, bf16[8,2560,256]{2,1,0:T(8,128)(2,1)}, u32[]{:S(2)}) %copy-start.7) | copy-done | bytes 10485784
  77.5 3.1 %shard_map.57.own_ref.refs_0_ = f32[256,2048]{1,0:T(8,128)S(1)} custom-call(bf16[256,2560]{1,0:T(8,128)(2,1)S(1)} %shard_map.55.extended_ref.refs_0_, bf16[8,2560,256]{2,1,0:T(8,128)(2,1)S(1)} %copy-done.7, bf16[256,512]{1,0:T(8,128)(2,1)S(1)} %get-tuple-element.25.refs_0_, bf16[256,512]{1,0:T(8,128)(2,1)S(1)} %get-tuple-element.27.refs_1_), custom_call_target="tpu_custom_call" | custom-call | flops 10737418240 | bytes 12582912 | tf_op jit(solution)/shard_map/pallas_call | solution.py:285
  80.6 1.3 shard_map.58
  82.8 0.8 fusion.18
  83.6 0.9 collective-permute-start.5
  84.5 3.8 %collective-permute-start.4 = (bf16[256,512]{1,0:T(8,128)(2,1)S(1)}, bf16[256,512]{1,0:T(8,128)(2,1)S(1)}, u32[]{:S(2)}, u32[]{:S(2)}) collective-permute-start(bf16[256,512]{1,0:T(8,128)(2,1)S(1)} %get-tuple-element.29.refs_1_), channel_id=1, source_target_pairs={{0,4},{4,0},{8,12},{12,8},{16,20},{20,16},{24,28},{28,24},{1,5},{5... | collective-permute-start | bytes 786440 | tf_op jit(solution)/shard_map/ppermute | solution.py:538
  88.4 3.2 %shard_map.59.own_ref.refs_0_ = f32[256,2048]{1,0:T(8,128)S(1)} custom-call(bf16[256,2560]{1,0:T(8,128)(2,1)S(1)} %get-tuple-element.15.extended_ref, bf16[8,2560,256]{2,1,0:T(8,128)(2,1)S(1)} %copy-done.8, bf16[256,2560]{1,0:T(8,128)(2,1)S(1)} %shard_map.55.extended_ref.refs_0_, bf16[256,512]{1,0:T(8,128)(2,1)S(1)} %get-tuple-element.29.refs_1_, ...), custom_call_target="tpu_custom_call" | custom-call | flops 10737418240 | bytes 12582912 | tf_op jit(solution)/shard_map/pallas_call | solution.py:285
  91.5 2.2 %shard_map.60 = (bf16[256,2560]{1,0:T(8,128)(2,1)S(1)}, f32[256,512]{1,0:T(8,128)}) custom-call(s32[2]{0:T(128)S(1)} %add_convert_fusion.2.there_ref, f32[256,2048]{1,0:T(8,128)S(1)} %shard_map.59.own_ref.refs_0_, bf16[256,512]{1,0:T(8,128)(2,1)S(1)} %collective-permute-done.4.got_a_ref.refs_1_, ...), custom_call_target="tpu_custom_call" | custom-call | tf_op jit(solution)/shard_map/pallas_call | solution.py:332
  94.6 0.8 fusion.20
  96.1 4.0 %collective-permute-start.6 = (bf16[256,512]{1,0:T(8,128)(2,1)S(1)}, bf16[256,512]{1,0:T(8,128)(2,1)S(1)}, u32[]{:S(2)}, u32[]{:S(2)}) collective-permute-start(bf16[256,512]{1,0:T(8,128)(2,1)S(1)} %get-tuple-element.33.refs_4_), channel_id=1, source_target_pairs={{0,4},{4,0},{8,12},{12,8},{16,20},{20,16},{24,28},{28,24},{1,5},{5... | collective-permute-start | bytes 786440 | tf_op jit(solution)/shard_map/ppermute | solution.py:538
  100.1 3.7 %shard_map.61.own_ref = f32[256,2048]{1,0:T(8,128)S(1)} custom-call(bf16[256,2560]{1,0:T(8,128)(2,1)S(1)} %get-tuple-element.16.extended_ref, bf16[8,2560,256]{2,1,0:T(8,128)(2,1)S(1)} %copy-done.8, f32[256,2048]{1,0:T(8,128)S(1)} %shard_map.57.own_ref.refs_0_, bf16[256,512]{1,0:T(8,128)(2,1)S(1)} %collective-permute-done.2.got_a_ref.refs_1_, ...), custom_call_target="tpu_custom_call" | custom-call | flops 10737418240 | bytes 12582912 | tf_op jit(solution)/shard_map/pallas_call | solution.py:285
  103.8 2.2 %shard_map.62 = (bf16[256,2560]{1,0:T(8,128)(2,1)S(1)}, f32[256,512]{1,0:T(8,128)}) custom-call(s32[2]{0:T(128)S(1)} %add_convert_fusion.2.there_ref, f32[256,2048]{1,0:T(8,128)S(1)} %shard_map.61.own_ref, bf16[256,512]{1,0:T(8,128)(2,1)S(1)} %collective-permute-done.6.got_a_ref, bf16[256,512]{1,0:T(8,128)(2,1)S(1)} %collective-permute-done.7.got_b_ref, ...), custom_call_target="tpu_custom_call" | custom-call | tf_op jit(solution)/shard_map/pallas_call | solution.py:332
  107.0 0.9 collective-permute-start.9
  107.9 5.4 %collective-permute-start.8 = (bf16[256,256]{1,0:T(8,128)(2,1)S(1)}, bf16[256,256]{1,0:T(8,128)(2,1)S(1)}, u32[]{:S(2)}, u32[]{:S(2)}) collective-permute-start(bf16[256,256]{1,0:T(8,128)(2,1)S(1)} %fusion.7.refs_4_), channel_id=1, source_target_pairs={{0,4},{4,0},{8,12},{12,8},{16,20},{20,16},{24,28},{28,24},{1,5},{5... | collective-permute-start | bytes 393224 | tf_op jit(solution)/shard_map/ppermute | solution.py:538
  113.2 3.6 %shard_map.63.own_ref = f32[256,2048]{1,0:T(8,128)S(1)} custom-call(bf16[256,2560]{1,0:T(8,128)(2,1)S(1)} %get-tuple-element.18.extended_ref, bf16[8,2560,256]{2,1,0:T(8,128)(2,1)S(1)} %copy-done.8, f32[256,2048]{1,0:T(8,128)S(1)} %shard_map.59.own_ref.refs_0_, bf16[256,512]{1,0:T(8,128)(2,1)S(1)} %collective-permute-done.4.got_a_ref.refs_1_, ...), custom_call_target="tpu_custom_call" | custom-call | flops 10737418240 | bytes 12582912 | tf_op jit(solution)/shard_map/pallas_call | solution.py:285
  116.9 1.3 shard_map.64.filtered_ref
  118.7 1.3 collective-permute-done.10
  120.1 4.0 %collective-permute-start.11 = (bf16[256,256]{1,0:T(8,128)(2,1)S(1)}, bf16[256,256]{1,0:T(8,128)(2,1)S(1)}, u32[]{:S(2)}, u32[]{:S(2)}) collective-permute-start(bf16[256,256]{1,0:T(8,128)(2,1)S(1)} %add_convert_fusion.1), channel_id=1, source_target_pairs={{0,8},{4,12},{8,0},{12,4},{16,24},{20,28},{24,16},{28,20},{1,9},{5... | collective-permute-start | bytes 393224 | tf_op jit(solution)/shard_map/ppermute | solution.py:458
  124.1 3.8 %collective-permute-done.11 = bf16[256,256]{1,0:T(8,128)(2,1)S(1)} collective-permute-done((bf16[256,256]{1,0:T(8,128)(2,1)S(1)}, bf16[256,256]{1,0:T(8,128)(2,1)S(1)}, u32[]{:S(2)}, u32[]{:S(2)}) %collective-permute-start.11) | collective-permute-done | bytes 131104 | tf_op jit(solution)/shard_map/ppermute | solution.py:458
  128.0 1.5 %collective-permute-start.12 = (bf16[256,256]{1,0:T(8,128)(2,1)S(1)}, bf16[256,256]{1,0:T(8,128)(2,1)S(1)}, u32[]{:S(2)}, u32[]{:S(2)}) collective-permute-start(bf16[256,256]{1,0:T(8,128)(2,1)S(1)} %add_convert_fusion), channel_id=1, source_target_pairs={{0,16},{4,20},{8,24},{12,28},{16,0},{20,4},{24,8},{28,12},{1,17},{... | collective-permute-start | bytes 393224 | tf_op jit(solution)/shard_map/ppermute | solution.py:458
  129.5 3.6 %collective-permute-done.12 = bf16[256,256]{1,0:T(8,128)(2,1)S(1)} collective-permute-done((bf16[256,256]{1,0:T(8,128)(2,1)S(1)}, bf16[256,256]{1,0:T(8,128)(2,1)S(1)}, u32[]{:S(2)}, u32[]{:S(2)}) %collective-permute-start.12) | collective-permute-done | bytes 131104 | tf_op jit(solution)/shard_map/ppermute | solution.py:458
  133.1 10.1 %shard_map.65 = f32[64,2048]{1,0:T(8,128)} custom-call(s32[1]{0:T(128)} %bitcast.block_ref, f32[256,256]{1,0:T(8,128)S(1)} %convert_add_fusion.gram_ref, bf16[256,2048]{1,0:T(8,128)(2,1)S(1)} %shard_map.64.filtered_ref), custom_call_target="tpu_custom_call" | custom-call | tf_op jit(solution)/shard_map/pallas_call | solution.py:430
  (59 shorter events, 11.3 us)
Async XLA Ops:
  6.5 52.7 %all-gather.2.cloned.1.call-start = ((), (), s32[]{:S(2)}) async-start(), calls=%async_computation | async-start | bytes 1638400 | tf_op jit(solution)/shard_map/all_gather | solution.py:517
  9.0 2.6 %copy-start.9 = (s32[8,512]{1,0:T(8,128)S(1)}, s32[8,512]{1,0:T(8,128)}, u32[]{:S(2)}) copy-start(s32[8,512]{1,0:T(8,128)} %param.7) | copy-start | bytes 49156
  10.0 1.8 %collective-permute-start = (bf16[64,256]{1,0:T(8,128)(2,1)S(1)}, bf16[64,256]{1,0:T(8,128)(2,1)S(1)}, u32[]{:S(2)}, u32[]{:S(2)}) collective-permute-start(bf16[64,256]{1,0:T(8,128)(2,1)S(1)} %get-tuple-element.23), channel_id=1, source_target_pairs={{0,4},{4,0},{8,12},{12,8},{16,20},{20,16},{24,28},{28,24},{1,5},{5... | collective-permute-start | bytes 98312 | tf_op jit(solution)/shard_map/ppermute | solution.py:515
  10.5 1.3 collective-permute-start.1
  12.5 1.0 copy-start.5
  13.5 2.2 %copy-start.6 = (bf16[8,512,512]{2,1,0:T(8,128)(2,1)S(1)}, bf16[8,512,512]{2,1,0:T(8,128)(2,1)}, u32[]{:S(2)}) copy-start(bf16[8,512,512]{2,1,0:T(8,128)(2,1)} %cell_ref.1) | copy-start | bytes 12582916
  56.2 1.6 %copy-start = (bf16[2560,512]{1,0:T(8,128)(2,1)}, bf16[2560,512]{1,0:T(8,128)(2,1)S(1)}, u32[]{:S(2)}) copy-start(bf16[2560,512]{1,0:T(8,128)(2,1)S(1)} %get-tuple-element.13) | copy-start | bytes 7864324
  57.8 1.5 copy-start.2
  59.3 1.3 copy-start.4
  60.6 1.7 %copy-start.3 = (bf16[2560,512]{1,0:T(8,128)(2,1)S(1)}, bf16[2560,512]{1,0:T(8,128)(2,1)}, u32[]{:S(2)}) copy-start(bf16[2560,512]{1,0:T(8,128)(2,1)} %copy-done.2) | copy-start | bytes 7864324
  62.3 1.7 %copy-start.1 = (bf16[2560,512]{1,0:T(8,128)(2,1)S(1)}, bf16[2560,512]{1,0:T(8,128)(2,1)}, u32[]{:S(2)}) copy-start(bf16[2560,512]{1,0:T(8,128)(2,1)} %copy-done) | copy-start | bytes 7864324
  64.9 15.7 %collective-permute-start.3 = (bf16[256,512]{1,0:T(8,128)(2,1)S(1)}, bf16[256,512]{1,0:T(8,128)(2,1)S(1)}, u32[]{:S(2)}, u32[]{:S(2)}) collective-permute-start(bf16[256,512]{1,0:T(8,128)(2,1)S(1)} %get-tuple-element.27.refs_1_), channel_id=1, source_target_pairs={{4,8},{8,4},{12,16},{16,12},{20,24},{24,20},{5,9},{9,5},{13,17},{1... | collective-permute-start | bytes 786440 | tf_op jit(solution)/shard_map/ppermute | solution.py:535
  65.6 15.0 %collective-permute-start.2 = (bf16[256,512]{1,0:T(8,128)(2,1)S(1)}, bf16[256,512]{1,0:T(8,128)(2,1)S(1)}, u32[]{:S(2)}, u32[]{:S(2)}) collective-permute-start(bf16[256,512]{1,0:T(8,128)(2,1)S(1)} %get-tuple-element.25.refs_0_), channel_id=1, source_target_pairs={{0,4},{4,0},{8,12},{12,8},{16,20},{20,16},{24,28},{28,24},{1,5},{5... | collective-permute-start | bytes 786440 | tf_op jit(solution)/shard_map/ppermute | solution.py:538
  73.5 4.0 %copy-start.7 = (bf16[8,2560,256]{2,1,0:T(8,128)(2,1)S(1)}, bf16[8,2560,256]{2,1,0:T(8,128)(2,1)}, u32[]{:S(2)}) copy-start(bf16[8,2560,256]{2,1,0:T(8,128)(2,1)} %get-tuple-element.12.matrix_ref) | copy-start | bytes 31457284
  80.6 7.7 %copy-start.8 = (bf16[8,2560,256]{2,1,0:T(8,128)(2,1)S(1)}, bf16[8,2560,256]{2,1,0:T(8,128)(2,1)}, u32[]{:S(2)}) copy-start(bf16[8,2560,256]{2,1,0:T(8,128)(2,1)} %get-tuple-element.12.matrix_ref) | copy-start | bytes 31457284
  83.6 7.9 %collective-permute-start.5 = (bf16[256,512]{1,0:T(8,128)(2,1)S(1)}, bf16[256,512]{1,0:T(8,128)(2,1)S(1)}, u32[]{:S(2)}, u32[]{:S(2)}) collective-permute-start(bf16[256,512]{1,0:T(8,128)(2,1)S(1)} %get-tuple-element.31.refs_2_), channel_id=1, source_target_pairs={{4,8},{8,4},{12,16},{16,12},{20,24},{24,20},{5,9},{9,5},{13,17},{1... | collective-permute-start | bytes 786440 | tf_op jit(solution)/shard_map/ppermute | solution.py:535
  84.5 7.0 %collective-permute-start.4 = (bf16[256,512]{1,0:T(8,128)(2,1)S(1)}, bf16[256,512]{1,0:T(8,128)(2,1)S(1)}, u32[]{:S(2)}, u32[]{:S(2)}) collective-permute-start(bf16[256,512]{1,0:T(8,128)(2,1)S(1)} %get-tuple-element.29.refs_1_), channel_id=1, source_target_pairs={{0,4},{4,0},{8,12},{12,8},{16,20},{20,16},{24,28},{28,24},{1,5},{5... | collective-permute-start | bytes 786440 | tf_op jit(solution)/shard_map/ppermute | solution.py:538
  95.4 8.3 %collective-permute-start.7 = (bf16[256,512]{1,0:T(8,128)(2,1)S(1)}, bf16[256,512]{1,0:T(8,128)(2,1)S(1)}, u32[]{:S(2)}, u32[]{:S(2)}) collective-permute-start(bf16[256,512]{1,0:T(8,128)(2,1)S(1)} %get-tuple-element.35.refs_5_), channel_id=1, source_target_pairs={{4,8},{8,4},{12,16},{16,12},{20,24},{24,20},{5,9},{9,5},{13,17},{1... | collective-permute-start | bytes 786440 | tf_op jit(solution)/shard_map/ppermute | solution.py:535
  96.1 7.6 %collective-permute-start.6 = (bf16[256,512]{1,0:T(8,128)(2,1)S(1)}, bf16[256,512]{1,0:T(8,128)(2,1)S(1)}, u32[]{:S(2)}, u32[]{:S(2)}) collective-permute-start(bf16[256,512]{1,0:T(8,128)(2,1)S(1)} %get-tuple-element.33.refs_4_), channel_id=1, source_target_pairs={{0,4},{4,0},{8,12},{12,8},{16,20},{20,16},{24,28},{28,24},{1,5},{5... | collective-permute-start | bytes 786440 | tf_op jit(solution)/shard_map/ppermute | solution.py:538
  107.0 9.9 %collective-permute-start.9 = (bf16[256,256]{1,0:T(8,128)(2,1)S(1)}, bf16[256,256]{1,0:T(8,128)(2,1)S(1)}, u32[]{:S(2)}, u32[]{:S(2)}) collective-permute-start(bf16[256,256]{1,0:T(8,128)(2,1)S(1)} %fusion.10.refs_5_), channel_id=1, source_target_pairs={{4,8},{8,4},{12,16},{16,12},{20,24},{24,20},{5,9},{9,5},{13,17},{1... | collective-permute-start | bytes 393224 | tf_op jit(solution)/shard_map/ppermute | solution.py:535
  107.9 9.0 %collective-permute-start.8 = (bf16[256,256]{1,0:T(8,128)(2,1)S(1)}, bf16[256,256]{1,0:T(8,128)(2,1)S(1)}, u32[]{:S(2)}, u32[]{:S(2)}) collective-permute-start(bf16[256,256]{1,0:T(8,128)(2,1)S(1)} %fusion.7.refs_4_), channel_id=1, source_target_pairs={{0,4},{4,0},{8,12},{12,8},{16,20},{20,16},{24,28},{28,24},{1,5},{5... | collective-permute-start | bytes 393224 | tf_op jit(solution)/shard_map/ppermute | solution.py:538
  118.6 1.4 collective-permute-start.10
  120.1 7.9 %collective-permute-start.11 = (bf16[256,256]{1,0:T(8,128)(2,1)S(1)}, bf16[256,256]{1,0:T(8,128)(2,1)S(1)}, u32[]{:S(2)}, u32[]{:S(2)}) collective-permute-start(bf16[256,256]{1,0:T(8,128)(2,1)S(1)} %add_convert_fusion.1), channel_id=1, source_target_pairs={{0,8},{4,12},{8,0},{12,4},{16,24},{20,28},{24,16},{28,20},{1,9},{5... | collective-permute-start | bytes 393224 | tf_op jit(solution)/shard_map/ppermute | solution.py:458
  128.0 5.1 %collective-permute-start.12 = (bf16[256,256]{1,0:T(8,128)(2,1)S(1)}, bf16[256,256]{1,0:T(8,128)(2,1)S(1)}, u32[]{:S(2)}, u32[]{:S(2)}) collective-permute-start(bf16[256,256]{1,0:T(8,128)(2,1)S(1)} %add_convert_fusion), channel_id=1, source_target_pairs={{0,16},{4,20},{8,24},{12,28},{16,0},{20,4},{24,8},{28,12},{1,17},{... | collective-permute-start | bytes 393224 | tf_op jit(solution)/shard_map/ppermute | solution.py:458
Sparse Core Ops, SparseCore 0:
  12.7 38.9 all-gather.1

commit v7 on v6

--- a/solution.py
+++ b/solution.py
@@ -225,7 +225,7 @@
                 pltpu.SemaphoreType.DMA((cells, CHUNK // TILE)),
             ],
         ),
-        compiler_params=pltpu.CompilerParams(vmem_limit_bytes=38 * 1024 * 1024),
+        compiler_params=pltpu.CompilerParams(vmem_limit_bytes=57 * 1024 * 1024),
         cost_estimate=pl.CostEstimate(
             flops=16 * cells * cell_nodes * cell_nodes * count,
             bytes_accessed=chunks * cells * cell_nodes * cell_nodes * 2 + ext_count * count * 2,
@@ -240,16 +240,25 @@
     )
 
 
-def hold_kernel(in_ref, out_ref):
-    out_ref[...] = in_ref[...]
-
-
-def hold(values):
+def hold_kernel(*refs):
+    count = len(refs) // 2
+    done = refs[-1]
+    copies = [pltpu.make_async_copy(refs[i], refs[count + i], done.at[i]) for i in range(count)]
+    for copy in copies:
+        copy.start()
+    for copy in copies:
+        copy.wait()
+
+
+def hold(*arrays):
     return pl.pallas_call(
         hold_kernel,
-        out_shape=jax.ShapeDtypeStruct(values.shape, values.dtype),
+        out_shape=tuple(jax.ShapeDtypeStruct(x.shape, x.dtype) for x in arrays),
+        in_specs=[pl.BlockSpec(memory_space=pl.ANY)] * len(arrays),
+        out_specs=(pl.BlockSpec(memory_space=pltpu.VMEM),) * len(arrays),
+        scratch_shapes=[pltpu.SemaphoreType.DMA((len(arrays),))],
         compiler_params=pltpu.CompilerParams(vmem_limit_bytes=16 * 1024 * 1024),
-    )(values)
+    )(*arrays)
 
 
 def arrived(got_a_ref, got_b_ref, table_ref, at):
@@ -370,8 +379,15 @@
             ]
             for g in later
         }
+        pivots = {
+            (i, j): over_rows(column[k][j], i) for i in range(SUBLANES) for j in range(i + 1)
+        }
         for q in range(SUBLANES):
-            scale = lax.rsqrt(over_rows(column[k][q], q))
+            scale = lax.rsqrt(pivots[q, q])
+            weights = {i: pivots[i, q] * scale for i in range(q + 1, SUBLANES)}
+            for i in range(q + 1, SUBLANES):
+                for j in range(q + 1, i + 1):
+                    pivots[i, j] = pivots[i, j] - weights[i] * weights[j]
             factor = {g: column[g][q] * scale for g in later}
             left_row = over_rows(left[k], q) * scale
             right_row = over_rows(right[k], q) * scale
@@ -379,9 +395,8 @@
             left[k] = jnp.where(row == q, left_row, left[k] - below * left_row)
             right[k] = jnp.where(row == q, right_row, right[k] - below * right_row)
             for other in range(q + 1, SUBLANES):
-                weight = over_rows(factor[k], other)
                 for g in later:
-                    column[g][other] = column[g][other] - factor[g] * weight
+                    column[g][other] = column[g][other] - factor[g] * weights[other]
             for g in range(k + 1, groups):
                 left[g] = left[g] - factor[g] * left_row
                 right[g] = right[g] - factor[g] * right_row
@@ -525,7 +540,7 @@
     )
 
     there = jnp.stack([has_a, has_b]).astype(jnp.int32)
-    field = hold(gathered)
+    field, matrix_b, matrix_a = hold(gathered, matrix_b, matrix_a)
     ghosts = [field[:, own_count:]]
     before = ()
     for step in range(DEGREE):

time: 150 us -> 147 us (0.980)
  local copies, waits for them, and re-layouts: 14.1 us -> 6.53 us
  Pallas kernels: 71.1 us -> 74.2 us
    unnamed x21 -> x13, local copies, waits for them, and re-layouts: 13.4 us -> 4.81 us
  transfers between devices with their start and end apart: 14 -> 14, of which waited for: 3 -> 3; matrix products, arithmetic and copies ran while one was open for 1% -> 2% of each run, Pallas kernels for 36% -> 38%
where the time goes in v7:
time: 147 us; the launch traced here: 146 us
  Pallas kernels  74.2 us (50%)
  starting transfers between devices  31.3 us (21%)
  between operations  13.8 us (9%)
  waiting for transfers between devices  8.8 us (6%)
  matrix products  7.44 us (5%)
  local copies, waits for them, and re-layouts  6.53 us (4%)
  other arithmetic  4.43 us (3%)
    pallas_call x1, Pallas kernels, assemble(): pl.pallas_call(assemble_kernel, out_shape=(half, half, jax.ShapeDtypeStru...  41.9 us
    ppermute x4, starting transfers between devices, per_device(): got_a = lax.ppermute(sent_a, 'slab', pairs_a)  21.7 us
    pallas_call x4, Pallas kernels, own_part(): pl.pallas_call(functools.partial(own_kernel, step), out_shape=jax.ShapeDt...  13.5 us
    pallas_call x1, Pallas kernels, orthonormal(): pl.pallas_call(functools.partial(orthonormal_kernel, scale), out_shape=ja...  11.3 us
    ppermute x3, waiting for transfers between devices, sum_over(): got = lax.ppermute(sent, axis, [(i, i ^ step) for i in range(count)])  8.74 us
    pallas_call x4, Pallas kernels, combine(): pl.pallas_call(functools.partial(combine_kernel, step), out_shape=out_sha...  6.94 us
    dot_general x8, matrix products, times(): return jnp.dot(left, right, preferred_element_type=jnp.float32)  6.03 us
    ppermute x3, starting transfers between devices, sum_over(): got = lax.ppermute(sent, axis, [(i, i ^ step) for i in range(count)])  5.37 us
  transfers between devices with their start and end apart: 14, of which 3 were waited for; matrix products, arithmetic and copies ran while one was open for 2% of the time, Pallas kernels for 38%

profile of v7, /device:TPU:0, one launch (start us, length us, event | category | flops | bytes accessed | tf_op | source)
XLA Modules:
  0.0 146.4 jit_solution(16613719672741789191)
XLA Ops:
  7.9 1.1 convert_element_type.67
  9.0 0.9 fusion.14
  13.1 1.7 %broadcast_in_dim.5.nodes_ref = s32[8,512,128]{2,1,0:T(8,128)} broadcast(s32[8,512]{1,0:T(8,128)S(1)} %copy-done.4), dimensions={0,1} | broadcast | bytes 2113536 | tf_op jit(solution)/shard_map/broadcast_in_dim | solution.py:512
  14.8 41.9 %shard_map.55 = (bf16[2560,512]{1,0:T(8,128)(2,1)}, bf16[2560,512]{1,0:T(8,128)(2,1)}, bf16[8,2560,256]{2,1,0:T(8,128)(2,1)}) custom-call(s32[8192]{0:T(1024)} %pad_add_fusion.places_ref, s32[1,3072]{1,0:T(1,128)} %bitcast.28, s32[8,512,128]{2,1,0:T(8,128)} %broadcast_in_dim.5.nodes_ref, bf16[8,512,512]{2,1,0:T(8,128)(2,1)} %cell_ref.1, ...), custom_call_target="tpu_custom_call" | custom-call | flops 103079215104 | bytes 28311552 | tf_op jit(solution)/shard_map/pallas_call | solution.py:203
  56.8 1.7 %copy-done = bf16[2560,512]{1,0:T(8,128)(2,1)S(1)} copy-done((bf16[2560,512]{1,0:T(8,128)(2,1)S(1)}, bf16[2560,512]{1,0:T(8,128)(2,1)}, u32[]{:S(2)}) %copy-start) | copy-done | bytes 2621464
  58.5 1.7 %copy-done.1 = bf16[2560,512]{1,0:T(8,128)(2,1)S(1)} copy-done((bf16[2560,512]{1,0:T(8,128)(2,1)S(1)}, bf16[2560,512]{1,0:T(8,128)(2,1)}, u32[]{:S(2)}) %copy-start.1) | copy-done | bytes 2621464
  60.3 1.3 copy-done.2
  62.1 0.8 fusion.17
  62.9 0.8 fusion.16
  64.6 7.5 %collective-permute-start.2 = (bf16[256,512]{1,0:T(8,128)(2,1)S(1)}, bf16[256,512]{1,0:T(8,128)(2,1)S(1)}, u32[]{:S(2)}, u32[]{:S(2)}) collective-permute-start(bf16[256,512]{1,0:T(8,128)(2,1)S(1)} %get-tuple-element.31.refs_0_), channel_id=1, source_target_pairs={{0,4},{4,0},{8,12},{12,8},{16,20},{20,16},{24,28},{28,24},{1,5},{5... | collective-permute-start | bytes 786440 | tf_op jit(solution)/shard_map/ppermute | solution.py:553
  72.1 3.1 %shard_map.57.own_ref.refs_0_ = f32[256,2048]{1,0:T(8,128)S(1)} custom-call(bf16[256,2560]{1,0:T(8,128)(2,1)S(1)} %get-tuple-element.17.extended_ref.refs_0_, bf16[8,2560,256]{2,1,0:T(8,128)(2,1)S(1)} %copy-done.3, bf16[256,512]{1,0:T(8,128)(2,1)S(1)} %get-tuple-element.31.refs_0_, bf16[256,512]{1,0:T(8,128)(2,1)S(1)} %get-tuple-element.33.refs_1_), custom_call_target="tpu_custom_call" | custom-call | flops 10737418240 | bytes 12582912 | tf_op jit(solution)/shard_map/pallas_call | solution.py:294
  75.3 1.3 shard_map.58
  76.6 0.8 fusion.19
  77.4 0.8 fusion.18
  78.3 0.9 collective-permute-start.5
  79.1 3.9 %collective-permute-start.4 = (bf16[256,512]{1,0:T(8,128)(2,1)S(1)}, bf16[256,512]{1,0:T(8,128)(2,1)S(1)}, u32[]{:S(2)}, u32[]{:S(2)}) collective-permute-start(bf16[256,512]{1,0:T(8,128)(2,1)S(1)} %get-tuple-element.35.refs_1_), channel_id=1, source_target_pairs={{0,4},{4,0},{8,12},{12,8},{16,20},{20,16},{24,28},{28,24},{1,5},{5... | collective-permute-start | bytes 786440 | tf_op jit(solution)/shard_map/ppermute | solution.py:553
  83.0 3.2 %shard_map.59.own_ref.refs_0_ = f32[256,2048]{1,0:T(8,128)S(1)} custom-call(bf16[256,2560]{1,0:T(8,128)(2,1)S(1)} %get-tuple-element.21.extended_ref, bf16[8,2560,256]{2,1,0:T(8,128)(2,1)S(1)} %copy-done.3, bf16[256,2560]{1,0:T(8,128)(2,1)S(1)} %get-tuple-element.17.extended_ref.refs_0_, bf16[256,512]{1,0:T(8,128)(2,1)S(1)} %get-tuple-element.35.refs_1_, ...), custom_call_target="tpu_custom_call" | custom-call | flops 10737418240 | bytes 12582912 | tf_op jit(solution)/shard_map/pallas_call | solution.py:294
  86.2 2.2 %shard_map.60 = (bf16[256,2560]{1,0:T(8,128)(2,1)S(1)}, f32[256,512]{1,0:T(8,128)}) custom-call(s32[2]{0:T(128)S(1)} %add_convert_fusion.2.there_ref, f32[256,2048]{1,0:T(8,128)S(1)} %shard_map.59.own_ref.refs_0_, bf16[256,512]{1,0:T(8,128)(2,1)S(1)} %collective-permute-done.4.got_a_ref.refs_1_, ...), custom_call_target="tpu_custom_call" | custom-call | tf_op jit(solution)/shard_map/pallas_call | solution.py:341
  88.4 0.8 fusion.21
  89.2 0.8 fusion.20
  90.8 5.7 %collective-permute-start.6 = (bf16[256,512]{1,0:T(8,128)(2,1)S(1)}, bf16[256,512]{1,0:T(8,128)(2,1)S(1)}, u32[]{:S(2)}, u32[]{:S(2)}) collective-permute-start(bf16[256,512]{1,0:T(8,128)(2,1)S(1)} %get-tuple-element.39.refs_4_), channel_id=1, source_target_pairs={{0,4},{4,0},{8,12},{12,8},{16,20},{20,16},{24,28},{28,24},{1,5},{5... | collective-permute-start | bytes 786440 | tf_op jit(solution)/shard_map/ppermute | solution.py:553
  96.5 3.7 %shard_map.61.own_ref = f32[256,2048]{1,0:T(8,128)S(1)} custom-call(bf16[256,2560]{1,0:T(8,128)(2,1)S(1)} %get-tuple-element.22.extended_ref, bf16[8,2560,256]{2,1,0:T(8,128)(2,1)S(1)} %copy-done.3, f32[256,2048]{1,0:T(8,128)S(1)} %shard_map.57.own_ref.refs_0_, bf16[256,512]{1,0:T(8,128)(2,1)S(1)} %collective-permute-done.2.got_a_ref.refs_1_, ...), custom_call_target="tpu_custom_call" | custom-call | flops 10737418240 | bytes 12582912 | tf_op jit(solution)/shard_map/pallas_call | solution.py:294
  100.2 2.2 %shard_map.62 = (bf16[256,2560]{1,0:T(8,128)(2,1)S(1)}, f32[256,512]{1,0:T(8,128)}) custom-call(s32[2]{0:T(128)S(1)} %add_convert_fusion.2.there_ref, f32[256,2048]{1,0:T(8,128)S(1)} %shard_map.61.own_ref, bf16[256,512]{1,0:T(8,128)(2,1)S(1)} %collective-permute-done.6.got_a_ref, bf16[256,512]{1,0:T(8,128)(2,1)S(1)} %collective-permute-done.7.got_b_ref, ...), custom_call_target="tpu_custom_call" | custom-call | tf_op jit(solution)/shard_map/pallas_call | solution.py:341
  104.0 4.6 %collective-permute-start.8 = (bf16[256,256]{1,0:T(8,128)(2,1)S(1)}, bf16[256,256]{1,0:T(8,128)(2,1)S(1)}, u32[]{:S(2)}, u32[]{:S(2)}) collective-permute-start(bf16[256,256]{1,0:T(8,128)(2,1)S(1)} %fusion.7.refs_4_), channel_id=1, source_target_pairs={{0,4},{4,0},{8,12},{12,8},{16,20},{20,16},{24,28},{28,24},{1,5},{5... | collective-permute-start | bytes 393224 | tf_op jit(solution)/shard_map/ppermute | solution.py:553
  108.6 3.7 %shard_map.63.own_ref = f32[256,2048]{1,0:T(8,128)S(1)} custom-call(bf16[256,2560]{1,0:T(8,128)(2,1)S(1)} %get-tuple-element.24.extended_ref, bf16[8,2560,256]{2,1,0:T(8,128)(2,1)S(1)} %copy-done.3, f32[256,2048]{1,0:T(8,128)S(1)} %shard_map.59.own_ref.refs_0_, bf16[256,512]{1,0:T(8,128)(2,1)S(1)} %collective-permute-done.4.got_a_ref.refs_1_, ...), custom_call_target="tpu_custom_call" | custom-call | flops 10737418240 | bytes 12582912 | tf_op jit(solution)/shard_map/pallas_call | solution.py:294
  112.3 1.3 shard_map.64.filtered_ref
  114.1 1.3 collective-permute-done.10
  115.5 3.4 %collective-permute-start.11 = (bf16[256,256]{1,0:T(8,128)(2,1)S(1)}, bf16[256,256]{1,0:T(8,128)(2,1)S(1)}, u32[]{:S(2)}, u32[]{:S(2)}) collective-permute-start(bf16[256,256]{1,0:T(8,128)(2,1)S(1)} %add_convert_fusion.1), channel_id=1, source_target_pairs={{0,8},{4,12},{8,0},{12,4},{16,24},{20,28},{24,16},{28,20},{1,9},{5... | collective-permute-start | bytes 393224 | tf_op jit(solution)/shard_map/ppermute | solution.py:473
  118.9 4.0 %collective-permute-done.11 = bf16[256,256]{1,0:T(8,128)(2,1)S(1)} collective-permute-done((bf16[256,256]{1,0:T(8,128)(2,1)S(1)}, bf16[256,256]{1,0:T(8,128)(2,1)S(1)}, u32[]{:S(2)}, u32[]{:S(2)}) %collective-permute-start.11) | collective-permute-done | bytes 131104 | tf_op jit(solution)/shard_map/ppermute | solution.py:473
  123.0 1.9 %collective-permute-start.12 = (bf16[256,256]{1,0:T(8,128)(2,1)S(1)}, bf16[256,256]{1,0:T(8,128)(2,1)S(1)}, u32[]{:S(2)}, u32[]{:S(2)}) collective-permute-start(bf16[256,256]{1,0:T(8,128)(2,1)S(1)} %add_convert_fusion), channel_id=1, source_target_pairs={{0,16},{4,20},{8,24},{12,28},{16,0},{20,4},{24,8},{28,12},{1,17},{... | collective-permute-start | bytes 393224 | tf_op jit(solution)/shard_map/ppermute | solution.py:473
  124.8 3.4 %collective-permute-done.12 = bf16[256,256]{1,0:T(8,128)(2,1)S(1)} collective-permute-done((bf16[256,256]{1,0:T(8,128)(2,1)S(1)}, bf16[256,256]{1,0:T(8,128)(2,1)S(1)}, u32[]{:S(2)}, u32[]{:S(2)}) %collective-permute-start.12) | collective-permute-done | bytes 131104 | tf_op jit(solution)/shard_map/ppermute | solution.py:473
  128.3 11.3 %shard_map.65 = f32[64,2048]{1,0:T(8,128)} custom-call(s32[1]{0:T(128)} %bitcast.block_ref, f32[256,256]{1,0:T(8,128)S(1)} %convert_add_fusion.gram_ref, bf16[256,2048]{1,0:T(8,128)(2,1)S(1)} %shard_map.64.filtered_ref), custom_call_target="tpu_custom_call" | custom-call | tf_op jit(solution)/shard_map/pallas_call | solution.py:445
  (51 shorter events, 8.8 us)
Async XLA Ops:
  6.5 50.2 %all-gather.2.cloned.1.call-start = ((), (), s32[]{:S(2)}) async-start(), calls=%async_computation | async-start | bytes 1638400 | tf_op jit(solution)/shard_map/all_gather | solution.py:532
  9.0 2.6 %copy-start.4 = (s32[8,512]{1,0:T(8,128)S(1)}, s32[8,512]{1,0:T(8,128)}, u32[]{:S(2)}) copy-start(s32[8,512]{1,0:T(8,128)} %param.7) | copy-start | bytes 49156
  10.0 2.4 %collective-permute-start = (bf16[64,256]{1,0:T(8,128)(2,1)S(1)}, bf16[64,256]{1,0:T(8,128)(2,1)S(1)}, u32[]{:S(2)}, u32[]{:S(2)}) collective-permute-start(bf16[64,256]{1,0:T(8,128)(2,1)S(1)} %get-tuple-element.29), channel_id=1, source_target_pairs={{0,4},{4,0},{8,12},{12,8},{16,20},{20,16},{24,28},{28,24},{1,5},{5... | collective-permute-start | bytes 98312 | tf_op jit(solution)/shard_map/ppermute | solution.py:530
  10.5 1.8 %collective-permute-start.1 = (bf16[64,256]{1,0:T(8,128)(2,1)S(1)}, bf16[64,256]{1,0:T(8,128)(2,1)S(1)}, u32[]{:S(2)}, u32[]{:S(2)}) collective-permute-start(bf16[64,256]{1,0:T(8,128)(2,1)S(1)} %get-tuple-element.30), channel_id=1, source_target_pairs={{4,8},{8,4},{12,16},{16,12},{20,24},{24,20},{5,9},{9,5},{13,17},{1... | collective-permute-start | bytes 98312 | tf_op jit(solution)/shard_map/ppermute | solution.py:529
  12.3 2.6 %copy-start.5 = (s32[3072]{0:T(1024)}, s32[3072]{0:T(1024)S(1)}, u32[]{:S(2)}) copy-start(s32[3072]{0:T(1024)S(1)} %add_dynamic-update-slice_fusion) | copy-start | bytes 36868
  56.8 1.7 %copy-start = (bf16[2560,512]{1,0:T(8,128)(2,1)S(1)}, bf16[2560,512]{1,0:T(8,128)(2,1)}, u32[]{:S(2)}) copy-start(bf16[2560,512]{1,0:T(8,128)(2,1)} %get-tuple-element.15.refs_1_) | copy-start | bytes 7864324
  58.5 1.7 %copy-start.1 = (bf16[2560,512]{1,0:T(8,128)(2,1)S(1)}, bf16[2560,512]{1,0:T(8,128)(2,1)}, u32[]{:S(2)}) copy-start(bf16[2560,512]{1,0:T(8,128)(2,1)} %get-tuple-element.16.refs_2_) | copy-start | bytes 7864324
  60.3 1.3 copy-start.2
  61.6 10.5 %copy-start.3 = (bf16[8,2560,256]{2,1,0:T(8,128)(2,1)S(1)}, bf16[8,2560,256]{2,1,0:T(8,128)(2,1)}, u32[]{:S(2)}) copy-start(bf16[8,2560,256]{2,1,0:T(8,128)(2,1)} %get-tuple-element.18.matrix_ref) | copy-start | bytes 31457284
  63.8 11.5 %collective-permute-start.3 = (bf16[256,512]{1,0:T(8,128)(2,1)S(1)}, bf16[256,512]{1,0:T(8,128)(2,1)S(1)}, u32[]{:S(2)}, u32[]{:S(2)}) collective-permute-start(bf16[256,512]{1,0:T(8,128)(2,1)S(1)} %get-tuple-element.33.refs_1_), channel_id=1, source_target_pairs={{4,8},{8,4},{12,16},{16,12},{20,24},{24,20},{5,9},{9,5},{13,17},{1... | collective-permute-start | bytes 786440 | tf_op jit(solution)/shard_map/ppermute | solution.py:550
  64.6 10.7 %collective-permute-start.2 = (bf16[256,512]{1,0:T(8,128)(2,1)S(1)}, bf16[256,512]{1,0:T(8,128)(2,1)S(1)}, u32[]{:S(2)}, u32[]{:S(2)}) collective-permute-start(bf16[256,512]{1,0:T(8,128)(2,1)S(1)} %get-tuple-element.31.refs_0_), channel_id=1, source_target_pairs={{0,4},{4,0},{8,12},{12,8},{16,20},{20,16},{24,28},{28,24},{1,5},{5... | collective-permute-start | bytes 786440 | tf_op jit(solution)/shard_map/ppermute | solution.py:553
  78.3 7.9 %collective-permute-start.5 = (bf16[256,512]{1,0:T(8,128)(2,1)S(1)}, bf16[256,512]{1,0:T(8,128)(2,1)S(1)}, u32[]{:S(2)}, u32[]{:S(2)}) collective-permute-start(bf16[256,512]{1,0:T(8,128)(2,1)S(1)} %get-tuple-element.37.refs_2_), channel_id=1, source_target_pairs={{4,8},{8,4},{12,16},{16,12},{20,24},{24,20},{5,9},{9,5},{13,17},{1... | collective-permute-start | bytes 786440 | tf_op jit(solution)/shard_map/ppermute | solution.py:550
  79.1 7.1 %collective-permute-start.4 = (bf16[256,512]{1,0:T(8,128)(2,1)S(1)}, bf16[256,512]{1,0:T(8,128)(2,1)S(1)}, u32[]{:S(2)}, u32[]{:S(2)}) collective-permute-start(bf16[256,512]{1,0:T(8,128)(2,1)S(1)} %get-tuple-element.35.refs_1_), channel_id=1, source_target_pairs={{0,4},{4,0},{8,12},{12,8},{16,20},{20,16},{24,28},{28,24},{1,5},{5... | collective-permute-start | bytes 786440 | tf_op jit(solution)/shard_map/ppermute | solution.py:553
  90.1 10.1 %collective-permute-start.7 = (bf16[256,512]{1,0:T(8,128)(2,1)S(1)}, bf16[256,512]{1,0:T(8,128)(2,1)S(1)}, u32[]{:S(2)}, u32[]{:S(2)}) collective-permute-start(bf16[256,512]{1,0:T(8,128)(2,1)S(1)} %get-tuple-element.41.refs_5_), channel_id=1, source_target_pairs={{4,8},{8,4},{12,16},{16,12},{20,24},{24,20},{5,9},{9,5},{13,17},{1... | collective-permute-start | bytes 786440 | tf_op jit(solution)/shard_map/ppermute | solution.py:550
  90.8 9.4 %collective-permute-start.6 = (bf16[256,512]{1,0:T(8,128)(2,1)S(1)}, bf16[256,512]{1,0:T(8,128)(2,1)S(1)}, u32[]{:S(2)}, u32[]{:S(2)}) collective-permute-start(bf16[256,512]{1,0:T(8,128)(2,1)S(1)} %get-tuple-element.39.refs_4_), channel_id=1, source_target_pairs={{0,4},{4,0},{8,12},{12,8},{16,20},{20,16},{24,28},{28,24},{1,5},{5... | collective-permute-start | bytes 786440 | tf_op jit(solution)/shard_map/ppermute | solution.py:553
  103.4 8.9 %collective-permute-start.9 = (bf16[256,256]{1,0:T(8,128)(2,1)S(1)}, bf16[256,256]{1,0:T(8,128)(2,1)S(1)}, u32[]{:S(2)}, u32[]{:S(2)}) collective-permute-start(bf16[256,256]{1,0:T(8,128)(2,1)S(1)} %fusion.10.refs_5_), channel_id=1, source_target_pairs={{4,8},{8,4},{12,16},{16,12},{20,24},{24,20},{5,9},{9,5},{13,17},{1... | collective-permute-start | bytes 393224 | tf_op jit(solution)/shard_map/ppermute | solution.py:550
  104.0 8.3 %collective-permute-start.8 = (bf16[256,256]{1,0:T(8,128)(2,1)S(1)}, bf16[256,256]{1,0:T(8,128)(2,1)S(1)}, u32[]{:S(2)}, u32[]{:S(2)}) collective-permute-start(bf16[256,256]{1,0:T(8,128)(2,1)S(1)} %fusion.7.refs_4_), channel_id=1, source_target_pairs={{0,4},{4,0},{8,12},{12,8},{16,20},{20,16},{24,28},{28,24},{1,5},{5... | collective-permute-start | bytes 393224 | tf_op jit(solution)/shard_map/ppermute | solution.py:553
  114.0 1.4 collective-permute-start.10
  115.5 7.5 %collective-permute-start.11 = (bf16[256,256]{1,0:T(8,128)(2,1)S(1)}, bf16[256,256]{1,0:T(8,128)(2,1)S(1)}, u32[]{:S(2)}, u32[]{:S(2)}) collective-permute-start(bf16[256,256]{1,0:T(8,128)(2,1)S(1)} %add_convert_fusion.1), channel_id=1, source_target_pairs={{0,8},{4,12},{8,0},{12,4},{16,24},{20,28},{24,16},{28,20},{1,9},{5... | collective-permute-start | bytes 393224 | tf_op jit(solution)/shard_map/ppermute | solution.py:473
  123.0 5.3 %collective-permute-start.12 = (bf16[256,256]{1,0:T(8,128)(2,1)S(1)}, bf16[256,256]{1,0:T(8,128)(2,1)S(1)}, u32[]{:S(2)}, u32[]{:S(2)}) collective-permute-start(bf16[256,256]{1,0:T(8,128)(2,1)S(1)} %add_convert_fusion), channel_id=1, source_target_pairs={{0,16},{4,20},{8,24},{12,28},{16,0},{20,4},{24,8},{28,12},{1,17},{... | collective-permute-start | bytes 393224 | tf_op jit(solution)/shard_map/ppermute | solution.py:473
Sparse Core Ops, SparseCore 0:
  13.3 38.4 all-gather.1

commit v8 on v5

--- a/solution.py
+++ b/solution.py
@@ -216,16 +216,25 @@
     )
 
 
-def hold_kernel(in_ref, out_ref):
-    out_ref[...] = in_ref[...]
-
-
-def hold(values):
+def hold_kernel(*refs):
+    count = len(refs) // 2
+    done = refs[-1]
+    copies = [pltpu.make_async_copy(refs[i], refs[count + i], done.at[i]) for i in range(count)]
+    for copy in copies:
+        copy.start()
+    for copy in copies:
+        copy.wait()
+
+
+def hold(*arrays):
     return pl.pallas_call(
         hold_kernel,
-        out_shape=jax.ShapeDtypeStruct(values.shape, values.dtype),
+        out_shape=tuple(jax.ShapeDtypeStruct(x.shape, x.dtype) for x in arrays),
+        in_specs=[pl.BlockSpec(memory_space=pl.ANY)] * len(arrays),
+        out_specs=(pl.BlockSpec(memory_space=pltpu.VMEM),) * len(arrays),
+        scratch_shapes=[pltpu.SemaphoreType.DMA((len(arrays),))],
         compiler_params=pltpu.CompilerParams(vmem_limit_bytes=16 * 1024 * 1024),
-    )(values)
+    )(*arrays)
 
 
 def arrived(got_a_ref, got_b_ref, table_ref, at):
@@ -249,7 +258,7 @@
         out_ref[:, at] = product
         return carry
 
-    lax.fori_loop(0, matrix_ref.shape[0], body, 0)
+    lax.fori_loop(0, matrix_ref.shape[0], body, 0, unroll=4)
 
 
 def own_part(step, extended, matrix, before, after):
@@ -501,7 +510,7 @@
     )
 
     there = jnp.stack([has_a, has_b]).astype(jnp.int32)
-    field = hold(gathered)
+    field, matrix_b, matrix_a = hold(gathered, matrix_b, matrix_a)
     ghosts = [field[:, own_count:]]
     before = ()
     for step in range(DEGREE):

time: 148 us -> 146 us (0.986)
  matrix products: 11.7 us -> 7.44 us
  Pallas kernels: 76.4 us -> 72.8 us
  starting transfers between devices: 28.1 us -> 31.4 us
  local copies, waits for them, and re-layouts: 4.38 us -> 6.53 us
    dot_general x8, matrix products: 10.3 us -> 6.03 us  [times(): return jnp.dot(left, right, preferred_element_type=jnp.float32)]
    pallas_call x4, Pallas kernels: 17.5 us -> 13.5 us  [own_part(): pl.pallas_call(functools.partial(own_kernel, step), out_shape=jax.ShapeDt...]
    unnamed x13, local copies, waits for them, and re-layouts: 2.63 us -> 4.81 us
    ppermute x4, starting transfers between devices: 19.8 us -> 21.6 us  [per_device(): got_a = lax.ppermute(sent_a, 'slab', pairs_a)]
  transfers between devices with their start and end apart: 14 -> 14, of which waited for: 3 -> 3; matrix products, arithmetic and copies ran while one was open for 2% -> 2% of each run, Pallas kernels for 40% -> 38%
where the time goes in v8:
time: 146 us; the launch traced here: 145 us
  Pallas kernels  72.8 us (50%)
  starting transfers between devices  31.4 us (22%)
  between operations  13.8 us (9%)
  waiting for transfers between devices  8.6 us (6%)
  matrix products  7.44 us (5%)
  local copies, waits for them, and re-layouts  6.53 us (4%)
  other arithmetic  4.43 us (3%)
    pallas_call x1, Pallas kernels, assemble(): pl.pallas_call(assemble_kernel, out_shape=(half, half, jax.ShapeDtypeStru...  41.8 us
    ppermute x4, starting transfers between devices, per_device(): got_a = lax.ppermute(sent_a, 'slab', pairs_a)  21.6 us
    pallas_call x4, Pallas kernels, own_part(): pl.pallas_call(functools.partial(own_kernel, step), out_shape=jax.ShapeDt...  13.5 us
    pallas_call x1, Pallas kernels, orthonormal(): pl.pallas_call(functools.partial(orthonormal_kernel, scale), out_shape=ja...  10.1 us
    ppermute x3, waiting for transfers between devices, sum_over(): got = lax.ppermute(sent, axis, [(i, i ^ step) for i in range(count)])  8.54 us
    pallas_call x4, Pallas kernels, combine(): pl.pallas_call(functools.partial(combine_kernel, step), out_shape=out_sha...  6.94 us
    dot_general x8, matrix products, times(): return jnp.dot(left, right, preferred_element_type=jnp.float32)  6.03 us
    ppermute x3, starting transfers between devices, sum_over(): got = lax.ppermute(sent, axis, [(i, i ^ step) for i in range(count)])  5.39 us
  transfers between devices with their start and end apart: 14, of which 3 were waited for; matrix products, arithmetic and copies ran while one was open for 2% of the time, Pallas kernels for 38%

profile of v8, /device:TPU:0, one launch (start us, length us, event | category | flops | bytes accessed | tf_op | source)
XLA Modules:
  0.0 145.0 jit_solution(1162733264120192212)
XLA Ops:
  7.9 1.1 convert_element_type.67
  9.0 0.9 fusion.14
  13.1 1.7 %broadcast_in_dim.5.nodes_ref = s32[8,512,128]{2,1,0:T(8,128)} broadcast(s32[8,512]{1,0:T(8,128)S(1)} %copy-done.4), dimensions={0,1} | broadcast | bytes 2113536 | tf_op jit(solution)/shard_map/broadcast_in_dim | solution.py:482
  14.8 41.8 %shard_map.55 = (bf16[2560,512]{1,0:T(8,128)(2,1)}, bf16[2560,512]{1,0:T(8,128)(2,1)}, bf16[8,2560,256]{2,1,0:T(8,128)(2,1)}) custom-call(s32[8192]{0:T(1024)} %pad_add_fusion.places_ref, s32[1,3072]{1,0:T(1,128)} %bitcast.28, s32[8,512,128]{2,1,0:T(8,128)} %broadcast_in_dim.5.nodes_ref, bf16[8,512,512]{2,1,0:T(8,128)(2,1)} %cell_ref.1, ...), custom_call_target="tpu_custom_call" | custom-call | flops 103079215104 | bytes 28311552 | tf_op jit(solution)/shard_map/pallas_call | solution.py:179
  56.7 1.7 %copy-done = bf16[2560,512]{1,0:T(8,128)(2,1)S(1)} copy-done((bf16[2560,512]{1,0:T(8,128)(2,1)S(1)}, bf16[2560,512]{1,0:T(8,128)(2,1)}, u32[]{:S(2)}) %copy-start) | copy-done | bytes 2621464
  58.4 1.7 %copy-done.1 = bf16[2560,512]{1,0:T(8,128)(2,1)S(1)} copy-done((bf16[2560,512]{1,0:T(8,128)(2,1)S(1)}, bf16[2560,512]{1,0:T(8,128)(2,1)}, u32[]{:S(2)}) %copy-start.1) | copy-done | bytes 2621464
  60.2 1.3 copy-done.2
  62.0 0.8 fusion.17
  62.8 0.8 fusion.16
  64.5 7.4 %collective-permute-start.2 = (bf16[256,512]{1,0:T(8,128)(2,1)S(1)}, bf16[256,512]{1,0:T(8,128)(2,1)S(1)}, u32[]{:S(2)}, u32[]{:S(2)}) collective-permute-start(bf16[256,512]{1,0:T(8,128)(2,1)S(1)} %get-tuple-element.31.refs_0_), channel_id=1, source_target_pairs={{0,4},{4,0},{8,12},{12,8},{16,20},{20,16},{24,28},{28,24},{1,5},{5... | collective-permute-start | bytes 786440 | tf_op jit(solution)/shard_map/ppermute | solution.py:523
  71.9 3.1 %shard_map.57.own_ref.refs_0_ = f32[256,2048]{1,0:T(8,128)S(1)} custom-call(bf16[256,2560]{1,0:T(8,128)(2,1)S(1)} %get-tuple-element.17.extended_ref.refs_0_, bf16[8,2560,256]{2,1,0:T(8,128)(2,1)S(1)} %copy-done.3, bf16[256,512]{1,0:T(8,128)(2,1)S(1)} %get-tuple-element.31.refs_0_, bf16[256,512]{1,0:T(8,128)(2,1)S(1)} %get-tuple-element.33.refs_1_), custom_call_target="tpu_custom_call" | custom-call | flops 10737418240 | bytes 12582912 | tf_op jit(solution)/shard_map/pallas_call | solution.py:270
  75.0 1.3 shard_map.58
  76.4 0.8 fusion.19
  77.2 0.8 fusion.18
  78.1 0.9 collective-permute-start.5
  78.9 3.9 %collective-permute-start.4 = (bf16[256,512]{1,0:T(8,128)(2,1)S(1)}, bf16[256,512]{1,0:T(8,128)(2,1)S(1)}, u32[]{:S(2)}, u32[]{:S(2)}) collective-permute-start(bf16[256,512]{1,0:T(8,128)(2,1)S(1)} %get-tuple-element.35.refs_1_), channel_id=1, source_target_pairs={{0,4},{4,0},{8,12},{12,8},{16,20},{20,16},{24,28},{28,24},{1,5},{5... | collective-permute-start | bytes 786440 | tf_op jit(solution)/shard_map/ppermute | solution.py:523
  82.8 3.2 %shard_map.59.own_ref.refs_0_ = f32[256,2048]{1,0:T(8,128)S(1)} custom-call(bf16[256,2560]{1,0:T(8,128)(2,1)S(1)} %get-tuple-element.21.extended_ref, bf16[8,2560,256]{2,1,0:T(8,128)(2,1)S(1)} %copy-done.3, bf16[256,2560]{1,0:T(8,128)(2,1)S(1)} %get-tuple-element.17.extended_ref.refs_0_, bf16[256,512]{1,0:T(8,128)(2,1)S(1)} %get-tuple-element.35.refs_1_, ...), custom_call_target="tpu_custom_call" | custom-call | flops 10737418240 | bytes 12582912 | tf_op jit(solution)/shard_map/pallas_call | solution.py:270
  86.0 2.2 %shard_map.60 = (bf16[256,2560]{1,0:T(8,128)(2,1)S(1)}, f32[256,512]{1,0:T(8,128)}) custom-call(s32[2]{0:T(128)S(1)} %add_convert_fusion.2.there_ref, f32[256,2048]{1,0:T(8,128)S(1)} %shard_map.59.own_ref.refs_0_, bf16[256,512]{1,0:T(8,128)(2,1)S(1)} %collective-permute-done.4.got_a_ref.refs_1_, ...), custom_call_target="tpu_custom_call" | custom-call | tf_op jit(solution)/shard_map/pallas_call | solution.py:317
  89.0 0.8 fusion.20
  90.6 5.7 %collective-permute-start.6 = (bf16[256,512]{1,0:T(8,128)(2,1)S(1)}, bf16[256,512]{1,0:T(8,128)(2,1)S(1)}, u32[]{:S(2)}, u32[]{:S(2)}) collective-permute-start(bf16[256,512]{1,0:T(8,128)(2,1)S(1)} %get-tuple-element.39.refs_4_), channel_id=1, source_target_pairs={{0,4},{4,0},{8,12},{12,8},{16,20},{20,16},{24,28},{28,24},{1,5},{5... | collective-permute-start | bytes 786440 | tf_op jit(solution)/shard_map/ppermute | solution.py:523
  96.3 3.7 %shard_map.61.own_ref = f32[256,2048]{1,0:T(8,128)S(1)} custom-call(bf16[256,2560]{1,0:T(8,128)(2,1)S(1)} %get-tuple-element.22.extended_ref, bf16[8,2560,256]{2,1,0:T(8,128)(2,1)S(1)} %copy-done.3, f32[256,2048]{1,0:T(8,128)S(1)} %shard_map.57.own_ref.refs_0_, bf16[256,512]{1,0:T(8,128)(2,1)S(1)} %collective-permute-done.2.got_a_ref.refs_1_, ...), custom_call_target="tpu_custom_call" | custom-call | flops 10737418240 | bytes 12582912 | tf_op jit(solution)/shard_map/pallas_call | solution.py:270
  99.9 2.2 %shard_map.62 = (bf16[256,2560]{1,0:T(8,128)(2,1)S(1)}, f32[256,512]{1,0:T(8,128)}) custom-call(s32[2]{0:T(128)S(1)} %add_convert_fusion.2.there_ref, f32[256,2048]{1,0:T(8,128)S(1)} %shard_map.61.own_ref, bf16[256,512]{1,0:T(8,128)(2,1)S(1)} %collective-permute-done.6.got_a_ref, bf16[256,512]{1,0:T(8,128)(2,1)S(1)} %collective-permute-done.7.got_b_ref, ...), custom_call_target="tpu_custom_call" | custom-call | tf_op jit(solution)/shard_map/pallas_call | solution.py:317
  103.1 0.9 collective-permute-start.9
  104.0 4.6 %collective-permute-start.8 = (bf16[256,256]{1,0:T(8,128)(2,1)S(1)}, bf16[256,256]{1,0:T(8,128)(2,1)S(1)}, u32[]{:S(2)}, u32[]{:S(2)}) collective-permute-start(bf16[256,256]{1,0:T(8,128)(2,1)S(1)} %fusion.7.refs_4_), channel_id=1, source_target_pairs={{0,4},{4,0},{8,12},{12,8},{16,20},{20,16},{24,28},{28,24},{1,5},{5... | collective-permute-start | bytes 393224 | tf_op jit(solution)/shard_map/ppermute | solution.py:523
  108.6 3.6 %shard_map.63.own_ref = f32[256,2048]{1,0:T(8,128)S(1)} custom-call(bf16[256,2560]{1,0:T(8,128)(2,1)S(1)} %get-tuple-element.24.extended_ref, bf16[8,2560,256]{2,1,0:T(8,128)(2,1)S(1)} %copy-done.3, f32[256,2048]{1,0:T(8,128)S(1)} %shard_map.59.own_ref.refs_0_, bf16[256,512]{1,0:T(8,128)(2,1)S(1)} %collective-permute-done.4.got_a_ref.refs_1_, ...), custom_call_target="tpu_custom_call" | custom-call | flops 10737418240 | bytes 12582912 | tf_op jit(solution)/shard_map/pallas_call | solution.py:270
  112.3 1.3 shard_map.64.filtered_ref
  114.1 1.3 collective-permute-done.10
  115.5 3.2 %collective-permute-start.11 = (bf16[256,256]{1,0:T(8,128)(2,1)S(1)}, bf16[256,256]{1,0:T(8,128)(2,1)S(1)}, u32[]{:S(2)}, u32[]{:S(2)}) collective-permute-start(bf16[256,256]{1,0:T(8,128)(2,1)S(1)} %add_convert_fusion.1), channel_id=1, source_target_pairs={{0,8},{4,12},{8,0},{12,4},{16,24},{20,28},{24,16},{28,20},{1,9},{5... | collective-permute-start | bytes 393224 | tf_op jit(solution)/shard_map/ppermute | solution.py:443
  118.7 4.0 %collective-permute-done.11 = bf16[256,256]{1,0:T(8,128)(2,1)S(1)} collective-permute-done((bf16[256,256]{1,0:T(8,128)(2,1)S(1)}, bf16[256,256]{1,0:T(8,128)(2,1)S(1)}, u32[]{:S(2)}, u32[]{:S(2)}) %collective-permute-start.11) | collective-permute-done | bytes 131104 | tf_op jit(solution)/shard_map/ppermute | solution.py:443
  122.8 2.1 %collective-permute-start.12 = (bf16[256,256]{1,0:T(8,128)(2,1)S(1)}, bf16[256,256]{1,0:T(8,128)(2,1)S(1)}, u32[]{:S(2)}, u32[]{:S(2)}) collective-permute-start(bf16[256,256]{1,0:T(8,128)(2,1)S(1)} %add_convert_fusion), channel_id=1, source_target_pairs={{0,16},{4,20},{8,24},{12,28},{16,0},{20,4},{24,8},{28,12},{1,17},{... | collective-permute-start | bytes 393224 | tf_op jit(solution)/shard_map/ppermute | solution.py:443
  124.8 3.2 %collective-permute-done.12 = bf16[256,256]{1,0:T(8,128)(2,1)S(1)} collective-permute-done((bf16[256,256]{1,0:T(8,128)(2,1)S(1)}, bf16[256,256]{1,0:T(8,128)(2,1)S(1)}, u32[]{:S(2)}, u32[]{:S(2)}) %collective-permute-start.12) | collective-permute-done | bytes 131104 | tf_op jit(solution)/shard_map/ppermute | solution.py:443
  128.1 10.1 %shard_map.65 = f32[64,2048]{1,0:T(8,128)} custom-call(s32[1]{0:T(128)} %bitcast.block_ref, f32[256,256]{1,0:T(8,128)S(1)} %convert_add_fusion.gram_ref, bf16[256,2048]{1,0:T(8,128)(2,1)S(1)} %shard_map.64.filtered_ref), custom_call_target="tpu_custom_call" | custom-call | tf_op jit(solution)/shard_map/pallas_call | solution.py:415
  (51 shorter events, 9.0 us)
Async XLA Ops:
  6.5 50.2 %all-gather.2.cloned.1.call-start = ((), (), s32[]{:S(2)}) async-start(), calls=%async_computation | async-start | bytes 1638400 | tf_op jit(solution)/shard_map/all_gather | solution.py:502
  9.0 2.6 %copy-start.4 = (s32[8,512]{1,0:T(8,128)S(1)}, s32[8,512]{1,0:T(8,128)}, u32[]{:S(2)}) copy-start(s32[8,512]{1,0:T(8,128)} %param.7) | copy-start | bytes 49156
  10.0 2.4 %collective-permute-start = (bf16[64,256]{1,0:T(8,128)(2,1)S(1)}, bf16[64,256]{1,0:T(8,128)(2,1)S(1)}, u32[]{:S(2)}, u32[]{:S(2)}) collective-permute-start(bf16[64,256]{1,0:T(8,128)(2,1)S(1)} %get-tuple-element.29), channel_id=1, source_target_pairs={{0,4},{4,0},{8,12},{12,8},{16,20},{20,16},{24,28},{28,24},{1,5},{5... | collective-permute-start | bytes 98312 | tf_op jit(solution)/shard_map/ppermute | solution.py:500
  10.5 1.8 %collective-permute-start.1 = (bf16[64,256]{1,0:T(8,128)(2,1)S(1)}, bf16[64,256]{1,0:T(8,128)(2,1)S(1)}, u32[]{:S(2)}, u32[]{:S(2)}) collective-permute-start(bf16[64,256]{1,0:T(8,128)(2,1)S(1)} %get-tuple-element.30), channel_id=1, source_target_pairs={{4,8},{8,4},{12,16},{16,12},{20,24},{24,20},{5,9},{9,5},{13,17},{1... | collective-permute-start | bytes 98312 | tf_op jit(solution)/shard_map/ppermute | solution.py:499
  12.3 2.6 %copy-start.5 = (s32[3072]{0:T(1024)}, s32[3072]{0:T(1024)S(1)}, u32[]{:S(2)}) copy-start(s32[3072]{0:T(1024)S(1)} %add_dynamic-update-slice_fusion) | copy-start | bytes 36868
  56.7 1.7 %copy-start = (bf16[2560,512]{1,0:T(8,128)(2,1)S(1)}, bf16[2560,512]{1,0:T(8,128)(2,1)}, u32[]{:S(2)}) copy-start(bf16[2560,512]{1,0:T(8,128)(2,1)} %get-tuple-element.15.refs_1_) | copy-start | bytes 7864324
  58.4 1.7 %copy-start.1 = (bf16[2560,512]{1,0:T(8,128)(2,1)S(1)}, bf16[2560,512]{1,0:T(8,128)(2,1)}, u32[]{:S(2)}) copy-start(bf16[2560,512]{1,0:T(8,128)(2,1)} %get-tuple-element.16.refs_2_) | copy-start | bytes 7864324
  60.2 1.3 copy-start.2
  61.5 10.4 %copy-start.3 = (bf16[8,2560,256]{2,1,0:T(8,128)(2,1)S(1)}, bf16[8,2560,256]{2,1,0:T(8,128)(2,1)}, u32[]{:S(2)}) copy-start(bf16[8,2560,256]{2,1,0:T(8,128)(2,1)} %get-tuple-element.18.matrix_ref) | copy-start | bytes 31457284
  63.7 11.4 %collective-permute-start.3 = (bf16[256,512]{1,0:T(8,128)(2,1)S(1)}, bf16[256,512]{1,0:T(8,128)(2,1)S(1)}, u32[]{:S(2)}, u32[]{:S(2)}) collective-permute-start(bf16[256,512]{1,0:T(8,128)(2,1)S(1)} %get-tuple-element.33.refs_1_), channel_id=1, source_target_pairs={{4,8},{8,4},{12,16},{16,12},{20,24},{24,20},{5,9},{9,5},{13,17},{1... | collective-permute-start | bytes 786440 | tf_op jit(solution)/shard_map/ppermute | solution.py:520
  64.5 10.6 %collective-permute-start.2 = (bf16[256,512]{1,0:T(8,128)(2,1)S(1)}, bf16[256,512]{1,0:T(8,128)(2,1)S(1)}, u32[]{:S(2)}, u32[]{:S(2)}) collective-permute-start(bf16[256,512]{1,0:T(8,128)(2,1)S(1)} %get-tuple-element.31.refs_0_), channel_id=1, source_target_pairs={{0,4},{4,0},{8,12},{12,8},{16,20},{20,16},{24,28},{28,24},{1,5},{5... | collective-permute-start | bytes 786440 | tf_op jit(solution)/shard_map/ppermute | solution.py:523
  78.1 7.9 %collective-permute-start.5 = (bf16[256,512]{1,0:T(8,128)(2,1)S(1)}, bf16[256,512]{1,0:T(8,128)(2,1)S(1)}, u32[]{:S(2)}, u32[]{:S(2)}) collective-permute-start(bf16[256,512]{1,0:T(8,128)(2,1)S(1)} %get-tuple-element.37.refs_2_), channel_id=1, source_target_pairs={{4,8},{8,4},{12,16},{16,12},{20,24},{24,20},{5,9},{9,5},{13,17},{1... | collective-permute-start | bytes 786440 | tf_op jit(solution)/shard_map/ppermute | solution.py:520
  78.9 7.1 %collective-permute-start.4 = (bf16[256,512]{1,0:T(8,128)(2,1)S(1)}, bf16[256,512]{1,0:T(8,128)(2,1)S(1)}, u32[]{:S(2)}, u32[]{:S(2)}) collective-permute-start(bf16[256,512]{1,0:T(8,128)(2,1)S(1)} %get-tuple-element.35.refs_1_), channel_id=1, source_target_pairs={{0,4},{4,0},{8,12},{12,8},{16,20},{20,16},{24,28},{28,24},{1,5},{5... | collective-permute-start | bytes 786440 | tf_op jit(solution)/shard_map/ppermute | solution.py:523
  89.9 10.1 %collective-permute-start.7 = (bf16[256,512]{1,0:T(8,128)(2,1)S(1)}, bf16[256,512]{1,0:T(8,128)(2,1)S(1)}, u32[]{:S(2)}, u32[]{:S(2)}) collective-permute-start(bf16[256,512]{1,0:T(8,128)(2,1)S(1)} %get-tuple-element.41.refs_5_), channel_id=1, source_target_pairs={{4,8},{8,4},{12,16},{16,12},{20,24},{24,20},{5,9},{9,5},{13,17},{1... | collective-permute-start | bytes 786440 | tf_op jit(solution)/shard_map/ppermute | solution.py:520
  90.6 9.4 %collective-permute-start.6 = (bf16[256,512]{1,0:T(8,128)(2,1)S(1)}, bf16[256,512]{1,0:T(8,128)(2,1)S(1)}, u32[]{:S(2)}, u32[]{:S(2)}) collective-permute-start(bf16[256,512]{1,0:T(8,128)(2,1)S(1)} %get-tuple-element.39.refs_4_), channel_id=1, source_target_pairs={{0,4},{4,0},{8,12},{12,8},{16,20},{20,16},{24,28},{28,24},{1,5},{5... | collective-permute-start | bytes 786440 | tf_op jit(solution)/shard_map/ppermute | solution.py:523
  103.1 9.1 %collective-permute-start.9 = (bf16[256,256]{1,0:T(8,128)(2,1)S(1)}, bf16[256,256]{1,0:T(8,128)(2,1)S(1)}, u32[]{:S(2)}, u32[]{:S(2)}) collective-permute-start(bf16[256,256]{1,0:T(8,128)(2,1)S(1)} %fusion.10.refs_5_), channel_id=1, source_target_pairs={{4,8},{8,4},{12,16},{16,12},{20,24},{24,20},{5,9},{9,5},{13,17},{1... | collective-permute-start | bytes 393224 | tf_op jit(solution)/shard_map/ppermute | solution.py:520
  104.0 8.3 %collective-permute-start.8 = (bf16[256,256]{1,0:T(8,128)(2,1)S(1)}, bf16[256,256]{1,0:T(8,128)(2,1)S(1)}, u32[]{:S(2)}, u32[]{:S(2)}) collective-permute-start(bf16[256,256]{1,0:T(8,128)(2,1)S(1)} %fusion.7.refs_4_), channel_id=1, source_target_pairs={{0,4},{4,0},{8,12},{12,8},{16,20},{20,16},{24,28},{28,24},{1,5},{5... | collective-permute-start | bytes 393224 | tf_op jit(solution)/shard_map/ppermute | solution.py:523
  114.0 1.4 collective-permute-start.10
  115.5 7.2 %collective-permute-start.11 = (bf16[256,256]{1,0:T(8,128)(2,1)S(1)}, bf16[256,256]{1,0:T(8,128)(2,1)S(1)}, u32[]{:S(2)}, u32[]{:S(2)}) collective-permute-start(bf16[256,256]{1,0:T(8,128)(2,1)S(1)} %add_convert_fusion.1), channel_id=1, source_target_pairs={{0,8},{4,12},{8,0},{12,4},{16,24},{20,28},{24,16},{28,20},{1,9},{5... | collective-permute-start | bytes 393224 | tf_op jit(solution)/shard_map/ppermute | solution.py:443
  122.8 5.3 %collective-permute-start.12 = (bf16[256,256]{1,0:T(8,128)(2,1)S(1)}, bf16[256,256]{1,0:T(8,128)(2,1)S(1)}, u32[]{:S(2)}, u32[]{:S(2)}) collective-permute-start(bf16[256,256]{1,0:T(8,128)(2,1)S(1)} %add_convert_fusion), channel_id=1, source_target_pairs={{0,16},{4,20},{8,24},{12,28},{16,0},{20,4},{24,8},{28,12},{1,17},{... | collective-permute-start | bytes 393224 | tf_op jit(solution)/shard_map/ppermute | solution.py:443
Sparse Core Ops, SparseCore 0:
  13.3 38.3 all-gather.1

commit v9 on v8

--- a/solution.py
+++ b/solution.py
@@ -194,9 +194,9 @@
             ],
             out_specs=(pl.BlockSpec(memory_space=pl.ANY),) * 3,
             scratch_shapes=[
-                pltpu.VMEM((2 * ext_count * PITCH, LANES), jnp.float32),
-                pltpu.VMEM((cell_nodes * PITCH, LANES), jnp.float32),
-                pltpu.VMEM((cell_nodes * PITCH, LANES), jnp.float32),
+                pltpu.VMEM(((2 * ext_count + SUBLANES) * PITCH, LANES), jnp.float32),
+                pltpu.VMEM(((cell_nodes + SUBLANES) * PITCH, LANES), jnp.float32),
+                pltpu.VMEM(((cell_nodes + SUBLANES) * PITCH, LANES), jnp.float32),
                 pltpu.VMEM((CHUNK // TILE, ext_count, TILE), jnp.bfloat16),
                 pltpu.SemaphoreType.DMA((cells, CHUNK // TILE)),
             ],
@@ -258,7 +258,7 @@
         out_ref[:, at] = product
         return carry
 
-    lax.fori_loop(0, matrix_ref.shape[0], body, 0, unroll=4)
+    lax.fori_loop(0, matrix_ref.shape[0], body, 0, unroll=8)
 
 
 def own_part(step, extended, matrix, before, after):

time: 146 us -> 146 us (level)
  no operation moved by 1% of the time
where the time goes in v9:
time: 146 us; the launch traced here: 145 us
  Pallas kernels  72.1 us (49%)
  starting transfers between devices  32.1 us (22%)
  between operations  13.8 us (9%)
  waiting for transfers between devices  8.82 us (6%)
  matrix products  7.45 us (5%)
  local copies, waits for them, and re-layouts  6.53 us (4%)
  other arithmetic  4.43 us (3%)
    pallas_call x1, Pallas kernels, assemble(): pl.pallas_call(assemble_kernel, out_shape=(half, half, jax.ShapeDtypeStru...  42 us
    ppermute x4, starting transfers between devices, per_device(): got_a = lax.ppermute(sent_a, 'slab', pairs_a)  22.2 us
    pallas_call x4, Pallas kernels, own_part(): pl.pallas_call(functools.partial(own_kernel, step), out_shape=jax.ShapeDt...  12.6 us
    pallas_call x1, Pallas kernels, orthonormal(): pl.pallas_call(functools.partial(orthonormal_kernel, scale), out_shape=ja...  10.1 us
    ppermute x3, waiting for transfers between devices, sum_over(): got = lax.ppermute(sent, axis, [(i, i ^ step) for i in range(count)])  8.75 us
    pallas_call x4, Pallas kernels, combine(): pl.pallas_call(functools.partial(combine_kernel, step), out_shape=out_sha...  6.94 us
    dot_general x8, matrix products, times(): return jnp.dot(left, right, preferred_element_type=jnp.float32)  6.03 us
    ppermute x3, starting transfers between devices, sum_over(): got = lax.ppermute(sent, axis, [(i, i ^ step) for i in range(count)])  5.49 us
  transfers between devices with their start and end apart: 14, of which 3 were waited for; matrix products, arithmetic and copies ran while one was open for 2% of the time, Pallas kernels for 38%

profile of v9, /device:TPU:0, one launch (start us, length us, event | category | flops | bytes accessed | tf_op | source)
XLA Modules:
  0.0 145.2 jit_solution(1707878994319997477)
XLA Ops:
  7.9 1.1 convert_element_type.67
  9.0 0.9 fusion.14
  13.1 1.7 %broadcast_in_dim.5.nodes_ref = s32[8,512,128]{2,1,0:T(8,128)} broadcast(s32[8,512]{1,0:T(8,128)S(1)} %copy-done.4), dimensions={0,1} | broadcast | bytes 2113536 | tf_op jit(solution)/shard_map/broadcast_in_dim | solution.py:482
  14.8 42.0 %shard_map.55 = (bf16[2560,512]{1,0:T(8,128)(2,1)}, bf16[2560,512]{1,0:T(8,128)(2,1)}, bf16[8,2560,256]{2,1,0:T(8,128)(2,1)}) custom-call(s32[8192]{0:T(1024)} %pad_add_fusion.places_ref, s32[1,3072]{1,0:T(1,128)} %bitcast.28, s32[8,512,128]{2,1,0:T(8,128)} %broadcast_in_dim.5.nodes_ref, bf16[8,512,512]{2,1,0:T(8,128)(2,1)} %cell_ref.1, ...), custom_call_target="tpu_custom_call" | custom-call | flops 103079215104 | bytes 28311552 | tf_op jit(solution)/shard_map/pallas_call | solution.py:179
  56.9 1.7 %copy-done = bf16[2560,512]{1,0:T(8,128)(2,1)S(1)} copy-done((bf16[2560,512]{1,0:T(8,128)(2,1)S(1)}, bf16[2560,512]{1,0:T(8,128)(2,1)}, u32[]{:S(2)}) %copy-start) | copy-done | bytes 2621464
  58.6 1.7 %copy-done.1 = bf16[2560,512]{1,0:T(8,128)(2,1)S(1)} copy-done((bf16[2560,512]{1,0:T(8,128)(2,1)S(1)}, bf16[2560,512]{1,0:T(8,128)(2,1)}, u32[]{:S(2)}) %copy-start.1) | copy-done | bytes 2621464
  60.4 1.3 copy-done.2
  62.2 0.8 fusion.17
  63.0 0.8 fusion.16
  64.7 7.5 %collective-permute-start.2 = (bf16[256,512]{1,0:T(8,128)(2,1)S(1)}, bf16[256,512]{1,0:T(8,128)(2,1)S(1)}, u32[]{:S(2)}, u32[]{:S(2)}) collective-permute-start(bf16[256,512]{1,0:T(8,128)(2,1)S(1)} %get-tuple-element.31.refs_0_), channel_id=1, source_target_pairs={{0,4},{4,0},{8,12},{12,8},{16,20},{20,16},{24,28},{28,24},{1,5},{5... | collective-permute-start | bytes 786440 | tf_op jit(solution)/shard_map/ppermute | solution.py:523
  72.1 2.9 %shard_map.57.own_ref.refs_0_ = f32[256,2048]{1,0:T(8,128)S(1)} custom-call(bf16[256,2560]{1,0:T(8,128)(2,1)S(1)} %get-tuple-element.17.extended_ref.refs_0_, bf16[8,2560,256]{2,1,0:T(8,128)(2,1)S(1)} %copy-done.3, bf16[256,512]{1,0:T(8,128)(2,1)S(1)} %get-tuple-element.31.refs_0_, bf16[256,512]{1,0:T(8,128)(2,1)S(1)} %get-tuple-element.33.refs_1_), custom_call_target="tpu_custom_call" | custom-call | flops 10737418240 | bytes 12582912 | tf_op jit(solution)/shard_map/pallas_call | solution.py:270
  75.1 1.3 shard_map.58
  76.4 0.8 fusion.19
  77.2 0.8 fusion.18
  78.1 0.9 collective-permute-start.5
  78.9 4.1 %collective-permute-start.4 = (bf16[256,512]{1,0:T(8,128)(2,1)S(1)}, bf16[256,512]{1,0:T(8,128)(2,1)S(1)}, u32[]{:S(2)}, u32[]{:S(2)}) collective-permute-start(bf16[256,512]{1,0:T(8,128)(2,1)S(1)} %get-tuple-element.35.refs_1_), channel_id=1, source_target_pairs={{0,4},{4,0},{8,12},{12,8},{16,20},{20,16},{24,28},{28,24},{1,5},{5... | collective-permute-start | bytes 786440 | tf_op jit(solution)/shard_map/ppermute | solution.py:523
  83.0 2.9 %shard_map.59.own_ref.refs_0_ = f32[256,2048]{1,0:T(8,128)S(1)} custom-call(bf16[256,2560]{1,0:T(8,128)(2,1)S(1)} %get-tuple-element.21.extended_ref, bf16[8,2560,256]{2,1,0:T(8,128)(2,1)S(1)} %copy-done.3, bf16[256,2560]{1,0:T(8,128)(2,1)S(1)} %get-tuple-element.17.extended_ref.refs_0_, bf16[256,512]{1,0:T(8,128)(2,1)S(1)} %get-tuple-element.35.refs_1_, ...), custom_call_target="tpu_custom_call" | custom-call | flops 10737418240 | bytes 12582912 | tf_op jit(solution)/shard_map/pallas_call | solution.py:270
  85.9 2.2 %shard_map.60 = (bf16[256,2560]{1,0:T(8,128)(2,1)S(1)}, f32[256,512]{1,0:T(8,128)}) custom-call(s32[2]{0:T(128)S(1)} %add_convert_fusion.2.there_ref, f32[256,2048]{1,0:T(8,128)S(1)} %shard_map.59.own_ref.refs_0_, bf16[256,512]{1,0:T(8,128)(2,1)S(1)} %collective-permute-done.4.got_a_ref.refs_1_, ...), custom_call_target="tpu_custom_call" | custom-call | tf_op jit(solution)/shard_map/pallas_call | solution.py:317
  89.0 0.8 fusion.20
  90.5 5.7 %collective-permute-start.6 = (bf16[256,512]{1,0:T(8,128)(2,1)S(1)}, bf16[256,512]{1,0:T(8,128)(2,1)S(1)}, u32[]{:S(2)}, u32[]{:S(2)}) collective-permute-start(bf16[256,512]{1,0:T(8,128)(2,1)S(1)} %get-tuple-element.39.refs_4_), channel_id=1, source_target_pairs={{0,4},{4,0},{8,12},{12,8},{16,20},{20,16},{24,28},{28,24},{1,5},{5... | collective-permute-start | bytes 786440 | tf_op jit(solution)/shard_map/ppermute | solution.py:523
  96.2 3.4 %shard_map.61.own_ref = f32[256,2048]{1,0:T(8,128)S(1)} custom-call(bf16[256,2560]{1,0:T(8,128)(2,1)S(1)} %get-tuple-element.22.extended_ref, bf16[8,2560,256]{2,1,0:T(8,128)(2,1)S(1)} %copy-done.3, f32[256,2048]{1,0:T(8,128)S(1)} %shard_map.57.own_ref.refs_0_, bf16[256,512]{1,0:T(8,128)(2,1)S(1)} %collective-permute-done.2.got_a_ref.refs_1_, ...), custom_call_target="tpu_custom_call" | custom-call | flops 10737418240 | bytes 12582912 | tf_op jit(solution)/shard_map/pallas_call | solution.py:270
  99.6 2.2 %shard_map.62 = (bf16[256,2560]{1,0:T(8,128)(2,1)S(1)}, f32[256,512]{1,0:T(8,128)}) custom-call(s32[2]{0:T(128)S(1)} %add_convert_fusion.2.there_ref, f32[256,2048]{1,0:T(8,128)S(1)} %shard_map.61.own_ref, bf16[256,512]{1,0:T(8,128)(2,1)S(1)} %collective-permute-done.6.got_a_ref, bf16[256,512]{1,0:T(8,128)(2,1)S(1)} %collective-permute-done.7.got_b_ref, ...), custom_call_target="tpu_custom_call" | custom-call | tf_op jit(solution)/shard_map/pallas_call | solution.py:317
  102.8 0.9 collective-permute-start.9
  103.7 5.0 %collective-permute-start.8 = (bf16[256,256]{1,0:T(8,128)(2,1)S(1)}, bf16[256,256]{1,0:T(8,128)(2,1)S(1)}, u32[]{:S(2)}, u32[]{:S(2)}) collective-permute-start(bf16[256,256]{1,0:T(8,128)(2,1)S(1)} %fusion.7.refs_4_), channel_id=1, source_target_pairs={{0,4},{4,0},{8,12},{12,8},{16,20},{20,16},{24,28},{28,24},{1,5},{5... | collective-permute-start | bytes 393224 | tf_op jit(solution)/shard_map/ppermute | solution.py:523
  108.7 3.4 %shard_map.63.own_ref = f32[256,2048]{1,0:T(8,128)S(1)} custom-call(bf16[256,2560]{1,0:T(8,128)(2,1)S(1)} %get-tuple-element.24.extended_ref, bf16[8,2560,256]{2,1,0:T(8,128)(2,1)S(1)} %copy-done.3, f32[256,2048]{1,0:T(8,128)S(1)} %shard_map.59.own_ref.refs_0_, bf16[256,512]{1,0:T(8,128)(2,1)S(1)} %collective-permute-done.4.got_a_ref.refs_1_, ...), custom_call_target="tpu_custom_call" | custom-call | flops 10737418240 | bytes 12582912 | tf_op jit(solution)/shard_map/pallas_call | solution.py:270
  112.2 1.3 shard_map.64.filtered_ref
  114.0 1.3 collective-permute-done.10
  115.3 3.6 %collective-permute-start.11 = (bf16[256,256]{1,0:T(8,128)(2,1)S(1)}, bf16[256,256]{1,0:T(8,128)(2,1)S(1)}, u32[]{:S(2)}, u32[]{:S(2)}) collective-permute-start(bf16[256,256]{1,0:T(8,128)(2,1)S(1)} %add_convert_fusion.1), channel_id=1, source_target_pairs={{0,8},{4,12},{8,0},{12,4},{16,24},{20,28},{24,16},{28,20},{1,9},{5... | collective-permute-start | bytes 393224 | tf_op jit(solution)/shard_map/ppermute | solution.py:443
  118.9 4.0 %collective-permute-done.11 = bf16[256,256]{1,0:T(8,128)(2,1)S(1)} collective-permute-done((bf16[256,256]{1,0:T(8,128)(2,1)S(1)}, bf16[256,256]{1,0:T(8,128)(2,1)S(1)}, u32[]{:S(2)}, u32[]{:S(2)}) %collective-permute-start.11) | collective-permute-done | bytes 131104 | tf_op jit(solution)/shard_map/ppermute | solution.py:443
  123.0 1.8 %collective-permute-start.12 = (bf16[256,256]{1,0:T(8,128)(2,1)S(1)}, bf16[256,256]{1,0:T(8,128)(2,1)S(1)}, u32[]{:S(2)}, u32[]{:S(2)}) collective-permute-start(bf16[256,256]{1,0:T(8,128)(2,1)S(1)} %add_convert_fusion), channel_id=1, source_target_pairs={{0,16},{4,20},{8,24},{12,28},{16,0},{20,4},{24,8},{28,12},{1,17},{... | collective-permute-start | bytes 393224 | tf_op jit(solution)/shard_map/ppermute | solution.py:443
  124.8 3.4 %collective-permute-done.12 = bf16[256,256]{1,0:T(8,128)(2,1)S(1)} collective-permute-done((bf16[256,256]{1,0:T(8,128)(2,1)S(1)}, bf16[256,256]{1,0:T(8,128)(2,1)S(1)}, u32[]{:S(2)}, u32[]{:S(2)}) %collective-permute-start.12) | collective-permute-done | bytes 131104 | tf_op jit(solution)/shard_map/ppermute | solution.py:443
  128.2 10.1 %shard_map.65 = f32[64,2048]{1,0:T(8,128)} custom-call(s32[1]{0:T(128)} %bitcast.block_ref, f32[256,256]{1,0:T(8,128)S(1)} %convert_add_fusion.gram_ref, bf16[256,2048]{1,0:T(8,128)(2,1)S(1)} %shard_map.64.filtered_ref), custom_call_target="tpu_custom_call" | custom-call | tf_op jit(solution)/shard_map/pallas_call | solution.py:415
  (51 shorter events, 9.0 us)
Async XLA Ops:
  6.5 50.3 %all-gather.2.cloned.1.call-start = ((), (), s32[]{:S(2)}) async-start(), calls=%async_computation | async-start | bytes 1638400 | tf_op jit(solution)/shard_map/all_gather | solution.py:502
  9.0 2.6 %copy-start.4 = (s32[8,512]{1,0:T(8,128)S(1)}, s32[8,512]{1,0:T(8,128)}, u32[]{:S(2)}) copy-start(s32[8,512]{1,0:T(8,128)} %param.7) | copy-start | bytes 49156
  10.0 2.4 %collective-permute-start = (bf16[64,256]{1,0:T(8,128)(2,1)S(1)}, bf16[64,256]{1,0:T(8,128)(2,1)S(1)}, u32[]{:S(2)}, u32[]{:S(2)}) collective-permute-start(bf16[64,256]{1,0:T(8,128)(2,1)S(1)} %get-tuple-element.29), channel_id=1, source_target_pairs={{0,4},{4,0},{8,12},{12,8},{16,20},{20,16},{24,28},{28,24},{1,5},{5... | collective-permute-start | bytes 98312 | tf_op jit(solution)/shard_map/ppermute | solution.py:500
  10.5 1.8 %collective-permute-start.1 = (bf16[64,256]{1,0:T(8,128)(2,1)S(1)}, bf16[64,256]{1,0:T(8,128)(2,1)S(1)}, u32[]{:S(2)}, u32[]{:S(2)}) collective-permute-start(bf16[64,256]{1,0:T(8,128)(2,1)S(1)} %get-tuple-element.30), channel_id=1, source_target_pairs={{4,8},{8,4},{12,16},{16,12},{20,24},{24,20},{5,9},{9,5},{13,17},{1... | collective-permute-start | bytes 98312 | tf_op jit(solution)/shard_map/ppermute | solution.py:499
  12.3 2.6 %copy-start.5 = (s32[3072]{0:T(1024)}, s32[3072]{0:T(1024)S(1)}, u32[]{:S(2)}) copy-start(s32[3072]{0:T(1024)S(1)} %add_dynamic-update-slice_fusion) | copy-start | bytes 36868
  56.9 1.7 %copy-start = (bf16[2560,512]{1,0:T(8,128)(2,1)S(1)}, bf16[2560,512]{1,0:T(8,128)(2,1)}, u32[]{:S(2)}) copy-start(bf16[2560,512]{1,0:T(8,128)(2,1)} %get-tuple-element.15.refs_1_) | copy-start | bytes 7864324
  58.6 1.7 %copy-start.1 = (bf16[2560,512]{1,0:T(8,128)(2,1)S(1)}, bf16[2560,512]{1,0:T(8,128)(2,1)}, u32[]{:S(2)}) copy-start(bf16[2560,512]{1,0:T(8,128)(2,1)} %get-tuple-element.16.refs_2_) | copy-start | bytes 7864324
  60.4 1.3 copy-start.2
  61.7 10.5 %copy-start.3 = (bf16[8,2560,256]{2,1,0:T(8,128)(2,1)S(1)}, bf16[8,2560,256]{2,1,0:T(8,128)(2,1)}, u32[]{:S(2)}) copy-start(bf16[8,2560,256]{2,1,0:T(8,128)(2,1)} %get-tuple-element.18.matrix_ref) | copy-start | bytes 31457284
  63.9 11.2 %collective-permute-start.3 = (bf16[256,512]{1,0:T(8,128)(2,1)S(1)}, bf16[256,512]{1,0:T(8,128)(2,1)S(1)}, u32[]{:S(2)}, u32[]{:S(2)}) collective-permute-start(bf16[256,512]{1,0:T(8,128)(2,1)S(1)} %get-tuple-element.33.refs_1_), channel_id=1, source_target_pairs={{4,8},{8,4},{12,16},{16,12},{20,24},{24,20},{5,9},{9,5},{13,17},{1... | collective-permute-start | bytes 786440 | tf_op jit(solution)/shard_map/ppermute | solution.py:520
  64.7 10.4 %collective-permute-start.2 = (bf16[256,512]{1,0:T(8,128)(2,1)S(1)}, bf16[256,512]{1,0:T(8,128)(2,1)S(1)}, u32[]{:S(2)}, u32[]{:S(2)}) collective-permute-start(bf16[256,512]{1,0:T(8,128)(2,1)S(1)} %get-tuple-element.31.refs_0_), channel_id=1, source_target_pairs={{0,4},{4,0},{8,12},{12,8},{16,20},{20,16},{24,28},{28,24},{1,5},{5... | collective-permute-start | bytes 786440 | tf_op jit(solution)/shard_map/ppermute | solution.py:523
  78.1 7.8 %collective-permute-start.5 = (bf16[256,512]{1,0:T(8,128)(2,1)S(1)}, bf16[256,512]{1,0:T(8,128)(2,1)S(1)}, u32[]{:S(2)}, u32[]{:S(2)}) collective-permute-start(bf16[256,512]{1,0:T(8,128)(2,1)S(1)} %get-tuple-element.37.refs_2_), channel_id=1, source_target_pairs={{4,8},{8,4},{12,16},{16,12},{20,24},{24,20},{5,9},{9,5},{13,17},{1... | collective-permute-start | bytes 786440 | tf_op jit(solution)/shard_map/ppermute | solution.py:520
  78.9 7.0 %collective-permute-start.4 = (bf16[256,512]{1,0:T(8,128)(2,1)S(1)}, bf16[256,512]{1,0:T(8,128)(2,1)S(1)}, u32[]{:S(2)}, u32[]{:S(2)}) collective-permute-start(bf16[256,512]{1,0:T(8,128)(2,1)S(1)} %get-tuple-element.35.refs_1_), channel_id=1, source_target_pairs={{0,4},{4,0},{8,12},{12,8},{16,20},{20,16},{24,28},{28,24},{1,5},{5... | collective-permute-start | bytes 786440 | tf_op jit(solution)/shard_map/ppermute | solution.py:523
  89.8 9.8 %collective-permute-start.7 = (bf16[256,512]{1,0:T(8,128)(2,1)S(1)}, bf16[256,512]{1,0:T(8,128)(2,1)S(1)}, u32[]{:S(2)}, u32[]{:S(2)}) collective-permute-start(bf16[256,512]{1,0:T(8,128)(2,1)S(1)} %get-tuple-element.41.refs_5_), channel_id=1, source_target_pairs={{4,8},{8,4},{12,16},{16,12},{20,24},{24,20},{5,9},{9,5},{13,17},{1... | collective-permute-start | bytes 786440 | tf_op jit(solution)/shard_map/ppermute | solution.py:520
  90.5 9.1 %collective-permute-start.6 = (bf16[256,512]{1,0:T(8,128)(2,1)S(1)}, bf16[256,512]{1,0:T(8,128)(2,1)S(1)}, u32[]{:S(2)}, u32[]{:S(2)}) collective-permute-start(bf16[256,512]{1,0:T(8,128)(2,1)S(1)} %get-tuple-element.39.refs_4_), channel_id=1, source_target_pairs={{0,4},{4,0},{8,12},{12,8},{16,20},{20,16},{24,28},{28,24},{1,5},{5... | collective-permute-start | bytes 786440 | tf_op jit(solution)/shard_map/ppermute | solution.py:523
  102.8 9.3 %collective-permute-start.9 = (bf16[256,256]{1,0:T(8,128)(2,1)S(1)}, bf16[256,256]{1,0:T(8,128)(2,1)S(1)}, u32[]{:S(2)}, u32[]{:S(2)}) collective-permute-start(bf16[256,256]{1,0:T(8,128)(2,1)S(1)} %fusion.10.refs_5_), channel_id=1, source_target_pairs={{4,8},{8,4},{12,16},{16,12},{20,24},{24,20},{5,9},{9,5},{13,17},{1... | collective-permute-start | bytes 393224 | tf_op jit(solution)/shard_map/ppermute | solution.py:520
  103.7 8.4 %collective-permute-start.8 = (bf16[256,256]{1,0:T(8,128)(2,1)S(1)}, bf16[256,256]{1,0:T(8,128)(2,1)S(1)}, u32[]{:S(2)}, u32[]{:S(2)}) collective-permute-start(bf16[256,256]{1,0:T(8,128)(2,1)S(1)} %fusion.7.refs_4_), channel_id=1, source_target_pairs={{0,4},{4,0},{8,12},{12,8},{16,20},{20,16},{24,28},{28,24},{1,5},{5... | collective-permute-start | bytes 393224 | tf_op jit(solution)/shard_map/ppermute | solution.py:523
  113.9 1.4 collective-permute-start.10
  115.3 7.6 %collective-permute-start.11 = (bf16[256,256]{1,0:T(8,128)(2,1)S(1)}, bf16[256,256]{1,0:T(8,128)(2,1)S(1)}, u32[]{:S(2)}, u32[]{:S(2)}) collective-permute-start(bf16[256,256]{1,0:T(8,128)(2,1)S(1)} %add_convert_fusion.1), channel_id=1, source_target_pairs={{0,8},{4,12},{8,0},{12,4},{16,24},{20,28},{24,16},{28,20},{1,9},{5... | collective-permute-start | bytes 393224 | tf_op jit(solution)/shard_map/ppermute | solution.py:443
  123.0 5.3 %collective-permute-start.12 = (bf16[256,256]{1,0:T(8,128)(2,1)S(1)}, bf16[256,256]{1,0:T(8,128)(2,1)S(1)}, u32[]{:S(2)}, u32[]{:S(2)}) collective-permute-start(bf16[256,256]{1,0:T(8,128)(2,1)S(1)} %add_convert_fusion), channel_id=1, source_target_pairs={{0,16},{4,20},{8,24},{12,28},{16,0},{20,4},{24,8},{28,12},{1,17},{... | collective-permute-start | bytes 393224 | tf_op jit(solution)/shard_map/ppermute | solution.py:443
Sparse Core Ops, SparseCore 0:
  13.3 38.4 all-gather.1
